TPU v7x, 32 devices: a whole 2x2x4 slice. The times are simulated.
32 devices in a mesh: acq: 2 (over y), tile: 16 (over z, x, core).
Axes of the slice: x: 2, y: 2, z: 4, core: 2. Of those that a mesh axis runs over, the one named last changes fastest.
Arguments:
- unprocessed_echo_data: float32 [2, 2, 768, 12288], P(None, 'acq', 'tile'), may hold values from -6 to 6
- slant_kernel_frequencies: float32 [2, 2, 12288], P(None, 'acq'), may hold values from -6 to 6
- along_track_kernel_angle: float32 [2, 768, 12288], P('acq', None, 'tile'), may hold values from -3.140625 to 3.140625
- pairs: int32 [2, 2], replicated, may hold values from 0 to 1, as said below
Outputs:
- interferogram: float32 [2, 2, 2, 128, 1536], P(None, None, 'acq', 'tile')
Inputs may be any that keep to these rules, and one draw needn't show every extreme that they name: `pairs`: in each of the 2 rounds the partners of the 2 acquisitions are a permutation of them; an acquisition may be its own partner.
All inputs are finite; a program needn't handle non-finite values.
Results may differ from a plain program's by a relative error of at most 0.000098.
Values sent between devices are 32-bit elements; how exact they have to be, the bound alone decides.
No kernel may reach another device: no remote copies, remote signals or barrier semaphores. Data moves between devices by JAX's collectives and lax.ppermute only.
A program may use at most 192 MiB of HBM per device.

v0:
```python
import math

import jax
import jax.numpy as jnp
from jax import lax
from jax.sharding import PartitionSpec as P

RADIX = 128
LOOK_AZ = 2
LOOK_RG = 8
AOI = 256


precision_mode = lax.Precision.HIGHEST


def factor_tables(length, radix_size, sign):
    outer_size = length // radix_size
    outer_ids = lax.iota(jnp.int32, outer_size)
    inner_ids = lax.iota(jnp.int32, radix_size)
    two_pi = 2.0 * math.pi
    outer_angle = (outer_ids[:, None] * outer_ids[None, :] % outer_size).astype(jnp.float32) * (
        two_pi / outer_size
    )
    inner_angle = (inner_ids[:, None] * inner_ids[None, :] % radix_size).astype(jnp.float32) * (
        two_pi / radix_size
    )
    twist_angle = (outer_ids[:, None] * inner_ids[None, :]).astype(jnp.float32) * (two_pi / length)
    return (
        (jnp.cos(outer_angle), sign * jnp.sin(outer_angle)),
        (jnp.cos(inner_angle), sign * jnp.sin(inner_angle)),
        (jnp.cos(twist_angle), sign * jnp.sin(twist_angle)),
    )


def complex_contract(subscripts, value_entries, matrix):
    real_in, imag_in = value_entries
    mat_real, mat_imag = matrix
    real_out = jnp.einsum(subscripts, real_in, mat_real, precision=precision_mode) - jnp.einsum(
        subscripts, imag_in, mat_imag, precision=precision_mode
    )
    imag_out = jnp.einsum(subscripts, real_in, mat_imag, precision=precision_mode) + jnp.einsum(
        subscripts, imag_in, mat_real, precision=precision_mode
    )
    return (real_out, imag_out)


def complex_times(value_entries, factor):
    return (
        value_entries[0] * factor[0] - value_entries[1] * factor[1],
        value_entries[0] * factor[1] + value_entries[1] * factor[0],
    )


def range_compress(echo_inphase, echo_quadrature, kernel_inphase, kernel_quadrature):
    line_count, length = echo_inphase.shape
    radix_size = RADIX
    outer_size = length // radix_size
    forward = factor_tables(length, radix_size, -1.0)
    backward = factor_tables(length, radix_size, 1.0)
    value_entries = (
        echo_inphase.reshape(line_count, outer_size, radix_size),
        echo_quadrature.reshape(line_count, outer_size, radix_size),
    )
    value_entries = complex_contract("apq,kp->akq", value_entries, forward[0])
    value_entries = complex_times(value_entries, forward[2])
    value_entries = complex_contract("akq,mq->akm", value_entries, forward[1])
    filter_pair = (
        kernel_inphase.reshape(radix_size, outer_size).T,
        kernel_quadrature.reshape(radix_size, outer_size).T,
    )
    value_entries = complex_times(value_entries, filter_pair)
    value_entries = complex_contract("akm,qm->akq", value_entries, backward[1])
    value_entries = complex_times(value_entries, backward[2])
    value_entries = complex_contract("akq,pk->apq", value_entries, backward[0])
    return (
        value_entries[0].reshape(line_count, length) / length,
        value_entries[1].reshape(line_count, length) / length,
    )


def azimuth_focus(value_entries, angle_term):
    length, column_count = value_entries[0].shape
    radix_size = RADIX
    outer_size = length // radix_size
    forward = factor_tables(length, radix_size, -1.0)
    backward = factor_tables(length, radix_size, 1.0)
    value_entries = (
        value_entries[0].reshape(outer_size, radix_size, column_count),
        value_entries[1].reshape(outer_size, radix_size, column_count),
    )
    value_entries = complex_contract("pqc,kp->kqc", value_entries, forward[0])
    value_entries = complex_times(
        value_entries, (forward[2][0][:, :, None], forward[2][1][:, :, None])
    )
    value_entries = complex_contract("kqc,mq->kmc", value_entries, forward[1])
    phase_ordered = jnp.transpose(
        angle_term.reshape(radix_size, outer_size, column_count), (1, 0, 2)
    )
    value_entries = complex_times(value_entries, (jnp.cos(phase_ordered), jnp.sin(phase_ordered)))
    value_entries = complex_contract("kmc,qm->kqc", value_entries, backward[1])
    value_entries = complex_times(
        value_entries, (backward[2][0][:, :, None], backward[2][1][:, :, None])
    )
    value_entries = complex_contract("kqc,pk->pqc", value_entries, backward[0])
    first_line = (length - AOI) // 2
    focused_real = (
        lax.slice_in_dim(
            value_entries[0].reshape(length, column_count), first_line, first_line + AOI, axis=0
        )
        / length
    )
    focused_imag = (
        lax.slice_in_dim(
            value_entries[1].reshape(length, column_count), first_line, first_line + AOI, axis=0
        )
        / length
    )
    return (focused_real, focused_imag)


def multilook(field, rounds):
    round_count, row_count, column_count = field.shape
    shaped = field.reshape(rounds, row_count // LOOK_AZ, LOOK_AZ, column_count // LOOK_RG, LOOK_RG)
    return jnp.sum(shaped, axis=(2, 4)) / (LOOK_AZ * LOOK_RG)


def shards(unprocessed_echo_data, slant_kernel_frequencies, along_track_kernel_angle, pairs):
    range_real, range_imaginary_part = range_compress(
        unprocessed_echo_data[0, 0],
        unprocessed_echo_data[1, 0],
        slant_kernel_frequencies[0, 0],
        slant_kernel_frequencies[1, 0],
    )
    line_stack = jnp.stack([range_real, range_imaginary_part])
    turned = lax.all_to_all(line_stack, "tile", split_axis=2, concat_axis=1, tiled=True)
    sharpened_scene = azimuth_focus((turned[0], turned[1]), along_track_kernel_angle[0])
    columns = jnp.stack(sharpened_scene)
    working_buffer = lax.all_to_all(columns, "tile", split_axis=1, concat_axis=2, tiled=True)
    rounds = pairs.shape[0]
    acq_index = lax.axis_index("acq")
    partners = lax.dynamic_index_in_dim(pairs, acq_index, 1, keepdims=False)
    mine = working_buffer[None]
    initial = jnp.zeros((rounds,) + working_buffer.shape, jnp.float32)
    shard_piece = lax.all_gather(mine, "acq", axis=0, tiled=True)
    how_many = shard_piece.shape[0]
    chosen = []
    for round_id in range(rounds):
        offset = partners[round_id]
        inside = (offset >= 0) & (offset < how_many)
        picked = lax.dynamic_index_in_dim(
            shard_piece, jnp.clip(offset, 0, how_many - 1), 0, keepdims=False
        )
        chosen.append(jnp.where(inside, picked, initial[round_id]))
    partner_data = jnp.stack(chosen)
    self_real = working_buffer[0][None]
    self_imag = working_buffer[1][None]
    cross_real = self_real * partner_data[:, 0] + self_imag * partner_data[:, 1]
    cross_imag = self_imag * partner_data[:, 0] - self_real * partner_data[:, 1]
    looked = jnp.stack([multilook(cross_real, rounds), multilook(cross_imag, rounds)])
    return looked[:, :, None]


def solution(mesh):
    in_specs = (P(None, "acq", "tile", None), P(None, "acq", None), P("acq", None, "tile"), P())
    out_specs = P(None, None, "acq", "tile", None)
    return jax.shard_map(shards, mesh=mesh, in_specs=in_specs, out_specs=out_specs, check_vma=False)
```

profile of v0, /device:TPU:0, one launch (start us, length us, event | category | flops | bytes accessed | tf_op | source)
XLA Modules:
  0.0 520.1 jit_solution(17608915318388454858)
XLA Ops:
  31.9 4.3 fusion.52
  50.3 4.4 multiply_bitcast_fusion.1
  57.8 6.5 %multiply_bitcast_fusion = f32[48,96,128]{2,1,0:T(8,128)} fusion(f32[96,48,128]{2,0,1:T(8,128)} %fusion.53, f32[48,96,128]{2,1,0:T(8,128)} %copy-done.4, f32[48,96,128]{2,1,0:T(8,128)S(1)} %copy-done.3, f32[96,128]{1,0:T(8,128)S(1)} %fusion.93, f32[96,128]{1,0:T(8,128)S(1)} %get-tuple-element.27), kind=kOutput, calls=%fused_computation.49 | convolution fusion | flops 682509312 | bytes 9535488 | tf_op jit(solution)/shard_map/akq,pk->apq/dot_general | solution.py:42
  67.3 4.4 pad_maximum_fusion
  71.7 15.4 %copy.114 = f32[2,48,12288]{1,0,2:T(2,128)} copy(f32[2,48,12288]{2,1,0:T(8,128)} %pad_maximum_fusion) | data formatting | bytes 9437184 | tf_op jit(solution)/shard_map/stack | solution.py:135
  87.1 23.1 %reshape.228 = f32[16,1,73728]{2,1,0:T(1,128)} reshape(f32[12288,2,48]{2,1,0:T(2,128)} %bitcast.173) | data formatting | bytes 9437184
  110.2 7.5 %all-to-all-start = ((f32[16,1,73728]{2,1,0:T(1,128)}), f32[16,1,73728]{2,1,0:T(1,128)}, u32[]{:S(2)}, u32[]{:S(2)}) async-start(f32[16,1,73728]{2,1,0:T(1,128)} %reshape.228), calls=%async_computation | async-start | bytes 9437184 | tf_op jit(solution)/shard_map/all_to_all | solution.py:136
  118.0 9.5 %fusion.330 = (f32[1,768,768]{2,1,0:T(8,128)}, f32[1,768,768]{2,1,0:T(8,128)}) fusion(f32[1,768,768]{2,1,0:T(8,128)S(1)} %copy-done.7), kind=kLoop, calls=%fused_computation.329 | loop fusion | bytes 7077888 | tf_op jit(solution)/shard_map/cos | solution.py:100
  133.6 70.9 %all-to-all-done = f32[16,1,73728]{2,1,0:T(1,128)} async-done(((f32[16,1,73728]{2,1,0:T(1,128)}), f32[16,1,73728]{2,1,0:T(1,128)}, u32[]{:S(2)}, u32[]{:S(2)}) %all-to-all-start) | async-done | bytes 4718624 | tf_op jit(solution)/shard_map/all_to_all | solution.py:136
  205.1 15.9 %reduce.8 = f32[16,73728]{1,0:T(8,128)} reduce(f32[16,1,73728]{2,1,0:T(1,128)} %all-to-all-done, f32[]{:T(128)} %broadcast.421), dimensions={1}, to_apply=%all_to_all.22.reduce_sub_computation | reduce | bytes 9437188 | tf_op jit(solution)/shard_map/all_to_all | solution.py:136
  220.9 29.2 %reshape.229 = f32[12288,2,48]{2,1,0:T(2,128)} reshape(f32[16,73728]{1,0:T(8,128)} %reduce.8) | data formatting | bytes 9437184
  250.1 12.1 %copy.140 = f32[2,48,16,768]{3,2,1,0:T(8,128)} copy(f32[2,48,16,768]{1,0,3,2:T(2,128)} %bitcast.174) | data formatting | bytes 9437184 | tf_op jit(solution)/shard_map/all_to_all | solution.py:136
  276.0 4.7 fusion.10
  310.1 4.7 fusion.6
  314.8 4.2 fusion.4
  319.1 4.2 fusion.2
  323.3 4.4 fusion
  331.1 57.6 %all_to_all.30 = f32[2,256,768]{2,0,1:T(2,128)S(1)} all-to-all(f32[2,256,768]{2,0,1:T(2,128)S(1)} %copy.138), channel_id=1, replica_groups=mesh['acq'=2,'tile'=16] {'tile'}, dimensions={1} | all-to-all | bytes 3145728 | tf_op jit(solution)/shard_map/all_to_all | solution.py:139
  395.9 8.5 %mul.860 = f32[8,2,1536,8]{3,2,1,0:T(8,128)} reshape(f32[1,16,16,768]{3,2,1,0:T(8,128)S(1)} %get-tuple-element.23) | data formatting | bytes 1572864 | tf_op jit(solution)/shard_map/mul | solution.py:158
  404.4 8.5 %mul.863 = f32[8,2,1536,8]{3,2,1,0:T(8,128)} reshape(f32[1,16,16,768]{3,2,1,0:T(8,128)S(1)} %get-tuple-element.24) | data formatting | bytes 1572864 | tf_op jit(solution)/shard_map/mul | solution.py:158
  412.8 23.7 %all-gather.2.cloned.1.call-done = f32[2,2,16,12288]{3,2,1,0:T(8,128)} async-done(((f32[1,2,16,12288]{3,2,1,0:T(8,128)}), f32[2,2,16,12288]{3,2,1,0:T(8,128)}) %all-gather.2.cloned.1.call-update) | async-done | bytes 3145744 | tf_op jit(solution)/shard_map/all_gather | solution.py:145
  438.9 24.1 %squeeze.16 = f32[2,8,2,1536,8]{4,3,2,1,0:T(8,128)} reshape(f32[2,1,16,12288]{3,2,1,0:T(8,128)S(1)} %get-tuple-element.18) | data formatting | bytes 3145728 | tf_op jit(solution)/shard_map/squeeze | solution.py:158
  463.0 24.3 %squeeze.9 = f32[2,8,2,1536,8]{4,3,2,1,0:T(8,128)} reshape(f32[2,1,16,12288]{3,2,1,0:T(8,128)S(1)} %get-tuple-element.17) | data formatting | bytes 3145728 | tf_op jit(solution)/shard_map/squeeze | solution.py:158
  487.4 24.9 %add_reduce_fusion = (f32[2,8,1536]{2,1,0:T(8,128)S(1)}, f32[2,8,1536]{2,1,0:T(8,128)S(1)}) fusion(f32[2,8,2,1536,8]{4,3,2,1,0:T(8,128)} %squeeze.16, f32[2,8,2,1536,8]{4,3,2,1,0:T(8,128)} %squeeze.9, f32[8,2,1536,8]{3,2,1,0:T(8,128)} %mul.863, f32[8,2,1536,8]{3,2,1,0:T(8,128)} %mul.860), kind=kLoop, calls=%fused_computation.1 | loop fusion | flops 3096576 | bytes 4915200 | tf_op jit(solution)/shard_map/reduce_sum | solution.py:125
  (84 shorter events, 104.9 us)
Async XLA Ops:
  6.5 384.5 %copy-start = (s32[2,2]{1,0:T(2,128)S(1)}, s32[2,2]{1,0:T(2,128)}, u32[]{:S(2)}) copy-start(s32[2,2]{1,0:T(2,128)} %param.7) | copy-start | bytes 52
  27.4 3.8 copy-start.8
  31.9 4.3 copy-start.1
  41.5 8.8 %copy-start.2 = (f32[48,96,128]{2,1,0:T(8,128)}, f32[48,96,128]{2,1,0:T(8,128)S(1)}, u32[]{:S(2)}) copy-start(f32[48,96,128]{2,1,0:T(8,128)S(1)} %convolution_subtract_fusion.1) | copy-start | bytes 7077892
  44.0 6.3 %copy-start.4 = (f32[48,96,128]{2,1,0:T(8,128)}, f32[48,96,128]{2,1,0:T(8,128)S(1)}, u32[]{:S(2)}) copy-start(f32[48,96,128]{2,1,0:T(8,128)S(1)} %convolution_add_fusion.1) | copy-start | bytes 7077892
  54.7 3.0 copy-start.3
  64.3 3.1 copy-start.6
  110.2 7.8 %copy-start.7 = (f32[1,768,768]{2,1,0:T(8,128)S(1)}, f32[1,768,768]{2,1,0:T(8,128)}, u32[]{:S(2)}) copy-start(f32[1,768,768]{2,1,0:T(8,128)} %param.6) | copy-start | bytes 7077892
  110.2 94.4 %all-to-all-start = ((f32[16,1,73728]{2,1,0:T(1,128)}), f32[16,1,73728]{2,1,0:T(1,128)}, u32[]{:S(2)}, u32[]{:S(2)}) async-start(f32[16,1,73728]{2,1,0:T(1,128)} %reshape.228), calls=%async_computation | async-start | bytes 9437184 | tf_op jit(solution)/shard_map/all_to_all | solution.py:136
  117.7 318.8 %all-gather.2.cloned.1.call-start = ((), (), s32[]{:S(2)}) async-start(), calls=%async_computation.2 | async-start | bytes 4718592 | tf_op jit(solution)/shard_map/all_gather | solution.py:145
  293.0 2.6 copy-start.5
Sparse Core Ops, SparseCore 0:
  391.2 45.3 all-gather.1
where the time goes:
time: 530 us; the launch traced here: 520 us
  local copies, waits for them, and re-layouts  183 us (35%)
  matrix products  107 us (20%)
  waiting for transfers between devices  94.6 us (18%)
  blocking collectives  57.6 us (11%)
  other arithmetic  51.8 us (10%)
  between operations  18.1 us (3%)
  starting transfers between devices  7.75 us (1%)
    all_to_all x1, waiting for transfers between devices, shards(): lax.all_to_all(line_stack, 'tile', split_axis=2, concat_axis=1, tiled=True)  70.9 us
    all_to_all x1, blocking collectives, shards(): lax.all_to_all(columns, 'tile', split_axis=1, concat_axis=2, tiled=True)  57.6 us
    unnamed x23, local copies, waits for them, and re-layouts  55.8 us
    squeeze x2, local copies, waits for them, and re-layouts, shards(): cross_real = self_real * partner_data[:, 0] + self_imag * partner_data[:, 1]  48.5 us
    dot_general x8, matrix products, complex_contract(): jnp.einsum(subscripts, imag_in, mat_real, precision=precision_mode)  28.8 us
    dot_general x8, matrix products, complex_contract(): jnp.einsum(subscripts, real_in, mat_imag, precision=precision_mode)  26.9 us
    dot_general x8, matrix products, complex_contract(): jnp.einsum(subscripts, imag_in, mat_imag, precision=precision_mode)  26 us
    dot_general x8, matrix products, complex_contract(): jnp.einsum(subscripts, real_in, mat_real, precision=precision_mode)  25.5 us
  transfers between devices with their start and end apart: 2, of which 2 were waited for; matrix products, arithmetic and copies ran while one was open for 6% of the time, Pallas kernels for 0%

commit v1 on v0

v1 whole, which is shorter than its diff:
```python
import functools
import math

import jax
import jax.numpy as jnp
import ml_dtypes
import numpy as np
from jax import lax
from jax.experimental import pallas as pl
from jax.experimental.pallas import tpu as pltpu
from jax.sharding import PartitionSpec as P

LOOK_AZ = 2
LOOK_RG = 8
AOI = 256
LANES = 128
SUB = 8
FAR = 4
BATCH = 4
VMEM_LIMIT = 56 * 1024 * 1024


def high_low(table):
    high = table.astype(ml_dtypes.bfloat16)
    low = (table - high.astype(np.float64)).astype(ml_dtypes.bfloat16)
    return np.stack([high, low])


def trig(product, period):
    angle = (product % period) * (2.0 * math.pi / period)
    return np.cos(angle), np.sin(angle)


def split(value):
    high = value.astype(jnp.bfloat16)
    return high, (value - high.astype(jnp.float32)).astype(jnp.bfloat16)


def dot(left, right):
    return jnp.dot(left, right, preferred_element_type=jnp.float32)


def dot_stacked(table, value):
    high, low = split(value)
    both = dot(table, jnp.concatenate([high, low], axis=0))
    rows = table.shape[0] // 2
    return both[:rows] + both[rows:]


def thirds(a, b, c, sign):
    scale = sign * math.sqrt(3.0) / 2.0
    tr, ti = b[0] + c[0], b[1] + c[1]
    vr, vi = (b[0] - c[0]) * scale, (b[1] - c[1]) * scale
    ur, ui = a[0] - 0.5 * tr, a[1] - 0.5 * ti
    return (a[0] + tr, a[1] + ti), (ur - vi, ui + vr), (ur + vi, ui - vr)


def dot_table_right(value, table):
    high, low = split(value)
    return dot(jnp.concatenate([high, low, high], axis=1), table)


def stacked(table):
    high, low = high_low(table)
    return np.block([[high, high], [low, np.zeros_like(low)]])


def range_tables(length, order, halves):
    inner = LANES
    outer = length // inner
    part = outer // 3
    k1 = np.arange(outer)
    q = np.arange(inner)
    inside = np.arange(part)
    per_tile = outer // len(order)
    blocks = per_tile // halves
    a1, a4 = [], []
    for p0 in range(3):
        c, s = trig(np.outer(inside, 3 * inside + p0), outer)
        a1.append(stacked(np.block([[c, s], [-s, c]])))
        c, s = trig(np.outer(3 * inside + p0, inside), outer)
        rows = [
            cc * part + (t * per_tile + half * blocks) // 3 + b
            for half in range(halves)
            for t in order
            for cc in range(2)
            for b in range(blocks // 3)
        ]
        a4.append(stacked(np.block([[c, -s], [s, c]])[np.array(rows)] / length))
    c2, s2 = trig(np.outer(q, q), inner)
    b2 = np.block([[c2, -s2], [s2, c2]])
    b3 = np.block([[c2, s2], [-s2, c2]])
    ct, st = trig(np.outer(k1, q), length)
    twiddle = np.stack([ct, st]).astype(np.float32)
    b2, b3 = [np.concatenate(high_low(t)[[0, 0, 1]]) for t in (b2, b3)]
    return np.stack(a1), b2, b3, np.stack(a4), twiddle


def spot(tile, low):
    return lax.rem(tile, low) * FAR + lax.div(tile, low)


def range_kernel(outer, early, me_ref, x_ref, slant_ref, a1_ref, b2_ref, b3_ref, a4_ref, t_ref, *rest):
    outs, (rows_ref, h_ref), held = rest[: 1 + early], rest[1 + early : 3 + early], rest[3 + early :]
    part = outer // 3

    @pl.when(pl.program_id(0) == 0)
    def _():
        for c in range(2):
            for k2 in range(LANES):
                rows_ref[c, k2 : k2 + 1, :outer] = slant_ref[c, :, k2 * outer : (k2 + 1) * outer]
            h_ref[c] = rows_ref[c].T[:outer]

    rows = outs[0].shape[2]
    turned = held[0] if early else outs[0].reshape(outs[0].shape[0] * rows, LANES)
    ct, st = t_ref[0], t_ref[1]
    hr, hi = h_ref[0], h_ref[1]

    def batch(first):
        lines = range(first, first + BATCH)
        y = []
        for p0 in range(3):
            x = [
                jnp.concatenate(
                    [x_ref[c, 0, pl.ds(p0 * SUB + l, part, stride=3 * SUB), :] for c in range(2)], axis=0
                )
                for l in lines
            ]
            value = dot_stacked(a1_ref[p0], jnp.concatenate(x, axis=1))
            y.append((value[:part], value[part:]))
        yield
        y = thirds(*y, -1.0)
        z = []
        for b in range(BATCH):
            yr, yi = [
                jnp.concatenate([v[c][:, b * LANES : (b + 1) * LANES] for v in y], axis=0) for c in range(2)
            ]
            z.append(jnp.concatenate([yr * ct + yi * st, yi * ct - yr * st], axis=1))
        y = dot_table_right(jnp.concatenate(z, axis=0), b2_ref[...])
        yield
        z = []
        for b in range(BATCH):
            yr = y[b * outer : (b + 1) * outer, :LANES]
            yi = y[b * outer : (b + 1) * outer, LANES:]
            z.append(jnp.concatenate([yr * hr - yi * hi, yr * hi + yi * hr], axis=1))
        y = dot_table_right(jnp.concatenate(z, axis=0), b3_ref[...])
        yield
        z = []
        for b in range(BATCH):
            yr = y[b * outer : (b + 1) * outer, :LANES]
            yi = y[b * outer : (b + 1) * outer, LANES:]
            zr, zi = yr * ct - yi * st, yi * ct + yr * st
            z.append(thirds(*[(zr[k * part : (k + 1) * part], zi[k * part : (k + 1) * part]) for k in range(3)], 1.0))
        y = []
        for p0 in range(3):
            value = jnp.concatenate([jnp.concatenate(z[b][p0], axis=0) for b in range(BATCH)], axis=1)
            y.append(dot_stacked(a4_ref[p0], value))
        yield
        for p0 in range(3):
            for b, l in enumerate(lines):
                turned[pl.ds(p0 * SUB + l, 2 * part, stride=3 * SUB), :] = y[p0][
                    :, b * LANES : (b + 1) * LANES
                ]
        yield

    batches = [batch(first) for first in range(0, SUB, BATCH)]
    for _ in range(5):
        for work in batches:
            next(work)
    if not early:
        return
    near = outs[0].shape[0] // 2
    for k, out in enumerate(outs):
        for s in range(2 * near):
            tile = jnp.bitwise_xor(me_ref[1], s % near + k * near)
            dest = jnp.bitwise_xor(me_ref[0], s // near) * 2 * near + spot(tile, 2 * near // FAR)
            out[s, 0] = turned[pl.ds(pl.multiple_of(dest * rows, SUB), rows), :]


def range_call(echo, slant, me, first, steps, order, halves, early=False):
    length = echo.shape[3]
    outer = length // LANES
    view = echo.reshape(2, -1, SUB, outer, LANES).transpose(0, 1, 3, 2, 4).reshape(2, -1, outer * SUB, LANES)
    tables = [slant, *range_tables(length, order, halves)]
    dests = len(order) * halves
    rows = 2 * outer // dests * SUB
    whole = lambda shape: pl.BlockSpec(shape, lambda s, me: (0,) * len(shape))
    macs = steps * SUB * length * 2 * (2 * outer + 2 * LANES) * 2 * 3
    outs = 1 + early
    return pl.pallas_call(
        functools.partial(range_kernel, outer, early),
        grid_spec=pltpu.PrefetchScalarGridSpec(
            num_scalar_prefetch=1,
            grid=(steps,),
            in_specs=[pl.BlockSpec((2, 1, outer * SUB, LANES), lambda s, me: (0, first + s, 0, 0))]
            + [whole(t.shape) for t in tables],
            out_specs=[pl.BlockSpec((dests // outs, 1, rows, LANES), lambda s, me: (0, s, 0, 0))] * outs,
            scratch_shapes=[
                pltpu.VMEM((2, LANES, LANES), jnp.float32),
                pltpu.VMEM((2, outer, LANES), jnp.float32),
            ]
            + [pltpu.VMEM((dests * rows, LANES), jnp.float32)] * early,
        ),
        out_shape=[jax.ShapeDtypeStruct((dests // outs, steps, rows, LANES), jnp.float32)] * outs,
        compiler_params=pltpu.CompilerParams(vmem_limit_bytes=VMEM_LIMIT),
        cost_estimate=pl.CostEstimate(
            flops=2 * macs, bytes_accessed=16 * steps * SUB * length, transcendentals=0
        ),
        name=f"range_compress_{first}",
    )(me, view, *[jnp.asarray(t) for t in tables])


def pair_kernel(kept_ref, came_ref, *outs):
    for s, out in enumerate(outs):
        out[0] = kept_ref[s, 0]
        out[1] = came_ref[s, 0]


def pair_call(kept, came):
    count, _, rows, _ = kept.shape
    vmem = pl.BlockSpec(memory_space=pltpu.VMEM)
    return pl.pallas_call(
        pair_kernel,
        in_specs=[vmem] * 2,
        out_specs=[vmem] * count,
        out_shape=[jax.ShapeDtypeStruct((2, rows, LANES), jnp.float32)] * count,
        compiler_params=pltpu.CompilerParams(vmem_limit_bytes=VMEM_LIMIT),
        cost_estimate=pl.CostEstimate(flops=10**12, bytes_accessed=4 * kept.size, transcendentals=0),
        name="pair_halves",
    )(kept, came)


def azimuth_tables(length):
    part = length // 6
    f1 = np.arange(part)
    forward, backward = [], []
    first = (length - AOI) // 2
    u, s = np.arange(part // LOOK_AZ), np.arange(LOOK_AZ)
    lines = (first + u[None, :] * LOOK_AZ + s[:, None]).reshape(-1)
    for f0 in range(6):
        c, s = trig(np.outer(6 * f1 + f0, np.arange(part)), length)
        forward.append(np.block([[c, s], [-s, c]]))
        c, s = trig(np.outer(lines, 6 * f1 + f0), length)
        backward.append(np.block([[c, -s], [s, c]]) / length)
    return [np.concatenate(high_low(np.stack(t)), axis=1) for t in (forward, backward)]


def cos_sin(angle):
    y = 0.5 * angle
    z = y * y
    sine = [1.0, -1 / 6, 1 / 120, -1 / 5040, 1 / 362880, -1 / 39916800]
    cosine = [1.0, -1 / 2, 1 / 24, -1 / 720, 1 / 40320, -1 / 3628800, 1 / 479001600]
    s, c = sine[-1], cosine[-1]
    for k in sine[-2::-1]:
        s = s * z + k
    for k in cosine[-2::-1]:
        c = c * z + k
    s = s * y
    return 1.0 - 2.0 * (s * s), 2.0 * (s * c)


def three_pass(table, value):
    high, low = split(value)
    both = dot(table, high)
    rows = table.shape[0] // 2
    return (both[:rows] + both[rows:]) + dot(table[:rows], low)


def focus(xr, xi, cos_sin_of, tables):
    fw, bw = tables
    part, width = xr.shape[0] // 6, xr.shape[1]
    x = [(xr[k * part : (k + 1) * part], xi[k * part : (k + 1) * part]) for k in range(6)]
    classes = [None] * 6
    sums = thirds(*[(x[k][0] + x[k + 3][0], x[k][1] + x[k + 3][1]) for k in range(3)], -1.0)
    signs = [(x[k][0] - x[k + 3][0], x[k][1] - x[k + 3][1]) for k in range(3)]
    signs[1] = (x[4][0] - x[1][0], x[4][1] - x[1][1])
    diffs = thirds(*signs, -1.0)
    for e in range(3):
        classes[2 * e] = sums[e]
        classes[(2 * e + 3) % 6] = diffs[e]
    z, forward = [], []
    for f0 in range(7):
        if f0 < 6:
            forward.append(three_pass(fw[f0], jnp.concatenate(classes[f0], axis=0)))
        if f0 > 0:
            y, k = forward[f0 - 1], f0 - 1
            dr, di = y[:part], y[part:]
            pc, ps = cos_sin_of(k)
            e = jnp.concatenate([dr * pc - di * ps, dr * ps + di * pc], axis=0)
            z.append(three_pass(bw[k], e))
    half = math.sqrt(3.0) / 2.0
    first = (z[0] + z[3]) + (z[1] + z[4]) + (z[2] + z[5])
    a, b, c = z[0] - z[3], z[1] - z[4], z[2] - z[5]
    real = a + 0.5 * (b - c)
    turned = (b + c) * half
    fr = jnp.concatenate([first[:part], real[:part] - turned[part:]], axis=0)
    fi = jnp.concatenate([first[part:], real[part:] + turned[:part]], axis=0)
    return fr, fi


def lines_of(refs, first, order, part):
    tiles = len(order)
    at = [x[pl.ds(first, tiles), :, part, 0] for x in refs]
    value = at[0] if len(at) == 1 else jnp.concatenate(at, axis=1)
    if order != list(range(tiles)):
        value = jnp.stack([value[order.index(t)] for t in range(tiles)])
    return value.reshape(-1, LANES)


def looked_at(field, look):
    half = AOI // 2
    quarter = half // LOOK_AZ
    added = [field[h * half : h * half + quarter] + field[h * half + quarter : (h + 1) * half] for h in range(2)]
    high, low = split(jnp.concatenate(added, axis=0))
    return dot(high, look) + dot(low, look)


def trig_kernel(_, own_ref, other_ref, out):
    part = own_ref.shape[0] // 6
    for k in range(6):
        angle = jnp.concatenate([a[pl.ds(k, part, stride=6), :] for a in (own_ref, other_ref)], axis=1)
        out[0, 0, k], out[0, 1, k] = cos_sin(angle)


def trig_call(acq, angle, other_angle):
    lines, width = other_angle.shape
    blocks = width // LANES
    shape = (2, 6, lines // 6, 2 * LANES)
    return pl.pallas_call(
        trig_kernel,
        grid_spec=pltpu.PrefetchScalarGridSpec(
            num_scalar_prefetch=1,
            grid=(blocks,),
            in_specs=[
                pl.BlockSpec((lines, LANES), lambda b, acq: (0, acq[0] * blocks + b)),
                pl.BlockSpec((lines, LANES), lambda b, acq: (0, b)),
            ],
            out_specs=pl.BlockSpec((1,) + shape, lambda b, acq: (b, 0, 0, 0, 0)),
        ),
        out_shape=jax.ShapeDtypeStruct((blocks,) + shape, jnp.float32),
        compiler_params=pltpu.CompilerParams(vmem_limit_bytes=VMEM_LIMIT),
        cost_estimate=pl.CostEstimate(
            flops=64 * lines * width, bytes_accessed=24 * lines * width, transcendentals=0
        ),
        name="angle_phases",
    )(acq, angle, other_angle)


def joint_kernel(order, rounds, me_ref, same_ref, x_ref, early_ref, trig_ref, fw, bw, look_ref, out, stage):
    acq = me_ref[0]
    tiles = len(order)
    near = tiles // 2
    firsts = [acq * tiles, (1 - acq) * tiles]
    for part in range(2):
        for k, first in enumerate(firsts):
            lanes = slice(k * LANES, (k + 1) * LANES)
            for place, t in enumerate(order):
                stage[part, t, 1:, :, lanes] = x_ref[first + place, :, part, 0]
            for s in range(near):
                for side in range(2):
                    tile = jnp.bitwise_xor(me_ref[1], s + side * near)
                    stage[part, tile, 0, :, lanes] = early_ref[k * near + s, side, part, 0]
    xr, xi = [stage[part].reshape(-1, 2 * LANES) for part in range(2)]
    fr, fi = focus(xr, xi, lambda k: (trig_ref[0, 0, k], trig_ref[0, 1, k]), [fw, bw])
    mr, mi, pr, pi = fr[:, :LANES], fi[:, :LANES], fr[:, LANES:], fi[:, LANES:]
    look = look_ref[0]
    cross_real = looked_at(mr * pr + mi * pi, look[0])
    cross_imag = looked_at(mi * pr - mr * pi, look[1])
    own_real = looked_at(mr * mr + mi * mi, look[0])
    own_imag = looked_at(mi * mr - mr * mi, look[1])
    other_real = looked_at(pr * pr + pi * pi, look[0])
    other_imag = looked_at(pi * pr - pr * pi, look[1])
    per = AOI // LOOK_AZ // tiles

    @pl.when(pl.program_id(0) == 0)
    def _():
        out[...] = jnp.zeros_like(out)

    for r in range(rounds):
        same = same_ref[r] != 0
        own = jnp.where(same, own_real + own_imag, cross_real + cross_imag)
        other = jnp.where(same, other_real + other_imag, cross_real - cross_imag)
        for first, value in zip(firsts, (own, other)):
            for place, t in enumerate(order):
                out[first + place, r * per : (r + 1) * per, :] += value[t * per : (t + 1) * per]


def joint_call(me, same, array, early, trig, tables, order):
    dests, steps, _, blocks = array.shape[:4]
    tiles = len(order)
    lines = 6 * trig.shape[3]
    rounds = same.shape[0]
    rows = rounds * (AOI // LOOK_AZ // tiles)
    wide = blocks * LANES // LOOK_RG
    look = np.stack(
        [
            np.stack([look_table(LANES, c * wide + b * LANES // LOOK_RG) for c in range(2)])
            for b in range(blocks)
        ]
    )
    block = lambda a: pl.BlockSpec(a.shape[:3] + (1, SUB, LANES), lambda b, me, same: (0, 0, 0, b, 0, 0))
    return pl.pallas_call(
        functools.partial(joint_kernel, order, rounds),
        grid_spec=pltpu.PrefetchScalarGridSpec(
            num_scalar_prefetch=2,
            grid=(blocks,),
            in_specs=[
                block(array),
                block(early),
                pl.BlockSpec((1,) + trig.shape[1:], lambda b, me, same: (b, 0, 0, 0, 0)),
                *[pl.BlockSpec(t.shape, lambda b, me, same: (0, 0, 0)) for t in tables],
                pl.BlockSpec((1,) + look.shape[1:], lambda b, me, same: (b, 0, 0, 0)),
            ],
            out_specs=pl.BlockSpec((dests, rows, LANES), lambda b, me, same: (0, 0, 0)),
            scratch_shapes=[pltpu.VMEM((2, tiles, steps + 1, SUB, 2 * LANES), jnp.float32)],
        ),
        out_shape=jax.ShapeDtypeStruct((dests, rows, LANES), jnp.float32),
        compiler_params=pltpu.CompilerParams(vmem_limit_bytes=VMEM_LIMIT),
        cost_estimate=pl.CostEstimate(
            flops=2 * 2 * 3 * 6 * 256 * 256 * 2 * LANES * blocks,
            bytes_accessed=20 * lines * 2 * LANES * blocks,
            transcendentals=0,
        ),
        name="azimuth_interferogram",
    )(me, same, array, early, trig, *[jnp.asarray(t) for t in tables], jnp.asarray(look))


def single_kernel(tiles, x_ref, angle_ref, fw, bw, out):
    xr, xi = [lines_of([x_ref], 0, list(range(tiles)), part) for part in range(2)]
    fr, fi = focus(xr, xi, lambda k: cos_sin(angle_ref[pl.ds(k, AOI // 2, stride=6), :]), [fw, bw])
    out[:AOI] = fr
    out[AOI:] = fi


def single_call(array, angle, tables):
    tiles = array.shape[0]
    lines, columns = angle.shape
    return pl.pallas_call(
        functools.partial(single_kernel, tiles),
        grid=(columns // LANES,),
        in_specs=[
            pl.BlockSpec((tiles, array.shape[1], 2, 1, SUB, LANES), lambda b: (0, 0, 0, b, 0, 0)),
            pl.BlockSpec((lines, LANES), lambda b: (0, b)),
        ]
        + [pl.BlockSpec(t.shape, lambda b: (0, 0, 0)) for t in tables],
        out_specs=pl.BlockSpec((2 * AOI, LANES), lambda b: (0, b)),
        out_shape=jax.ShapeDtypeStruct((2 * AOI, columns), jnp.float32),
        compiler_params=pltpu.CompilerParams(vmem_limit_bytes=VMEM_LIMIT),
        name="azimuth_focus",
    )(array, angle, *[jnp.asarray(t) for t in tables])


def look_table(width, offset):
    table = np.zeros((width, LANES), np.float64)
    table[np.arange(width), offset + np.arange(width) // LOOK_RG] = 1.0 / (LOOK_AZ * LOOK_RG)
    return table.astype(ml_dtypes.bfloat16)


def cross_kernel(rounds, tiles, mine_ref, *refs):
    partner_refs, look_ref, out = refs[:rounds], refs[-2], refs[-1]
    mr, mi = mine_ref[:AOI], mine_ref[AOI:]
    per = AOI // LOOK_AZ // tiles
    for r in range(rounds):
        pr, pi = partner_refs[r][:AOI], partner_refs[r][AOI:]
        for c, field in enumerate((mr * pr + mi * pi, mi * pr - mr * pi)):
            looked = looked_at(field, look_ref[...])
            at = (c * rounds + r) * per
            for t in range(tiles):
                out[t, at : at + per, :] = looked[t * per : (t + 1) * per]


def cross_call(mine, partners, tiles):
    rounds = len(partners)
    width = mine.shape[1]
    look = jnp.asarray(look_table(width, 0))
    shape = (tiles, 2 * rounds * (AOI // LOOK_AZ // tiles), LANES)
    vmem = lambda: pl.BlockSpec(memory_space=pltpu.VMEM)
    return pl.pallas_call(
        functools.partial(cross_kernel, rounds, tiles),
        in_specs=[vmem() for _ in range(rounds + 2)],
        out_specs=vmem(),
        out_shape=jax.ShapeDtypeStruct(shape, jnp.float32),
        compiler_params=pltpu.CompilerParams(vmem_limit_bytes=VMEM_LIMIT),
        name="interferogram",
    )(mine, *partners, look)


def place_kernel(sources, valid, parts, in_ref, out):
    rows = in_ref.shape[1]
    lane = lax.broadcasted_iota(jnp.int32, (rows, LANES), 1)
    for c in range(parts):
        for o in range(len(sources) * valid // LANES):
            acc = None
            for place, source in enumerate(sources):
                shift = place * valid - o * LANES
                if shift + valid <= 0 or shift >= LANES:
                    continue
                value = in_ref[source]
                turn_by = (shift - c * valid) % LANES
                if turn_by:
                    value = pltpu.roll(value, turn_by, 1)
                acc = value if acc is None else jnp.where(lane >= shift, value, acc)
            out[c * rows : (c + 1) * rows, o * LANES : (o + 1) * LANES] = acc


def place_call(received, sources, valid, parts):
    _, rows, _ = received.shape
    return pl.pallas_call(
        functools.partial(place_kernel, sources, valid, parts),
        in_specs=[pl.BlockSpec(memory_space=pltpu.VMEM)],
        out_specs=pl.BlockSpec(memory_space=pltpu.VMEM),
        out_shape=jax.ShapeDtypeStruct((parts * rows, len(sources) * valid), jnp.float32),
        compiler_params=pltpu.CompilerParams(vmem_limit_bytes=VMEM_LIMIT),
        name="place_samples",
    )(received)


def turn(array, axes):
    return lax.all_to_all(array, axes, split_axis=0, concat_axis=0, tiled=True)


def by_block(array):
    dests, steps, rows, _ = array.shape
    return array.reshape(dests, steps, 2, rows // (2 * SUB), SUB, LANES)


def joint(tiles, echo, slant, angle, pairs):
    steps = echo.shape[2] // SUB
    columns = angle.shape[1]
    rounds = pairs.shape[0]
    acq = lax.axis_index("acq")
    side = acq.astype(jnp.int32).reshape(1)
    same = (lax.dynamic_index_in_dim(pairs, acq, 1, keepdims=False) == acq).astype(jnp.int32)
    theirs = lax.dynamic_slice_in_dim(angle, (1 - acq) * (columns // 2), columns // 2, 1)
    other_angle = lax.ppermute(theirs, "acq", [(0, 1), (1, 0)])
    low = lax.axis_size("low")
    order = [h * low + k for k in range(low) for h in range(tiles // low)]
    axes = ("acq", "low", "high")
    tile = lax.axis_index("high") * low + lax.axis_index("low")
    me = jnp.stack([acq, tile]).astype(jnp.int32)
    kept, given = range_call(echo, slant, me, 0, 1, order, 2, early=True)
    came = lax.ppermute(given, "high", [(h, h ^ (FAR // 2)) for h in range(FAR)])
    (sent,) = range_call(echo, slant, me, 1, steps - 1, order, 2)
    array = by_block(turn(sent, axes))
    early = list(pair_call(kept, came))
    near = tiles // 2
    for s in range(1, tiles):
        flip = s // near * tiles + s % near
        early[s] = lax.ppermute(early[s], ("acq", "high", "low"), [(i, i ^ flip) for i in range(2 * tiles)])
    early = by_block(jnp.stack(early))
    trig = trig_call(side, angle, other_angle)
    looked = joint_call(me, same, array, early, trig, azimuth_tables(angle.shape[0]), order)
    sources = [half * tiles + order.index(t) for t in range(tiles) for half in range(2)]
    result = place_call(turn(looked, axes), sources, columns // 2 // LOOK_RG, 2)
    return result.reshape(2, rounds, 1, -1, result.shape[1])


def separate(tiles, echo, slant, angle, pairs):
    columns = angle.shape[1]
    rounds = pairs.shape[0]
    (sent,) = range_call(echo, slant, jnp.zeros((2,), jnp.int32), 0, echo.shape[2] // SUB, list(range(tiles)), 1)
    mine = single_call(by_block(turn(sent, ("high", "low"))), angle, azimuth_tables(angle.shape[0]))
    every = lax.all_gather(mine, "acq", axis=0)
    partner = lax.dynamic_index_in_dim(pairs, lax.axis_index("acq"), 1, keepdims=False)
    partners = [lax.dynamic_index_in_dim(every, partner[r], 0, keepdims=False) for r in range(rounds)]
    looked = turn(cross_call(mine, partners, tiles), ("high", "low"))
    result = place_call(looked, list(range(tiles)), columns // LOOK_RG, 1)
    return result.reshape(2, rounds, 1, -1, result.shape[1])


def shards(tiles, acqs, echo, slant, angle, pairs):
    fits = echo.shape[2] > SUB and tiles == FAR * FAR and angle.shape[2] % (6 * LANES) == 0 and AOI // LOOK_AZ % (tiles * SUB) == 0
    program = joint if acqs == 2 and fits else separate
    return program(tiles, echo, slant, angle[0], pairs)


def solution(mesh):
    acqs, tiles = mesh.shape["acq"], mesh.shape["tile"]
    low = 1 << (tiles.bit_length() // 2)
    low = low if tiles % low == 0 else 1
    split_mesh = jax.sharding.Mesh(mesh.devices.reshape(acqs, tiles // low, low), ("acq", "high", "low"))
    tile = ("high", "low")
    in_specs = (P(None, "acq", tile, None), P(None, "acq", None), P("acq", None, tile), P())
    out_specs = P(None, None, "acq", tile, None)
    body = functools.partial(shards, tiles, acqs)
    return jax.shard_map(body, mesh=split_mesh, in_specs=in_specs, out_specs=out_specs, check_vma=False)
```

time: 530 us -> 146 us (0.28); the launches traced: 520 us -> 146 us
  local copies, waits for them, and re-layouts: 183 us -> 2.77 us
  matrix products: 107 us -> 0 us
  other arithmetic: 51.8 us -> 1.36 us
  blocking collectives: 57.6 us -> 14.7 us
  Pallas kernels: 0 us -> 36.6 us
  waiting for transfers between devices: 94.6 us -> 59.7 us
  starting transfers between devices: 7.75 us -> 30.6 us
  between operations: 18.1 us -> 0.15 us
    dot_general x32 -> x0, matrix products: 107 us -> none  [the longest x8 28.8 us: complex_contract(): jnp.einsum(subscripts, imag_in, mat_real, precision=precision_mode)]
    all_to_all x1, waiting for transfers between devices: 70.9 us -> 0.01 us  [turn(): return lax.all_to_all(array, axes, split_axis=0, concat_axis=0, tiled=True)]
    ppermute x0 -> x17, waiting for transfers between devices: none -> 59.7 us  [the longest x15 59.7 us: joint(): lax.ppermute(early[s], ('acq', 'high', 'low'), [(i, i ^ flip) for i in ra...]
    unnamed x23, local copies, waits for them, and re-layouts: 55.8 us -> 1.65 us
    squeeze x2 -> x0, local copies, waits for them, and re-layouts: 48.5 us -> none  [shards(): cross_real = self_real * partner_data[:, 0] + self_imag * partner_data[:, 1]]
    all_to_all x1, blocking collectives: 57.6 us -> 14.7 us  [turn(): return lax.all_to_all(array, axes, split_axis=0, concat_axis=0, tiled=True)]
    pallas_call x0 -> x6, Pallas kernels: none -> 36.6 us  [the longest x2 15.3 us: range_call(): pl.pallas_call(functools.partial(range_kernel, outer, early), grid_spec=p...]
    ppermute x0 -> x17, starting transfers between devices: none -> 26.6 us  [the longest x15 20.9 us: joint(): lax.ppermute(early[s], ('acq', 'high', 'low'), [(i, i ^ flip) for i in ra...]
  transfers between devices with their start and end apart: 2 -> 18, of which waited for: 2 -> 6; matrix products, arithmetic and copies ran while one was open for 6% -> 2% of each run, Pallas kernels for 0% -> 13%
where the time goes in v1:
time: 146 us
  waiting for transfers between devices  59.7 us (41%)
  Pallas kernels  36.6 us (25%)
  starting transfers between devices  30.6 us (21%)
  blocking collectives  14.7 us (10%)
  local copies, waits for them, and re-layouts  2.77 us (2%)
    ppermute x15, waiting for transfers between devices, joint(): lax.ppermute(early[s], ('acq', 'high', 'low'), [(i, i ^ flip) for i in ra...  59.7 us
    ppermute x15, starting transfers between devices, joint(): lax.ppermute(early[s], ('acq', 'high', 'low'), [(i, i ^ flip) for i in ra...  20.9 us
    pallas_call x2, Pallas kernels, range_call(): pl.pallas_call(functools.partial(range_kernel, outer, early), grid_spec=p...  15.3 us
    all_to_all x1, blocking collectives, turn(): return lax.all_to_all(array, axes, split_axis=0, concat_axis=0, tiled=True)  14.7 us
    pallas_call x1, Pallas kernels, joint_call(): pl.pallas_call(functools.partial(joint_kernel, order, rounds), grid_spec=...  11.6 us
    pallas_call x1, Pallas kernels, trig_call(): pl.pallas_call(trig_kernel, grid_spec=pltpu.PrefetchScalarGridSpec(num_sc...  5.86 us
    ppermute x1, starting transfers between devices, joint(): came = lax.ppermute(given, 'high', [(h, h ^ FAR // 2) for h in range(FAR)])  4.03 us
    all_to_all x1, starting transfers between devices, turn(): return lax.all_to_all(array, axes, split_axis=0, concat_axis=0, tiled=True)  3.94 us
  transfers between devices with their start and end apart: 18, of which 6 were waited for; matrix products, arithmetic and copies ran while one was open for 2% of the time, Pallas kernels for 13%

profile of v1, /device:TPU:0, one launch (start us, length us, event | category | flops | bytes accessed | tf_op | source)
XLA Modules:
  0.0 145.9 jit_solution(10151945102732318902)
XLA Ops:
  0.7 4.5 %range_compress_0.1 = (f32[16,1,48,128]{3,2,1,0:T(8,128)}, f32[16,1,48,128]{3,2,1,0:T(8,128)}) custom-call(s32[2]{0:T(128)} %pad_add_fusion.me_ref, f32[2,6,768,128]{3,2,1,0:T(8,128)} %bitcast.31, f32[2,1,12288]{2,1,0:T(1,128)} %slant_ref.3, bf16[3,128,128]{2,1,0:T(8,128)(2,1)} %constant.45.clone.a1_ref, bf16[768,256]{1,0:T(8,128)(2,1)} %constant.46.clone.b2_ref, ...), custom_call_target="tpu_custom_call" | custom-call | flops 1056964608 | bytes 1572864 | tf_op jit(solution)/shard_map/range_compress_0/pallas_call | solution.py:190
  5.1 4.0 %collective-permute-start = (f32[16,1,48,128]{3,2,1,0:T(8,128)}, f32[16,1,48,128]{3,2,1,0:T(8,128)S(1)}, u32[]{:S(2)}, u32[]{:S(2)}) collective-permute-start(f32[16,1,48,128]{3,2,1,0:T(8,128)} %get-tuple-element.24), channel_id=1, source_target_pairs={{0,8},{4,12},{8,0},{12,4},{1,9},{5,13},{9,1},{13,5},{2,10},{6,14},... | collective-permute-start | bytes 1179656 | tf_op jit(solution)/shard_map/ppermute | solution.py:542
  9.2 10.8 %range_compress_1.1 = f32[32,5,48,128]{3,2,1,0:T(8,128)} custom-call(s32[2]{0:T(128)} %pad_add_fusion.me_ref, f32[2,6,768,128]{3,2,1,0:T(8,128)} %bitcast.32, f32[2,1,12288]{2,1,0:T(1,128)} %slant_ref.3, bf16[3,128,128]{2,1,0:T(8,128)(2,1)} %constant.45.clone.a1_ref, bf16[768,256]{1,0:T(8,128)(2,1)} %constant.46.clone.b2_ref, ...), custom_call_target="tpu_custom_call" | custom-call | flops 5284823040 | bytes 7864320 | tf_op jit(solution)/shard_map/range_compress_1/pallas_call | solution.py:190
  20.0 3.9 %all-to-all-start = ((f32[32,5,48,128]{3,2,1,0:T(8,128)}), f32[32,5,48,128]{3,2,1,0:T(8,128)}, u32[]{:S(2)}, u32[]{:S(2)}) async-start(f32[32,5,48,128]{3,2,1,0:T(8,128)} %range_compress_1.1), calls=%async_computation | async-start | bytes 7864320 | tf_op jit(solution)/shard_map/all_to_all | solution.py:519
  24.0 1.1 dynamic-slice_bitcast_fusion
  25.1 1.7 %collective-permute-start.16 = (f32[768,384]{1,0:T(8,128)}, f32[768,384]{1,0:T(8,128)}, u32[]{:S(2)}, u32[]{:S(2)}) collective-permute-start(f32[768,384]{1,0:T(8,128)} %dynamic-slice_bitcast_fusion), channel_id=1, source_target_pairs={{0,16},{16,0},{1,17},{17,1},{2,18},{18,2},{3,19},{19,3},{4,20},{20... | collective-permute-start | bytes 3538952 | tf_op jit(solution)/shard_map/ppermute | solution.py:535
  26.8 0.7 fusion.same_ref
  27.5 0.8 copy-done.3
  28.3 2.0 %pair_halves.1 = (f32[2,48,128]{2,1,0:T(8,128)}, f32[2,48,128]{2,1,0:T(8,128)}, f32[2,48,128]{2,1,0:T(8,128)}, f32[2,48,128]{2,1,0:T(8,128)}, f32[2,48,128]{2,1,...) custom-call(f32[16,1,48,128]{3,2,1,0:T(8,128)} %get-tuple-element.23, ...), custom_call_target="tpu_custom_call" | custom-call | flops 999999995904 | bytes 393216 | tf_op jit(solution)/shard_map/pair_halves/pallas_call | solution.py:222
  30.3 0.8 constant_dynamic-update-slice_fusion.15
  31.1 1.5 %collective-permute-start.2 = (f32[2,48,128]{2,1,0:T(8,128)}, f32[2,48,128]{2,1,0:T(8,128)S(1)}, u32[]{:S(2)}, u32[]{:S(2)}) collective-permute-start(f32[2,48,128]{2,1,0:T(8,128)} %get-tuple-element.27), channel_id=1, source_target_pairs={{0,2},{1,3},{2,0},{3,1},{4,6},{5,7},{6,4},{7,5},{8,10},{9,11},{10,... | collective-permute-start | bytes 147464 | tf_op jit(solution)/shard_map/ppermute | solution.py:549
  33.0 1.5 %collective-permute-start.4 = (f32[2,48,128]{2,1,0:T(8,128)}, f32[2,48,128]{2,1,0:T(8,128)S(1)}, u32[]{:S(2)}, u32[]{:S(2)}) collective-permute-start(f32[2,48,128]{2,1,0:T(8,128)} %get-tuple-element.29), channel_id=1, source_target_pairs={{0,4},{1,5},{2,6},{3,7},{4,0},{5,1},{6,2},{7,3},{8,12},{9,13},{10,... | collective-permute-start | bytes 147464 | tf_op jit(solution)/shard_map/ppermute | solution.py:549
  34.6 20.6 %collective-permute-done.2 = f32[2,48,128]{2,1,0:T(8,128)S(1)} collective-permute-done((f32[2,48,128]{2,1,0:T(8,128)}, f32[2,48,128]{2,1,0:T(8,128)S(1)}, u32[]{:S(2)}, u32[]{:S(2)}) %collective-permute-start.2) | collective-permute-done | bytes 49184 | tf_op jit(solution)/shard_map/ppermute | solution.py:549
  55.4 34.9 %collective-permute-done.4 = f32[2,48,128]{2,1,0:T(8,128)S(1)} collective-permute-done((f32[2,48,128]{2,1,0:T(8,128)}, f32[2,48,128]{2,1,0:T(8,128)S(1)}, u32[]{:S(2)}, u32[]{:S(2)}) %collective-permute-start.4) | collective-permute-done | bytes 49184 | tf_op jit(solution)/shard_map/ppermute | solution.py:549
  90.3 1.5 %collective-permute-start.8 = (f32[2,48,128]{2,1,0:T(8,128)}, f32[2,48,128]{2,1,0:T(8,128)S(1)}, u32[]{:S(2)}, u32[]{:S(2)}) collective-permute-start(f32[2,48,128]{2,1,0:T(8,128)} %get-tuple-element.33), channel_id=1, source_target_pairs={{0,16},{1,17},{2,18},{3,19},{4,20},{5,21},{6,22},{7,23},{8,24},{9,... | collective-permute-start | bytes 147464 | tf_op jit(solution)/shard_map/ppermute | solution.py:549
  92.4 4.0 %collective-permute-start.10 = (f32[2,48,128]{2,1,0:T(8,128)}, f32[2,48,128]{2,1,0:T(8,128)S(1)}, u32[]{:S(2)}, u32[]{:S(2)}) collective-permute-start(f32[2,48,128]{2,1,0:T(8,128)} %get-tuple-element.35), channel_id=1, source_target_pairs={{0,18},{1,19},{2,16},{3,17},{4,22},{5,23},{6,20},{7,21},{8,26},{9,... | collective-permute-start | bytes 147464 | tf_op jit(solution)/shard_map/ppermute | solution.py:549
  96.5 4.0 %collective-permute-start.12 = (f32[2,48,128]{2,1,0:T(8,128)}, f32[2,48,128]{2,1,0:T(8,128)S(1)}, u32[]{:S(2)}, u32[]{:S(2)}) collective-permute-start(f32[2,48,128]{2,1,0:T(8,128)} %get-tuple-element.37), channel_id=1, source_target_pairs={{0,20},{1,21},{2,22},{3,23},{4,16},{5,17},{6,18},{7,19},{8,28},{9,... | collective-permute-start | bytes 147464 | tf_op jit(solution)/shard_map/ppermute | solution.py:549
  101.1 2.8 %collective-permute-start.14 = (f32[2,48,128]{2,1,0:T(8,128)}, f32[2,48,128]{2,1,0:T(8,128)S(1)}, u32[]{:S(2)}, u32[]{:S(2)}) collective-permute-start(f32[2,48,128]{2,1,0:T(8,128)} %get-tuple-element.39), channel_id=1, source_target_pairs={{0,22},{1,23},{2,20},{3,21},{4,18},{5,19},{6,16},{7,17},{8,30},{9,... | collective-permute-start | bytes 147464 | tf_op jit(solution)/shard_map/ppermute | solution.py:549
  104.0 4.3 %collective-permute-start.15 = (f32[2,48,128]{2,1,0:T(8,128)}, f32[2,48,128]{2,1,0:T(8,128)S(1)}, u32[]{:S(2)}, u32[]{:S(2)}) collective-permute-start(f32[2,48,128]{2,1,0:T(8,128)} %get-tuple-element.40), channel_id=1, source_target_pairs={{0,23},{1,22},{2,21},{3,20},{4,19},{5,18},{6,17},{7,16},{8,31},{9,... | collective-permute-start | bytes 147464 | tf_op jit(solution)/shard_map/ppermute | solution.py:549
  108.4 3.5 %collective-permute-done.15 = f32[2,48,128]{2,1,0:T(8,128)S(1)} collective-permute-done((f32[2,48,128]{2,1,0:T(8,128)}, f32[2,48,128]{2,1,0:T(8,128)S(1)}, u32[]{:S(2)}, u32[]{:S(2)}) %collective-permute-start.15) | collective-permute-done | bytes 49184 | tf_op jit(solution)/shard_map/ppermute | solution.py:549
  111.9 5.9 %angle_phases.1.trig_ref = f32[3,2,6,128,256]{4,3,2,1,0:T(8,128)} custom-call(s32[1]{0:T(128)} %bitcast._, f32[768,768]{1,0:T(8,128)} %bitcast.30, f32[768,384]{1,0:T(8,128)} %collective-permute-done.16.other_ref), custom_call_target="tpu_custom_call" | custom-call | flops 18874368 | bytes 7077888 | tf_op jit(solution)/shard_map/angle_phases/pallas_call | solution.py:329
  117.7 11.6 %azimuth_interferogram.1 = f32[32,16,128]{2,1,0:T(8,128)} custom-call(s32[2]{0:T(128)} %pad_add_fusion.me_ref, s32[2]{0:T(128)} %fusion.same_ref, f32[32,5,2,3,8,128]{5,4,3,2,1,0:T(8,128)} %bitcast.5.x_ref, f32[16,2,2,3,8,128]{5,4,3,2,1,0:T(8,128)} %copy-done.1, f32[3,2,6,128,256]{4,3,2,1,0:T(8,128)} %angle_phases.1.trig_ref, ...), custom_call_target="tpu_custom_call" | custom-call | flops 3623878656 | bytes 11796480 | tf_op jit(solution)/shard_map/azimuth_interferogram/pallas_call | solution.py:402
  129.3 14.7 %all_to_all.10.in_ref = f32[32,16,128]{2,1,0:T(8,128)} all-to-all(f32[32,16,128]{2,1,0:T(8,128)} %azimuth_interferogram.1), channel_id=1, replica_groups=mesh['acq'=2,'high'=4,'low'=4] {'acq','low','high'}, dimensions={0} | all-to-all | bytes 524288 | tf_op jit(solution)/shard_map/all_to_all | solution.py:519
  144.0 1.8 %place_samples.1 = f32[32,1536]{1,0:T(8,128)} custom-call(f32[32,16,128]{2,1,0:T(8,128)} %all_to_all.10.in_ref), custom_call_target="tpu_custom_call" | custom-call | tf_op jit(solution)/shard_map/place_samples/pallas_call | solution.py:508
  (46 shorter events, 2.9 us)
Async XLA Ops:
  5.1 22.4 %collective-permute-start = (f32[16,1,48,128]{3,2,1,0:T(8,128)}, f32[16,1,48,128]{3,2,1,0:T(8,128)S(1)}, u32[]{:S(2)}, u32[]{:S(2)}) collective-permute-start(f32[16,1,48,128]{3,2,1,0:T(8,128)} %get-tuple-element.24), channel_id=1, source_target_pairs={{0,8},{4,12},{8,0},{12,4},{1,9},{5,13},{9,1},{13,5},{2,10},{6,14},... | collective-permute-start | bytes 1179656 | tf_op jit(solution)/shard_map/ppermute | solution.py:542
  20.0 4.0 %copy-start = (f32[1,768,768]{2,1,0:T(8,128)S(1)}, f32[1,768,768]{2,1,0:T(8,128)}, u32[]{:S(2)}) copy-start(f32[1,768,768]{2,1,0:T(8,128)} %param.19) | copy-start | bytes 7077892
  20.0 97.7 %all-to-all-start = ((f32[32,5,48,128]{3,2,1,0:T(8,128)}), f32[32,5,48,128]{3,2,1,0:T(8,128)}, u32[]{:S(2)}, u32[]{:S(2)}) async-start(f32[32,5,48,128]{3,2,1,0:T(8,128)} %range_compress_1.1), calls=%async_computation | async-start | bytes 7864320 | tf_op jit(solution)/shard_map/all_to_all | solution.py:519
  24.0 2.9 %copy-start.2 = (s32[2,2]{1,0:T(2,128)S(1)}, s32[2,2]{1,0:T(2,128)}, u32[]{:S(2)}) copy-start(s32[2,2]{1,0:T(2,128)} %param.20) | copy-start | bytes 52
  25.1 86.8 %collective-permute-start.16 = (f32[768,384]{1,0:T(8,128)}, f32[768,384]{1,0:T(8,128)}, u32[]{:S(2)}, u32[]{:S(2)}) collective-permute-start(f32[768,384]{1,0:T(8,128)} %dynamic-slice_bitcast_fusion), channel_id=1, source_target_pairs={{0,16},{16,0},{1,17},{17,1},{2,18},{18,2},{3,19},{19,3},{4,20},{20... | collective-permute-start | bytes 3538952 | tf_op jit(solution)/shard_map/ppermute | solution.py:535
  27.5 0.8 copy-start.3
  30.3 4.2 %collective-permute-start.1 = (f32[2,48,128]{2,1,0:T(8,128)}, f32[2,48,128]{2,1,0:T(8,128)S(1)}, u32[]{:S(2)}, u32[]{:S(2)}) collective-permute-start(f32[2,48,128]{2,1,0:T(8,128)} %get-tuple-element.26), channel_id=1, source_target_pairs={{0,1},{1,0},{2,3},{3,2},{4,5},{5,4},{6,7},{7,6},{8,9},{9,8},{10,11... | collective-permute-start | bytes 147464 | tf_op jit(solution)/shard_map/ppermute | solution.py:549
  31.1 24.1 %collective-permute-start.2 = (f32[2,48,128]{2,1,0:T(8,128)}, f32[2,48,128]{2,1,0:T(8,128)S(1)}, u32[]{:S(2)}, u32[]{:S(2)}) collective-permute-start(f32[2,48,128]{2,1,0:T(8,128)} %get-tuple-element.27), channel_id=1, source_target_pairs={{0,2},{1,3},{2,0},{3,1},{4,6},{5,7},{6,4},{7,5},{8,10},{9,11},{10,... | collective-permute-start | bytes 147464 | tf_op jit(solution)/shard_map/ppermute | solution.py:549
  32.6 22.8 %collective-permute-start.3 = (f32[2,48,128]{2,1,0:T(8,128)}, f32[2,48,128]{2,1,0:T(8,128)S(1)}, u32[]{:S(2)}, u32[]{:S(2)}) collective-permute-start(f32[2,48,128]{2,1,0:T(8,128)} %get-tuple-element.28), channel_id=1, source_target_pairs={{0,3},{1,2},{2,1},{3,0},{4,7},{5,6},{6,5},{7,4},{8,11},{9,10},{10,... | collective-permute-start | bytes 147464 | tf_op jit(solution)/shard_map/ppermute | solution.py:549
  33.0 57.3 %collective-permute-start.4 = (f32[2,48,128]{2,1,0:T(8,128)}, f32[2,48,128]{2,1,0:T(8,128)S(1)}, u32[]{:S(2)}, u32[]{:S(2)}) collective-permute-start(f32[2,48,128]{2,1,0:T(8,128)} %get-tuple-element.29), channel_id=1, source_target_pairs={{0,4},{1,5},{2,6},{3,7},{4,0},{5,1},{6,2},{7,3},{8,12},{9,13},{10,... | collective-permute-start | bytes 147464 | tf_op jit(solution)/shard_map/ppermute | solution.py:549
  34.4 57.4 %collective-permute-start.5 = (f32[2,48,128]{2,1,0:T(8,128)}, f32[2,48,128]{2,1,0:T(8,128)S(1)}, u32[]{:S(2)}, u32[]{:S(2)}) collective-permute-start(f32[2,48,128]{2,1,0:T(8,128)} %get-tuple-element.30), channel_id=1, source_target_pairs={{0,5},{1,4},{2,7},{3,6},{4,1},{5,0},{6,3},{7,2},{8,13},{9,12},{10,... | collective-permute-start | bytes 147464 | tf_op jit(solution)/shard_map/ppermute | solution.py:549
  55.2 37.2 %collective-permute-start.6 = (f32[2,48,128]{2,1,0:T(8,128)}, f32[2,48,128]{2,1,0:T(8,128)S(1)}, u32[]{:S(2)}, u32[]{:S(2)}) collective-permute-start(f32[2,48,128]{2,1,0:T(8,128)} %get-tuple-element.31), channel_id=1, source_target_pairs={{0,6},{1,7},{2,4},{3,5},{4,2},{5,3},{6,0},{7,1},{8,14},{9,15},{10,... | collective-permute-start | bytes 147464 | tf_op jit(solution)/shard_map/ppermute | solution.py:549
  55.4 41.1 %collective-permute-start.7 = (f32[2,48,128]{2,1,0:T(8,128)}, f32[2,48,128]{2,1,0:T(8,128)S(1)}, u32[]{:S(2)}, u32[]{:S(2)}) collective-permute-start(f32[2,48,128]{2,1,0:T(8,128)} %get-tuple-element.32), channel_id=1, source_target_pairs={{0,7},{1,6},{2,5},{3,4},{4,3},{5,2},{6,1},{7,0},{8,15},{9,14},{10,... | collective-permute-start | bytes 147464 | tf_op jit(solution)/shard_map/ppermute | solution.py:549
  90.3 6.2 %collective-permute-start.8 = (f32[2,48,128]{2,1,0:T(8,128)}, f32[2,48,128]{2,1,0:T(8,128)S(1)}, u32[]{:S(2)}, u32[]{:S(2)}) collective-permute-start(f32[2,48,128]{2,1,0:T(8,128)} %get-tuple-element.33), channel_id=1, source_target_pairs={{0,16},{1,17},{2,18},{3,19},{4,20},{5,21},{6,22},{7,23},{8,24},{9,... | collective-permute-start | bytes 147464 | tf_op jit(solution)/shard_map/ppermute | solution.py:549
  91.8 8.7 %collective-permute-start.9 = (f32[2,48,128]{2,1,0:T(8,128)}, f32[2,48,128]{2,1,0:T(8,128)S(1)}, u32[]{:S(2)}, u32[]{:S(2)}) collective-permute-start(f32[2,48,128]{2,1,0:T(8,128)} %get-tuple-element.34), channel_id=1, source_target_pairs={{0,17},{1,16},{2,19},{3,18},{4,21},{5,20},{6,23},{7,22},{8,25},{9,... | collective-permute-start | bytes 147464 | tf_op jit(solution)/shard_map/ppermute | solution.py:549
  92.4 8.7 %collective-permute-start.10 = (f32[2,48,128]{2,1,0:T(8,128)}, f32[2,48,128]{2,1,0:T(8,128)S(1)}, u32[]{:S(2)}, u32[]{:S(2)}) collective-permute-start(f32[2,48,128]{2,1,0:T(8,128)} %get-tuple-element.35), channel_id=1, source_target_pairs={{0,18},{1,19},{2,16},{3,17},{4,22},{5,23},{6,20},{7,21},{8,26},{9,... | collective-permute-start | bytes 147464 | tf_op jit(solution)/shard_map/ppermute | solution.py:549
  96.4 7.5 %collective-permute-start.11 = (f32[2,48,128]{2,1,0:T(8,128)}, f32[2,48,128]{2,1,0:T(8,128)S(1)}, u32[]{:S(2)}, u32[]{:S(2)}) collective-permute-start(f32[2,48,128]{2,1,0:T(8,128)} %get-tuple-element.36), channel_id=1, source_target_pairs={{0,19},{1,18},{2,17},{3,16},{4,23},{5,22},{6,21},{7,20},{8,27},{9,... | collective-permute-start | bytes 147464 | tf_op jit(solution)/shard_map/ppermute | solution.py:549
  96.5 11.7 %collective-permute-start.12 = (f32[2,48,128]{2,1,0:T(8,128)}, f32[2,48,128]{2,1,0:T(8,128)S(1)}, u32[]{:S(2)}, u32[]{:S(2)}) collective-permute-start(f32[2,48,128]{2,1,0:T(8,128)} %get-tuple-element.37), channel_id=1, source_target_pairs={{0,20},{1,21},{2,22},{3,23},{4,16},{5,17},{6,18},{7,19},{8,28},{9,... | collective-permute-start | bytes 147464 | tf_op jit(solution)/shard_map/ppermute | solution.py:549
  100.5 7.8 %collective-permute-start.13 = (f32[2,48,128]{2,1,0:T(8,128)}, f32[2,48,128]{2,1,0:T(8,128)S(1)}, u32[]{:S(2)}, u32[]{:S(2)}) collective-permute-start(f32[2,48,128]{2,1,0:T(8,128)} %get-tuple-element.38), channel_id=1, source_target_pairs={{0,21},{1,20},{2,23},{3,22},{4,17},{5,16},{6,19},{7,18},{8,29},{9,... | collective-permute-start | bytes 147464 | tf_op jit(solution)/shard_map/ppermute | solution.py:549
  101.1 7.2 %collective-permute-start.14 = (f32[2,48,128]{2,1,0:T(8,128)}, f32[2,48,128]{2,1,0:T(8,128)S(1)}, u32[]{:S(2)}, u32[]{:S(2)}) collective-permute-start(f32[2,48,128]{2,1,0:T(8,128)} %get-tuple-element.39), channel_id=1, source_target_pairs={{0,22},{1,23},{2,20},{3,21},{4,18},{5,19},{6,16},{7,17},{8,30},{9,... | collective-permute-start | bytes 147464 | tf_op jit(solution)/shard_map/ppermute | solution.py:549
  104.0 7.9 %collective-permute-start.15 = (f32[2,48,128]{2,1,0:T(8,128)}, f32[2,48,128]{2,1,0:T(8,128)S(1)}, u32[]{:S(2)}, u32[]{:S(2)}) collective-permute-start(f32[2,48,128]{2,1,0:T(8,128)} %get-tuple-element.40), channel_id=1, source_target_pairs={{0,23},{1,22},{2,21},{3,20},{4,19},{5,18},{6,17},{7,16},{8,31},{9,... | collective-permute-start | bytes 147464 | tf_op jit(solution)/shard_map/ppermute | solution.py:549
  111.9 5.9 %copy-start.1 = (f32[16,2,2,3,8,128]{5,4,3,2,1,0:T(8,128)}, f32[16,2,2,3,8,128]{5,4,3,2,1,0:T(8,128)S(1)}, u32[]{:S(2)}) copy-start(f32[16,2,2,3,8,128]{5,4,3,2,1,0:T(8,128)S(1)} %constant_dynamic-update-slice_fusion.early_ref) | copy-start | bytes 2359300

commit v2 on v1

--- a/solution.py
+++ b/solution.py
@@ -100,7 +100,7 @@
     return lax.rem(tile, low) * FAR + lax.div(tile, low)
 
 
-def range_kernel(outer, early, me_ref, x_ref, slant_ref, a1_ref, b2_ref, b3_ref, a4_ref, t_ref, *rest):
+def range_kernel(outer, early, x_ref, slant_ref, a1_ref, b2_ref, b3_ref, a4_ref, t_ref, *rest):
     outs, (rows_ref, h_ref), held = rest[: 1 + early], rest[1 + early : 3 + early], rest[3 + early :]
     part = outer // 3
 
@@ -170,44 +170,43 @@
     if not early:
         return
     near = outs[0].shape[0] // 2
+    acq = lax.axis_index("acq")
+    place = lax.axis_index("high") * (2 * near // FAR) + lax.axis_index("low")
     for k, out in enumerate(outs):
         for s in range(2 * near):
-            tile = jnp.bitwise_xor(me_ref[1], s % near + k * near)
-            dest = jnp.bitwise_xor(me_ref[0], s // near) * 2 * near + spot(tile, 2 * near // FAR)
+            tile = jnp.bitwise_xor(place, s % near + k * near)
+            dest = jnp.bitwise_xor(acq, s // near) * 2 * near + spot(tile, 2 * near // FAR)
             out[s, 0] = turned[pl.ds(pl.multiple_of(dest * rows, SUB), rows), :]
 
 
-def range_call(echo, slant, me, first, steps, order, halves, early=False):
+def range_call(echo, slant, first, steps, order, halves, early=False):
     length = echo.shape[3]
     outer = length // LANES
     view = echo.reshape(2, -1, SUB, outer, LANES).transpose(0, 1, 3, 2, 4).reshape(2, -1, outer * SUB, LANES)
     tables = [slant, *range_tables(length, order, halves)]
     dests = len(order) * halves
     rows = 2 * outer // dests * SUB
-    whole = lambda shape: pl.BlockSpec(shape, lambda s, me: (0,) * len(shape))
+    whole = lambda shape: pl.BlockSpec(shape, lambda s: (0,) * len(shape))
     macs = steps * SUB * length * 2 * (2 * outer + 2 * LANES) * 2 * 3
     outs = 1 + early
     return pl.pallas_call(
         functools.partial(range_kernel, outer, early),
-        grid_spec=pltpu.PrefetchScalarGridSpec(
-            num_scalar_prefetch=1,
-            grid=(steps,),
-            in_specs=[pl.BlockSpec((2, 1, outer * SUB, LANES), lambda s, me: (0, first + s, 0, 0))]
-            + [whole(t.shape) for t in tables],
-            out_specs=[pl.BlockSpec((dests // outs, 1, rows, LANES), lambda s, me: (0, s, 0, 0))] * outs,
-            scratch_shapes=[
-                pltpu.VMEM((2, LANES, LANES), jnp.float32),
-                pltpu.VMEM((2, outer, LANES), jnp.float32),
-            ]
-            + [pltpu.VMEM((dests * rows, LANES), jnp.float32)] * early,
-        ),
+        grid=(steps,),
+        in_specs=[pl.BlockSpec((2, 1, outer * SUB, LANES), lambda s: (0, first + s, 0, 0))]
+        + [whole(t.shape) for t in tables],
+        out_specs=[pl.BlockSpec((dests // outs, 1, rows, LANES), lambda s: (0, s, 0, 0))] * outs,
+        scratch_shapes=[
+            pltpu.VMEM((2, LANES, LANES), jnp.float32),
+            pltpu.VMEM((2, outer, LANES), jnp.float32),
+        ]
+        + [pltpu.VMEM((dests * rows, LANES), jnp.float32)] * early,
         out_shape=[jax.ShapeDtypeStruct((dests // outs, steps, rows, LANES), jnp.float32)] * outs,
         compiler_params=pltpu.CompilerParams(vmem_limit_bytes=VMEM_LIMIT),
         cost_estimate=pl.CostEstimate(
             flops=2 * macs, bytes_accessed=16 * steps * SUB * length, transcendentals=0
         ),
         name=f"range_compress_{first}",
-    )(me, view, *[jnp.asarray(t) for t in tables])
+    )(view, *[jnp.asarray(t) for t in tables])
 
 
 def pair_kernel(kept_ref, came_ref, *outs):
@@ -315,38 +314,7 @@
     return dot(high, look) + dot(low, look)
 
 
-def trig_kernel(_, own_ref, other_ref, out):
-    part = own_ref.shape[0] // 6
-    for k in range(6):
-        angle = jnp.concatenate([a[pl.ds(k, part, stride=6), :] for a in (own_ref, other_ref)], axis=1)
-        out[0, 0, k], out[0, 1, k] = cos_sin(angle)
-
-
-def trig_call(acq, angle, other_angle):
-    lines, width = other_angle.shape
-    blocks = width // LANES
-    shape = (2, 6, lines // 6, 2 * LANES)
-    return pl.pallas_call(
-        trig_kernel,
-        grid_spec=pltpu.PrefetchScalarGridSpec(
-            num_scalar_prefetch=1,
-            grid=(blocks,),
-            in_specs=[
-                pl.BlockSpec((lines, LANES), lambda b, acq: (0, acq[0] * blocks + b)),
-                pl.BlockSpec((lines, LANES), lambda b, acq: (0, b)),
-            ],
-            out_specs=pl.BlockSpec((1,) + shape, lambda b, acq: (b, 0, 0, 0, 0)),
-        ),
-        out_shape=jax.ShapeDtypeStruct((blocks,) + shape, jnp.float32),
-        compiler_params=pltpu.CompilerParams(vmem_limit_bytes=VMEM_LIMIT),
-        cost_estimate=pl.CostEstimate(
-            flops=64 * lines * width, bytes_accessed=24 * lines * width, transcendentals=0
-        ),
-        name="angle_phases",
-    )(acq, angle, other_angle)
-
-
-def joint_kernel(order, rounds, me_ref, same_ref, x_ref, early_ref, trig_ref, fw, bw, look_ref, out, stage):
+def joint_kernel(order, rounds, me_ref, same_ref, x_ref, early_ref, own_angle, other_angle, fw, bw, look_ref, out, stage):
     acq = me_ref[0]
     tiles = len(order)
     near = tiles // 2
@@ -361,7 +329,9 @@
                     tile = jnp.bitwise_xor(me_ref[1], s + side * near)
                     stage[part, tile, 0, :, lanes] = early_ref[k * near + s, side, part, 0]
     xr, xi = [stage[part].reshape(-1, 2 * LANES) for part in range(2)]
-    fr, fi = focus(xr, xi, lambda k: (trig_ref[0, 0, k], trig_ref[0, 1, k]), [fw, bw])
+    class_of = lambda k: pl.ds(k, AOI // 2, stride=6)
+    phases = lambda k: cos_sin(jnp.concatenate([a[class_of(k), :] for a in (own_angle, other_angle)], axis=1))
+    fr, fi = focus(xr, xi, phases, [fw, bw])
     mr, mi, pr, pi = fr[:, :LANES], fi[:, :LANES], fr[:, LANES:], fi[:, LANES:]
     look = look_ref[0]
     cross_real = looked_at(mr * pr + mi * pi, look[0])
@@ -385,10 +355,10 @@
                 out[first + place, r * per : (r + 1) * per, :] += value[t * per : (t + 1) * per]
 
 
-def joint_call(me, same, array, early, trig, tables, order):
+def joint_call(me, same, array, early, angle, other_angle, tables, order):
     dests, steps, _, blocks = array.shape[:4]
     tiles = len(order)
-    lines = 6 * trig.shape[3]
+    lines = angle.shape[0]
     rounds = same.shape[0]
     rows = rounds * (AOI // LOOK_AZ // tiles)
     wide = blocks * LANES // LOOK_RG
@@ -407,7 +377,8 @@
             in_specs=[
                 block(array),
                 block(early),
-                pl.BlockSpec((1,) + trig.shape[1:], lambda b, me, same: (b, 0, 0, 0, 0)),
+                pl.BlockSpec((lines, LANES), lambda b, me, same: (0, me[0] * blocks + b)),
+                pl.BlockSpec((lines, LANES), lambda b, me, same: (0, b)),
                 *[pl.BlockSpec(t.shape, lambda b, me, same: (0, 0, 0)) for t in tables],
                 pl.BlockSpec((1,) + look.shape[1:], lambda b, me, same: (b, 0, 0, 0)),
             ],
@@ -422,7 +393,7 @@
             transcendentals=0,
         ),
         name="azimuth_interferogram",
-    )(me, same, array, early, trig, *[jnp.asarray(t) for t in tables], jnp.asarray(look))
+    )(me, same, array, early, angle, other_angle, *[jnp.asarray(t) for t in tables], jnp.asarray(look))
 
 
 def single_kernel(tiles, x_ref, angle_ref, fw, bw, out):
@@ -529,7 +500,6 @@
     columns = angle.shape[1]
     rounds = pairs.shape[0]
     acq = lax.axis_index("acq")
-    side = acq.astype(jnp.int32).reshape(1)
     same = (lax.dynamic_index_in_dim(pairs, acq, 1, keepdims=False) == acq).astype(jnp.int32)
     theirs = lax.dynamic_slice_in_dim(angle, (1 - acq) * (columns // 2), columns // 2, 1)
     other_angle = lax.ppermute(theirs, "acq", [(0, 1), (1, 0)])
@@ -538,9 +508,9 @@
     axes = ("acq", "low", "high")
     tile = lax.axis_index("high") * low + lax.axis_index("low")
     me = jnp.stack([acq, tile]).astype(jnp.int32)
-    kept, given = range_call(echo, slant, me, 0, 1, order, 2, early=True)
+    kept, given = range_call(echo, slant, 0, 1, order, 2, early=True)
     came = lax.ppermute(given, "high", [(h, h ^ (FAR // 2)) for h in range(FAR)])
-    (sent,) = range_call(echo, slant, me, 1, steps - 1, order, 2)
+    (sent,) = range_call(echo, slant, 1, steps - 1, order, 2)
     array = by_block(turn(sent, axes))
     early = list(pair_call(kept, came))
     near = tiles // 2
@@ -548,8 +518,7 @@
         flip = s // near * tiles + s % near
         early[s] = lax.ppermute(early[s], ("acq", "high", "low"), [(i, i ^ flip) for i in range(2 * tiles)])
     early = by_block(jnp.stack(early))
-    trig = trig_call(side, angle, other_angle)
-    looked = joint_call(me, same, array, early, trig, azimuth_tables(angle.shape[0]), order)
+    looked = joint_call(me, same, array, early, angle, other_angle, azimuth_tables(angle.shape[0]), order)
     sources = [half * tiles + order.index(t) for t in range(tiles) for half in range(2)]
     result = place_call(turn(looked, axes), sources, columns // 2 // LOOK_RG, 2)
     return result.reshape(2, rounds, 1, -1, result.shape[1])
@@ -558,7 +527,7 @@
 def separate(tiles, echo, slant, angle, pairs):
     columns = angle.shape[1]
     rounds = pairs.shape[0]
-    (sent,) = range_call(echo, slant, jnp.zeros((2,), jnp.int32), 0, echo.shape[2] // SUB, list(range(tiles)), 1)
+    (sent,) = range_call(echo, slant, 0, echo.shape[2] // SUB, list(range(tiles)), 1)
     mine = single_call(by_block(turn(sent, ("high", "low"))), angle, azimuth_tables(angle.shape[0]))
     every = lax.all_gather(mine, "acq", axis=0)
     partner = lax.dynamic_index_in_dim(pairs, lax.axis_index("acq"), 1, keepdims=False)

time: 146 us -> 141 us (0.966)
  Pallas kernels: 36.6 us -> 30.2 us
  waiting for transfers between devices: 59.7 us -> 57.8 us
    pallas_call x3 -> x2, Pallas kernels: 21.2 us -> 14 us  [range_call(): pl.pallas_call(functools.partial(range_kernel, outer, early), grid=(steps...]
    ppermute x15, waiting for transfers between devices: 59.7 us -> 57.8 us  [joint(): lax.ppermute(early[s], ('acq', 'high', 'low'), [(i, i ^ flip) for i in ra...]
  transfers between devices with their start and end apart: 18 -> 18, of which waited for: 6 -> 6; matrix products, arithmetic and copies ran while one was open for 2% -> 2% of each run, Pallas kernels for 13% -> 9%
where the time goes in v2:
time: 141 us
  waiting for transfers between devices  57.8 us (41%)
  starting transfers between devices  32 us (23%)
  Pallas kernels  30.2 us (21%)
  blocking collectives  15.4 us (11%)
  local copies, waits for them, and re-layouts  3.61 us (3%)
    ppermute x15, waiting for transfers between devices, joint(): lax.ppermute(early[s], ('acq', 'high', 'low'), [(i, i ^ flip) for i in ra...  57.8 us
    ppermute x15, starting transfers between devices, joint(): lax.ppermute(early[s], ('acq', 'high', 'low'), [(i, i ^ flip) for i in ra...  22.3 us
    all_to_all x1, blocking collectives, turn(): return lax.all_to_all(array, axes, split_axis=0, concat_axis=0, tiled=True)  15.4 us
    pallas_call x2, Pallas kernels, range_call(): pl.pallas_call(functools.partial(range_kernel, outer, early), grid=(steps...  14 us
    pallas_call x1, Pallas kernels, joint_call(): pl.pallas_call(functools.partial(joint_kernel, order, rounds), grid_spec=...  12.4 us
    ppermute x1, starting transfers between devices, joint(): came = lax.ppermute(given, 'high', [(h, h ^ FAR // 2) for h in range(FAR)])  4.04 us
    all_to_all x1, starting transfers between devices, turn(): return lax.all_to_all(array, axes, split_axis=0, concat_axis=0, tiled=True)  3.94 us
  transfers between devices with their start and end apart: 18, of which 6 were waited for; matrix products, arithmetic and copies ran while one was open for 2% of the time, Pallas kernels for 9%

profile of v2, /device:TPU:0, one launch (start us, length us, event | category | flops | bytes accessed | tf_op | source)
XLA Modules:
  0.0 140.5 jit_solution(633051723556749004)
XLA Ops:
  0.0 3.8 %range_compress_0.1 = (f32[16,1,48,128]{3,2,1,0:T(8,128)}, f32[16,1,48,128]{3,2,1,0:T(8,128)}) custom-call(f32[2,6,768,128]{3,2,1,0:T(8,128)} %bitcast.30, f32[2,1,12288]{2,1,0:T(1,128)} %slant_ref.3, bf16[3,128,128]{2,1,0:T(8,128)(2,1)} %constant.45.clone.a1_ref, bf16[768,256]{1,0:T(8,128)(2,1)} %constant.46.clone.b2_ref, ...), custom_call_target="tpu_custom_call" | custom-call | flops 1056964608 | bytes 1572864 | tf_op jit(solution)/shard_map/range_compress_0/pallas_call | solution.py:192
  3.8 4.0 %collective-permute-start = (f32[16,1,48,128]{3,2,1,0:T(8,128)}, f32[16,1,48,128]{3,2,1,0:T(8,128)S(1)}, u32[]{:S(2)}, u32[]{:S(2)}) collective-permute-start(f32[16,1,48,128]{3,2,1,0:T(8,128)} %get-tuple-element.24), channel_id=1, source_target_pairs={{0,8},{4,12},{8,0},{12,4},{1,9},{5,13},{9,1},{13,5},{2,10},{6,14},... | collective-permute-start | bytes 1179656 | tf_op jit(solution)/shard_map/ppermute | solution.py:512
  7.9 10.1 %range_compress_1.1 = f32[32,5,48,128]{3,2,1,0:T(8,128)} custom-call(f32[2,6,768,128]{3,2,1,0:T(8,128)} %bitcast.31, f32[2,1,12288]{2,1,0:T(1,128)} %slant_ref.3, bf16[3,128,128]{2,1,0:T(8,128)(2,1)} %constant.45.clone.a1_ref, bf16[768,256]{1,0:T(8,128)(2,1)} %constant.46.clone.b2_ref, bf16[768,256]{1,0:T(8,128)(2,1)} %constant.47.clone.b3_ref, ...), custom_call_target="tpu_custom_call" | custom-call | flops 5284823040 | bytes 7864320 | tf_op jit(solution)/shard_map/range_compress_1/pallas_call | solution.py:192
  18.0 3.9 %all-to-all-start = ((f32[32,5,48,128]{3,2,1,0:T(8,128)}), f32[32,5,48,128]{3,2,1,0:T(8,128)}, u32[]{:S(2)}, u32[]{:S(2)}) async-start(f32[32,5,48,128]{3,2,1,0:T(8,128)} %range_compress_1.1), calls=%async_computation | async-start | bytes 7864320 | tf_op jit(solution)/shard_map/all_to_all | solution.py:490
  22.0 1.1 dynamic-slice_bitcast_fusion
  23.1 1.7 %collective-permute-start.16 = (f32[768,384]{1,0:T(8,128)}, f32[768,384]{1,0:T(8,128)}, u32[]{:S(2)}, u32[]{:S(2)}) collective-permute-start(f32[768,384]{1,0:T(8,128)} %dynamic-slice_bitcast_fusion), channel_id=1, source_target_pairs={{0,16},{16,0},{1,17},{17,1},{2,18},{18,2},{3,19},{19,3},{4,20},{20... | collective-permute-start | bytes 3538952 | tf_op jit(solution)/shard_map/ppermute | solution.py:505
  26.1 0.8 copy-done.3
  26.8 2.0 %pair_halves.1 = (f32[2,48,128]{2,1,0:T(8,128)}, f32[2,48,128]{2,1,0:T(8,128)}, f32[2,48,128]{2,1,0:T(8,128)}, f32[2,48,128]{2,1,0:T(8,128)}, f32[2,48,128]{2,1,...) custom-call(f32[16,1,48,128]{3,2,1,0:T(8,128)} %get-tuple-element.23, ...), custom_call_target="tpu_custom_call" | custom-call | flops 999999995904 | bytes 393216 | tf_op jit(solution)/shard_map/pair_halves/pallas_call | solution.py:221
  28.9 0.8 constant_dynamic-update-slice_fusion.15
  29.7 1.5 %collective-permute-start.2 = (f32[2,48,128]{2,1,0:T(8,128)}, f32[2,48,128]{2,1,0:T(8,128)S(1)}, u32[]{:S(2)}, u32[]{:S(2)}) collective-permute-start(f32[2,48,128]{2,1,0:T(8,128)} %get-tuple-element.27), channel_id=1, source_target_pairs={{0,2},{1,3},{2,0},{3,1},{4,6},{5,7},{6,4},{7,5},{8,10},{9,11},{10,... | collective-permute-start | bytes 147464 | tf_op jit(solution)/shard_map/ppermute | solution.py:519
  31.5 1.5 %collective-permute-start.4 = (f32[2,48,128]{2,1,0:T(8,128)}, f32[2,48,128]{2,1,0:T(8,128)S(1)}, u32[]{:S(2)}, u32[]{:S(2)}) collective-permute-start(f32[2,48,128]{2,1,0:T(8,128)} %get-tuple-element.29), channel_id=1, source_target_pairs={{0,4},{1,5},{2,6},{3,7},{4,0},{5,1},{6,2},{7,3},{8,12},{9,13},{10,... | collective-permute-start | bytes 147464 | tf_op jit(solution)/shard_map/ppermute | solution.py:519
  33.2 17.7 %collective-permute-done.2 = f32[2,48,128]{2,1,0:T(8,128)S(1)} collective-permute-done((f32[2,48,128]{2,1,0:T(8,128)}, f32[2,48,128]{2,1,0:T(8,128)S(1)}, u32[]{:S(2)}, u32[]{:S(2)}) %collective-permute-start.2) | collective-permute-done | bytes 49184 | tf_op jit(solution)/shard_map/ppermute | solution.py:519
  51.0 1.5 %collective-permute-start.7 = (f32[2,48,128]{2,1,0:T(8,128)}, f32[2,48,128]{2,1,0:T(8,128)S(1)}, u32[]{:S(2)}, u32[]{:S(2)}) collective-permute-start(f32[2,48,128]{2,1,0:T(8,128)} %get-tuple-element.32), channel_id=1, source_target_pairs={{0,7},{1,6},{2,5},{3,4},{4,3},{5,2},{6,1},{7,0},{8,15},{9,14},{10,... | collective-permute-start | bytes 147464 | tf_op jit(solution)/shard_map/ppermute | solution.py:519
  52.4 35.8 %collective-permute-done.4 = f32[2,48,128]{2,1,0:T(8,128)S(1)} collective-permute-done((f32[2,48,128]{2,1,0:T(8,128)}, f32[2,48,128]{2,1,0:T(8,128)S(1)}, u32[]{:S(2)}, u32[]{:S(2)}) %collective-permute-start.4) | collective-permute-done | bytes 49184 | tf_op jit(solution)/shard_map/ppermute | solution.py:519
  88.2 1.6 %collective-permute-start.8 = (f32[2,48,128]{2,1,0:T(8,128)}, f32[2,48,128]{2,1,0:T(8,128)S(1)}, u32[]{:S(2)}, u32[]{:S(2)}) collective-permute-start(f32[2,48,128]{2,1,0:T(8,128)} %get-tuple-element.33), channel_id=1, source_target_pairs={{0,16},{1,17},{2,18},{3,19},{4,20},{5,21},{6,22},{7,23},{8,24},{9,... | collective-permute-start | bytes 147464 | tf_op jit(solution)/shard_map/ppermute | solution.py:519
  90.3 4.1 %collective-permute-start.10 = (f32[2,48,128]{2,1,0:T(8,128)}, f32[2,48,128]{2,1,0:T(8,128)S(1)}, u32[]{:S(2)}, u32[]{:S(2)}) collective-permute-start(f32[2,48,128]{2,1,0:T(8,128)} %get-tuple-element.35), channel_id=1, source_target_pairs={{0,18},{1,19},{2,16},{3,17},{4,22},{5,23},{6,20},{7,21},{8,26},{9,... | collective-permute-start | bytes 147464 | tf_op jit(solution)/shard_map/ppermute | solution.py:519
  94.5 3.9 %collective-permute-start.12 = (f32[2,48,128]{2,1,0:T(8,128)}, f32[2,48,128]{2,1,0:T(8,128)S(1)}, u32[]{:S(2)}, u32[]{:S(2)}) collective-permute-start(f32[2,48,128]{2,1,0:T(8,128)} %get-tuple-element.37), channel_id=1, source_target_pairs={{0,20},{1,21},{2,22},{3,23},{4,16},{5,17},{6,18},{7,19},{8,28},{9,... | collective-permute-start | bytes 147464 | tf_op jit(solution)/shard_map/ppermute | solution.py:519
  99.2 2.9 %collective-permute-start.14 = (f32[2,48,128]{2,1,0:T(8,128)}, f32[2,48,128]{2,1,0:T(8,128)S(1)}, u32[]{:S(2)}, u32[]{:S(2)}) collective-permute-start(f32[2,48,128]{2,1,0:T(8,128)} %get-tuple-element.39), channel_id=1, source_target_pairs={{0,22},{1,23},{2,20},{3,21},{4,18},{5,19},{6,16},{7,17},{8,30},{9,... | collective-permute-start | bytes 147464 | tf_op jit(solution)/shard_map/ppermute | solution.py:519
  102.1 4.0 %collective-permute-start.15 = (f32[2,48,128]{2,1,0:T(8,128)}, f32[2,48,128]{2,1,0:T(8,128)S(1)}, u32[]{:S(2)}, u32[]{:S(2)}) collective-permute-start(f32[2,48,128]{2,1,0:T(8,128)} %get-tuple-element.40), channel_id=1, source_target_pairs={{0,23},{1,22},{2,21},{3,20},{4,19},{5,18},{6,17},{7,16},{8,31},{9,... | collective-permute-start | bytes 147464 | tf_op jit(solution)/shard_map/ppermute | solution.py:519
  106.3 3.7 %collective-permute-done.15 = f32[2,48,128]{2,1,0:T(8,128)S(1)} collective-permute-done((f32[2,48,128]{2,1,0:T(8,128)}, f32[2,48,128]{2,1,0:T(8,128)S(1)}, u32[]{:S(2)}, u32[]{:S(2)}) %collective-permute-start.15) | collective-permute-done | bytes 49184 | tf_op jit(solution)/shard_map/ppermute | solution.py:519
  110.0 0.9 copy-done.1
  110.8 12.4 %azimuth_interferogram.1 = f32[32,16,128]{2,1,0:T(8,128)} custom-call(s32[2]{0:T(128)} %pad_add_fusion.me_ref, s32[2]{0:T(128)} %fusion.same_ref, f32[32,5,2,3,8,128]{5,4,3,2,1,0:T(8,128)} %bitcast.5.x_ref, f32[16,2,2,3,8,128]{5,4,3,2,1,0:T(8,128)} %copy-done.1, f32[768,768]{1,0:T(8,128)} %bitcast.32, f32[768,384]{1,0:T(8,128)} %collective-permute-done.16.other_angle, ...), custom_call_target="tpu_custom_call" | custom-call | flops 3623878656 | bytes 11796480 | tf_op jit(solution)/shard_map/azimuth_interferogram/pallas_call | solution.py:372
  123.2 15.4 %all_to_all.10.in_ref = f32[32,16,128]{2,1,0:T(8,128)} all-to-all(f32[32,16,128]{2,1,0:T(8,128)} %azimuth_interferogram.1), channel_id=1, replica_groups=mesh['acq'=2,'high'=4,'low'=4] {'acq','low','high'}, dimensions={0} | all-to-all | bytes 524288 | tf_op jit(solution)/shard_map/all_to_all | solution.py:490
  138.7 1.8 %place_samples.1 = f32[32,1536]{1,0:T(8,128)} custom-call(f32[32,16,128]{2,1,0:T(8,128)} %all_to_all.10.in_ref), custom_call_target="tpu_custom_call" | custom-call | tf_op jit(solution)/shard_map/place_samples/pallas_call | solution.py:479
  (45 shorter events, 3.6 us)
Async XLA Ops:
  3.8 22.3 %collective-permute-start = (f32[16,1,48,128]{3,2,1,0:T(8,128)}, f32[16,1,48,128]{3,2,1,0:T(8,128)S(1)}, u32[]{:S(2)}, u32[]{:S(2)}) collective-permute-start(f32[16,1,48,128]{3,2,1,0:T(8,128)} %get-tuple-element.24), channel_id=1, source_target_pairs={{0,8},{4,12},{8,0},{12,4},{1,9},{5,13},{9,1},{13,5},{2,10},{6,14},... | collective-permute-start | bytes 1179656 | tf_op jit(solution)/shard_map/ppermute | solution.py:512
  18.0 4.0 %copy-start = (f32[1,768,768]{2,1,0:T(8,128)S(1)}, f32[1,768,768]{2,1,0:T(8,128)}, u32[]{:S(2)}) copy-start(f32[1,768,768]{2,1,0:T(8,128)} %param.19) | copy-start | bytes 7077892
  18.0 92.0 %all-to-all-start = ((f32[32,5,48,128]{3,2,1,0:T(8,128)}), f32[32,5,48,128]{3,2,1,0:T(8,128)}, u32[]{:S(2)}, u32[]{:S(2)}) async-start(f32[32,5,48,128]{3,2,1,0:T(8,128)} %range_compress_1.1), calls=%async_computation | async-start | bytes 7864320 | tf_op jit(solution)/shard_map/all_to_all | solution.py:490
  22.0 2.8 %copy-start.2 = (s32[2,2]{1,0:T(2,128)S(1)}, s32[2,2]{1,0:T(2,128)}, u32[]{:S(2)}) copy-start(s32[2,2]{1,0:T(2,128)} %param.20) | copy-start | bytes 52
  23.1 86.9 %collective-permute-start.16 = (f32[768,384]{1,0:T(8,128)}, f32[768,384]{1,0:T(8,128)}, u32[]{:S(2)}, u32[]{:S(2)}) collective-permute-start(f32[768,384]{1,0:T(8,128)} %dynamic-slice_bitcast_fusion), channel_id=1, source_target_pairs={{0,16},{16,0},{1,17},{17,1},{2,18},{18,2},{3,19},{19,3},{4,20},{20... | collective-permute-start | bytes 3538952 | tf_op jit(solution)/shard_map/ppermute | solution.py:505
  26.1 0.8 copy-start.3
  28.8 4.2 %collective-permute-start.1 = (f32[2,48,128]{2,1,0:T(8,128)}, f32[2,48,128]{2,1,0:T(8,128)S(1)}, u32[]{:S(2)}, u32[]{:S(2)}) collective-permute-start(f32[2,48,128]{2,1,0:T(8,128)} %get-tuple-element.26), channel_id=1, source_target_pairs={{0,1},{1,0},{2,3},{3,2},{4,5},{5,4},{6,7},{7,6},{8,9},{9,8},{10,11... | collective-permute-start | bytes 147464 | tf_op jit(solution)/shard_map/ppermute | solution.py:519
  29.7 21.2 %collective-permute-start.2 = (f32[2,48,128]{2,1,0:T(8,128)}, f32[2,48,128]{2,1,0:T(8,128)S(1)}, u32[]{:S(2)}, u32[]{:S(2)}) collective-permute-start(f32[2,48,128]{2,1,0:T(8,128)} %get-tuple-element.27), channel_id=1, source_target_pairs={{0,2},{1,3},{2,0},{3,1},{4,6},{5,7},{6,4},{7,5},{8,10},{9,11},{10,... | collective-permute-start | bytes 147464 | tf_op jit(solution)/shard_map/ppermute | solution.py:519
  31.1 19.8 %collective-permute-start.3 = (f32[2,48,128]{2,1,0:T(8,128)}, f32[2,48,128]{2,1,0:T(8,128)S(1)}, u32[]{:S(2)}, u32[]{:S(2)}) collective-permute-start(f32[2,48,128]{2,1,0:T(8,128)} %get-tuple-element.28), channel_id=1, source_target_pairs={{0,3},{1,2},{2,1},{3,0},{4,7},{5,6},{6,5},{7,4},{8,11},{9,10},{10,... | collective-permute-start | bytes 147464 | tf_op jit(solution)/shard_map/ppermute | solution.py:519
  31.5 56.7 %collective-permute-start.4 = (f32[2,48,128]{2,1,0:T(8,128)}, f32[2,48,128]{2,1,0:T(8,128)S(1)}, u32[]{:S(2)}, u32[]{:S(2)}) collective-permute-start(f32[2,48,128]{2,1,0:T(8,128)} %get-tuple-element.29), channel_id=1, source_target_pairs={{0,4},{1,5},{2,6},{3,7},{4,0},{5,1},{6,2},{7,3},{8,12},{9,13},{10,... | collective-permute-start | bytes 147464 | tf_op jit(solution)/shard_map/ppermute | solution.py:519
  33.0 56.8 %collective-permute-start.5 = (f32[2,48,128]{2,1,0:T(8,128)}, f32[2,48,128]{2,1,0:T(8,128)S(1)}, u32[]{:S(2)}, u32[]{:S(2)}) collective-permute-start(f32[2,48,128]{2,1,0:T(8,128)} %get-tuple-element.30), channel_id=1, source_target_pairs={{0,5},{1,4},{2,7},{3,6},{4,1},{5,0},{6,3},{7,2},{8,13},{9,12},{10,... | collective-permute-start | bytes 147464 | tf_op jit(solution)/shard_map/ppermute | solution.py:519
  50.8 39.5 %collective-permute-start.6 = (f32[2,48,128]{2,1,0:T(8,128)}, f32[2,48,128]{2,1,0:T(8,128)S(1)}, u32[]{:S(2)}, u32[]{:S(2)}) collective-permute-start(f32[2,48,128]{2,1,0:T(8,128)} %get-tuple-element.31), channel_id=1, source_target_pairs={{0,6},{1,7},{2,4},{3,5},{4,2},{5,3},{6,0},{7,1},{8,14},{9,15},{10,... | collective-permute-start | bytes 147464 | tf_op jit(solution)/shard_map/ppermute | solution.py:519
  51.0 43.4 %collective-permute-start.7 = (f32[2,48,128]{2,1,0:T(8,128)}, f32[2,48,128]{2,1,0:T(8,128)S(1)}, u32[]{:S(2)}, u32[]{:S(2)}) collective-permute-start(f32[2,48,128]{2,1,0:T(8,128)} %get-tuple-element.32), channel_id=1, source_target_pairs={{0,7},{1,6},{2,5},{3,4},{4,3},{5,2},{6,1},{7,0},{8,15},{9,14},{10,... | collective-permute-start | bytes 147464 | tf_op jit(solution)/shard_map/ppermute | solution.py:519
  88.2 6.3 %collective-permute-start.8 = (f32[2,48,128]{2,1,0:T(8,128)}, f32[2,48,128]{2,1,0:T(8,128)S(1)}, u32[]{:S(2)}, u32[]{:S(2)}) collective-permute-start(f32[2,48,128]{2,1,0:T(8,128)} %get-tuple-element.33), channel_id=1, source_target_pairs={{0,16},{1,17},{2,18},{3,19},{4,20},{5,21},{6,22},{7,23},{8,24},{9,... | collective-permute-start | bytes 147464 | tf_op jit(solution)/shard_map/ppermute | solution.py:519
  89.8 8.6 %collective-permute-start.9 = (f32[2,48,128]{2,1,0:T(8,128)}, f32[2,48,128]{2,1,0:T(8,128)S(1)}, u32[]{:S(2)}, u32[]{:S(2)}) collective-permute-start(f32[2,48,128]{2,1,0:T(8,128)} %get-tuple-element.34), channel_id=1, source_target_pairs={{0,17},{1,16},{2,19},{3,18},{4,21},{5,20},{6,23},{7,22},{8,25},{9,... | collective-permute-start | bytes 147464 | tf_op jit(solution)/shard_map/ppermute | solution.py:519
  90.3 8.8 %collective-permute-start.10 = (f32[2,48,128]{2,1,0:T(8,128)}, f32[2,48,128]{2,1,0:T(8,128)S(1)}, u32[]{:S(2)}, u32[]{:S(2)}) collective-permute-start(f32[2,48,128]{2,1,0:T(8,128)} %get-tuple-element.35), channel_id=1, source_target_pairs={{0,18},{1,19},{2,16},{3,17},{4,22},{5,23},{6,20},{7,21},{8,26},{9,... | collective-permute-start | bytes 147464 | tf_op jit(solution)/shard_map/ppermute | solution.py:519
  94.4 7.6 %collective-permute-start.11 = (f32[2,48,128]{2,1,0:T(8,128)}, f32[2,48,128]{2,1,0:T(8,128)S(1)}, u32[]{:S(2)}, u32[]{:S(2)}) collective-permute-start(f32[2,48,128]{2,1,0:T(8,128)} %get-tuple-element.36), channel_id=1, source_target_pairs={{0,19},{1,18},{2,17},{3,16},{4,23},{5,22},{6,21},{7,20},{8,27},{9,... | collective-permute-start | bytes 147464 | tf_op jit(solution)/shard_map/ppermute | solution.py:519
  94.5 11.5 %collective-permute-start.12 = (f32[2,48,128]{2,1,0:T(8,128)}, f32[2,48,128]{2,1,0:T(8,128)S(1)}, u32[]{:S(2)}, u32[]{:S(2)}) collective-permute-start(f32[2,48,128]{2,1,0:T(8,128)} %get-tuple-element.37), channel_id=1, source_target_pairs={{0,20},{1,21},{2,22},{3,23},{4,16},{5,17},{6,18},{7,19},{8,28},{9,... | collective-permute-start | bytes 147464 | tf_op jit(solution)/shard_map/ppermute | solution.py:519
  98.4 7.7 %collective-permute-start.13 = (f32[2,48,128]{2,1,0:T(8,128)}, f32[2,48,128]{2,1,0:T(8,128)S(1)}, u32[]{:S(2)}, u32[]{:S(2)}) collective-permute-start(f32[2,48,128]{2,1,0:T(8,128)} %get-tuple-element.38), channel_id=1, source_target_pairs={{0,21},{1,20},{2,23},{3,22},{4,17},{5,16},{6,19},{7,18},{8,29},{9,... | collective-permute-start | bytes 147464 | tf_op jit(solution)/shard_map/ppermute | solution.py:519
  99.2 7.1 %collective-permute-start.14 = (f32[2,48,128]{2,1,0:T(8,128)}, f32[2,48,128]{2,1,0:T(8,128)S(1)}, u32[]{:S(2)}, u32[]{:S(2)}) collective-permute-start(f32[2,48,128]{2,1,0:T(8,128)} %get-tuple-element.39), channel_id=1, source_target_pairs={{0,22},{1,23},{2,20},{3,21},{4,18},{5,19},{6,16},{7,17},{8,30},{9,... | collective-permute-start | bytes 147464 | tf_op jit(solution)/shard_map/ppermute | solution.py:519
  102.1 7.9 %collective-permute-start.15 = (f32[2,48,128]{2,1,0:T(8,128)}, f32[2,48,128]{2,1,0:T(8,128)S(1)}, u32[]{:S(2)}, u32[]{:S(2)}) collective-permute-start(f32[2,48,128]{2,1,0:T(8,128)} %get-tuple-element.40), channel_id=1, source_target_pairs={{0,23},{1,22},{2,21},{3,20},{4,19},{5,18},{6,17},{7,16},{8,31},{9,... | collective-permute-start | bytes 147464 | tf_op jit(solution)/shard_map/ppermute | solution.py:519
  110.0 0.9 copy-start.1

commit v3 on v2

--- a/solution.py
+++ b/solution.py
@@ -16,6 +16,7 @@
 LANES = 128
 SUB = 8
 FAR = 4
+CLASSES = 12
 BATCH = 4
 VMEM_LIMIT = 56 * 1024 * 1024
 
@@ -81,9 +82,9 @@
         c, s = trig(np.outer(3 * inside + p0, inside), outer)
         rows = [
             cc * part + (t * per_tile + half * blocks) // 3 + b
+            for cc in range(2)
             for half in range(halves)
             for t in order
-            for cc in range(2)
             for b in range(blocks // 3)
         ]
         a4.append(stacked(np.block([[c, -s], [s, c]])[np.array(rows)] / length))
@@ -111,7 +112,7 @@
                 rows_ref[c, k2 : k2 + 1, :outer] = slant_ref[c, :, k2 * outer : (k2 + 1) * outer]
             h_ref[c] = rows_ref[c].T[:outer]
 
-    rows = outs[0].shape[2]
+    rows = outs[0].shape[1] * outs[0].shape[3]
     turned = held[0] if early else outs[0].reshape(outs[0].shape[0] * rows, LANES)
     ct, st = t_ref[0], t_ref[1]
     hr, hi = h_ref[0], h_ref[1]
@@ -158,9 +159,10 @@
         yield
         for p0 in range(3):
             for b, l in enumerate(lines):
-                turned[pl.ds(p0 * SUB + l, 2 * part, stride=3 * SUB), :] = y[p0][
-                    :, b * LANES : (b + 1) * LANES
-                ]
+                for c in range(2):
+                    turned[pl.ds((2 * p0 + c) * SUB + l, part, stride=6 * SUB), :] = y[p0][
+                        c * part : (c + 1) * part, b * LANES : (b + 1) * LANES
+                    ]
         yield
 
     batches = [batch(first) for first in range(0, SUB, BATCH)]
@@ -176,7 +178,8 @@
         for s in range(2 * near):
             tile = jnp.bitwise_xor(place, s % near + k * near)
             dest = jnp.bitwise_xor(acq, s // near) * 2 * near + spot(tile, 2 * near // FAR)
-            out[s, 0] = turned[pl.ds(pl.multiple_of(dest * rows, SUB), rows), :]
+            value = turned[pl.ds(pl.multiple_of(dest * rows, SUB), rows), :]
+            out[s, :, 0] = value.reshape(out.shape[1], out.shape[3], LANES)
 
 
 def range_call(echo, slant, first, steps, order, halves, early=False):
@@ -185,7 +188,8 @@
     view = echo.reshape(2, -1, SUB, outer, LANES).transpose(0, 1, 3, 2, 4).reshape(2, -1, outer * SUB, LANES)
     tables = [slant, *range_tables(length, order, halves)]
     dests = len(order) * halves
-    rows = 2 * outer // dests * SUB
+    blocks = outer // dests
+    rows = 2 * blocks * SUB
     whole = lambda shape: pl.BlockSpec(shape, lambda s: (0,) * len(shape))
     macs = steps * SUB * length * 2 * (2 * outer + 2 * LANES) * 2 * 3
     outs = 1 + early
@@ -194,13 +198,13 @@
         grid=(steps,),
         in_specs=[pl.BlockSpec((2, 1, outer * SUB, LANES), lambda s: (0, first + s, 0, 0))]
         + [whole(t.shape) for t in tables],
-        out_specs=[pl.BlockSpec((dests // outs, 1, rows, LANES), lambda s: (0, s, 0, 0))] * outs,
+        out_specs=[pl.BlockSpec((dests // outs, blocks, 1, 2 * SUB, LANES), lambda s: (0, 0, s, 0, 0))] * outs,
         scratch_shapes=[
             pltpu.VMEM((2, LANES, LANES), jnp.float32),
             pltpu.VMEM((2, outer, LANES), jnp.float32),
         ]
         + [pltpu.VMEM((dests * rows, LANES), jnp.float32)] * early,
-        out_shape=[jax.ShapeDtypeStruct((dests // outs, steps, rows, LANES), jnp.float32)] * outs,
+        out_shape=[jax.ShapeDtypeStruct((dests // outs, blocks, steps, 2 * SUB, LANES), jnp.float32)] * outs,
         compiler_params=pltpu.CompilerParams(vmem_limit_bytes=VMEM_LIMIT),
         cost_estimate=pl.CostEstimate(
             flops=2 * macs, bytes_accessed=16 * steps * SUB * length, transcendentals=0
@@ -211,18 +215,18 @@
 
 def pair_kernel(kept_ref, came_ref, *outs):
     for s, out in enumerate(outs):
-        out[0] = kept_ref[s, 0]
-        out[1] = came_ref[s, 0]
+        out[0] = kept_ref[s, :, 0]
+        out[1] = came_ref[s, :, 0]
 
 
 def pair_call(kept, came):
-    count, _, rows, _ = kept.shape
+    count, blocks, _, rows, _ = kept.shape
     vmem = pl.BlockSpec(memory_space=pltpu.VMEM)
     return pl.pallas_call(
         pair_kernel,
         in_specs=[vmem] * 2,
         out_specs=[vmem] * count,
-        out_shape=[jax.ShapeDtypeStruct((2, rows, LANES), jnp.float32)] * count,
+        out_shape=[jax.ShapeDtypeStruct((2, blocks, rows, LANES), jnp.float32)] * count,
         compiler_params=pltpu.CompilerParams(vmem_limit_bytes=VMEM_LIMIT),
         cost_estimate=pl.CostEstimate(flops=10**12, bytes_accessed=4 * kept.size, transcendentals=0),
         name="pair_halves",
@@ -230,18 +234,18 @@
 
 
 def azimuth_tables(length):
-    part = length // 6
+    part = length // CLASSES
     f1 = np.arange(part)
-    forward, backward = [], []
+    ahead, back = [], []
     first = (length - AOI) // 2
     u, s = np.arange(part // LOOK_AZ), np.arange(LOOK_AZ)
     lines = (first + u[None, :] * LOOK_AZ + s[:, None]).reshape(-1)
-    for f0 in range(6):
-        c, s = trig(np.outer(6 * f1 + f0, np.arange(part)), length)
-        forward.append(np.block([[c, s], [-s, c]]))
-        c, s = trig(np.outer(lines, 6 * f1 + f0), length)
-        backward.append(np.block([[c, -s], [s, c]]) / length)
-    return [np.concatenate(high_low(np.stack(t)), axis=1) for t in (forward, backward)]
+    for f0 in range(CLASSES):
+        c, s = trig(np.outer(CLASSES * f1 + f0, np.arange(part)), length)
+        ahead.append(stacked(np.block([[c, s], [-s, c]])))
+        c, s = trig(np.outer(lines, CLASSES * f1 + f0), length)
+        back.append(stacked(np.block([[c, -s], [s, c]]) / length))
+    return [np.stack(ahead), np.stack(back)]
 
 
 def cos_sin(angle):
@@ -258,58 +262,49 @@
     return 1.0 - 2.0 * (s * s), 2.0 * (s * c)
 
 
-def three_pass(table, value):
-    high, low = split(value)
-    both = dot(table, high)
-    rows = table.shape[0] // 2
-    return (both[:rows] + both[rows:]) + dot(table[:rows], low)
-
-
-def focus(xr, xi, cos_sin_of, tables):
+def fours(a, b, c, d):
+    (ar, ai), (br, bi), (cr, ci), (dr, di) = a, b, c, d
+    pr, pi, mr, mi = ar + cr, ai + ci, ar - cr, ai - ci
+    qr, qi, nr, ni = br + dr, bi + di, br - dr, bi - di
+    return (pr + qr, pi + qi), (mr + ni, mi - nr), (pr - qr, pi - qi), (mr - ni, mi + nr)
+
+
+def class_of(e, g):
+    return (4 * e + 9 * g) % CLASSES
+
+
+def focus(xr, xi, phases, tables):
     fw, bw = tables
-    part, width = xr.shape[0] // 6, xr.shape[1]
-    x = [(xr[k * part : (k + 1) * part], xi[k * part : (k + 1) * part]) for k in range(6)]
-    classes = [None] * 6
-    sums = thirds(*[(x[k][0] + x[k + 3][0], x[k][1] + x[k + 3][1]) for k in range(3)], -1.0)
-    signs = [(x[k][0] - x[k + 3][0], x[k][1] - x[k + 3][1]) for k in range(3)]
-    signs[1] = (x[4][0] - x[1][0], x[4][1] - x[1][1])
-    diffs = thirds(*signs, -1.0)
+    part = xr.shape[0] // CLASSES
+    x = [(xr[k * part : (k + 1) * part], xi[k * part : (k + 1) * part]) for k in range(CLASSES)]
+    columns = [thirds(*[x[(4 * i + 3 * j) % CLASSES] for i in range(3)], -1.0) for j in range(4)]
+    classes = [None] * CLASSES
     for e in range(3):
-        classes[2 * e] = sums[e]
-        classes[(2 * e + 3) % 6] = diffs[e]
+        for g, pair in enumerate(fours(*[columns[j][e] for j in range(4)])):
+            classes[class_of(e, g)] = pair
     z, forward = [], []
-    for f0 in range(7):
-        if f0 < 6:
-            forward.append(three_pass(fw[f0], jnp.concatenate(classes[f0], axis=0)))
+    for f0 in range(CLASSES + 1):
+        if f0 < CLASSES:
+            forward.append(dot_stacked(fw[f0], jnp.concatenate(classes[f0], axis=0)))
         if f0 > 0:
             y, k = forward[f0 - 1], f0 - 1
             dr, di = y[:part], y[part:]
-            pc, ps = cos_sin_of(k)
+            pc, ps = phases(k)
             e = jnp.concatenate([dr * pc - di * ps, dr * ps + di * pc], axis=0)
-            z.append(three_pass(bw[k], e))
-    half = math.sqrt(3.0) / 2.0
-    first = (z[0] + z[3]) + (z[1] + z[4]) + (z[2] + z[5])
-    a, b, c = z[0] - z[3], z[1] - z[4], z[2] - z[5]
-    real = a + 0.5 * (b - c)
-    turned = (b + c) * half
-    fr = jnp.concatenate([first[:part], real[:part] - turned[part:]], axis=0)
-    fi = jnp.concatenate([first[part:], real[part:] + turned[:part]], axis=0)
-    return fr, fi
-
-
-def lines_of(refs, first, order, part):
-    tiles = len(order)
-    at = [x[pl.ds(first, tiles), :, part, 0] for x in refs]
-    value = at[0] if len(at) == 1 else jnp.concatenate(at, axis=1)
-    if order != list(range(tiles)):
-        value = jnp.stack([value[order.index(t)] for t in range(tiles)])
-    return value.reshape(-1, LANES)
+            y = dot_stacked(bw[k], e)
+            z.append((y[:part], y[part:]))
+    sums = [fours(*[z[class_of(e, g)] for g in range(4)]) for e in range(3)]
+    outs = []
+    for h in range(AOI // part):
+        terms = [sums[e][h] for e in range(3)]
+        outs.append(thirds(*terms, 1.0)[h % 3])
+    return [jnp.concatenate([pair[c] for pair in outs], axis=0) for c in range(2)]
 
 
 def looked_at(field, look):
-    half = AOI // 2
-    quarter = half // LOOK_AZ
-    added = [field[h * half : h * half + quarter] + field[h * half + quarter : (h + 1) * half] for h in range(2)]
+    lines = AOI // 4 // LOOK_AZ
+    groups = [field[k * lines : (k + 1) * lines] for k in range(AOI // lines)]
+    added = [groups[k] + groups[k + 1] for k in range(0, len(groups), LOOK_AZ)]
     high, low = split(jnp.concatenate(added, axis=0))
     return dot(high, look) + dot(low, look)
 
@@ -323,14 +318,14 @@
         for k, first in enumerate(firsts):
             lanes = slice(k * LANES, (k + 1) * LANES)
             for place, t in enumerate(order):
-                stage[part, t, 1:, :, lanes] = x_ref[first + place, :, part, 0]
+                stage[part, t, 1:, :, lanes] = x_ref[first + place, 0, :, part * SUB : (part + 1) * SUB, :]
             for s in range(near):
                 for side in range(2):
                     tile = jnp.bitwise_xor(me_ref[1], s + side * near)
-                    stage[part, tile, 0, :, lanes] = early_ref[k * near + s, side, part, 0]
+                    stage[part, tile, 0, :, lanes] = early_ref[k * near + s, side, 0, part * SUB : (part + 1) * SUB, :]
     xr, xi = [stage[part].reshape(-1, 2 * LANES) for part in range(2)]
-    class_of = lambda k: pl.ds(k, AOI // 2, stride=6)
-    phases = lambda k: cos_sin(jnp.concatenate([a[class_of(k), :] for a in (own_angle, other_angle)], axis=1))
+    rows_of = lambda k: pl.ds(k, own_angle.shape[0] // CLASSES, stride=CLASSES)
+    phases = lambda k: cos_sin(jnp.concatenate([a[rows_of(k), :] for a in (own_angle, other_angle)], axis=1))
     fr, fi = focus(xr, xi, phases, [fw, bw])
     mr, mi, pr, pi = fr[:, :LANES], fi[:, :LANES], fr[:, LANES:], fi[:, LANES:]
     look = look_ref[0]
@@ -356,7 +351,7 @@
 
 
 def joint_call(me, same, array, early, angle, other_angle, tables, order):
-    dests, steps, _, blocks = array.shape[:4]
+    dests, blocks, steps = array.shape[:3]
     tiles = len(order)
     lines = angle.shape[0]
     rounds = same.shape[0]
@@ -368,15 +363,14 @@
             for b in range(blocks)
         ]
     )
-    block = lambda a: pl.BlockSpec(a.shape[:3] + (1, SUB, LANES), lambda b, me, same: (0, 0, 0, b, 0, 0))
     return pl.pallas_call(
         functools.partial(joint_kernel, order, rounds),
         grid_spec=pltpu.PrefetchScalarGridSpec(
             num_scalar_prefetch=2,
             grid=(blocks,),
             in_specs=[
-                block(array),
-                block(early),
+                pl.BlockSpec((dests, 1) + array.shape[2:], lambda b, me, same: (0, b, 0, 0, 0)),
+                pl.BlockSpec(early.shape[:2] + (1,) + early.shape[3:], lambda b, me, same: (0, 0, b, 0, 0)),
                 pl.BlockSpec((lines, LANES), lambda b, me, same: (0, me[0] * blocks + b)),
                 pl.BlockSpec((lines, LANES), lambda b, me, same: (0, b)),
                 *[pl.BlockSpec(t.shape, lambda b, me, same: (0, 0, 0)) for t in tables],
@@ -397,8 +391,8 @@
 
 
 def single_kernel(tiles, x_ref, angle_ref, fw, bw, out):
-    xr, xi = [lines_of([x_ref], 0, list(range(tiles)), part) for part in range(2)]
-    fr, fi = focus(xr, xi, lambda k: cos_sin(angle_ref[pl.ds(k, AOI // 2, stride=6), :]), [fw, bw])
+    xr, xi = [x_ref[:, 0, :, part * SUB : (part + 1) * SUB, :].reshape(-1, LANES) for part in range(2)]
+    fr, fi = focus(xr, xi, lambda k: cos_sin(angle_ref[pl.ds(k, angle_ref.shape[0] // CLASSES, stride=CLASSES), :]), [fw, bw])
     out[:AOI] = fr
     out[AOI:] = fi
 
@@ -410,7 +404,7 @@
         functools.partial(single_kernel, tiles),
         grid=(columns // LANES,),
         in_specs=[
-            pl.BlockSpec((tiles, array.shape[1], 2, 1, SUB, LANES), lambda b: (0, 0, 0, b, 0, 0)),
+            pl.BlockSpec((tiles, 1) + array.shape[2:], lambda b: (0, b, 0, 0, 0)),
             pl.BlockSpec((lines, LANES), lambda b: (0, b)),
         ]
         + [pl.BlockSpec(t.shape, lambda b: (0, 0, 0)) for t in tables],
@@ -490,11 +484,6 @@
     return lax.all_to_all(array, axes, split_axis=0, concat_axis=0, tiled=True)
 
 
-def by_block(array):
-    dests, steps, rows, _ = array.shape
-    return array.reshape(dests, steps, 2, rows // (2 * SUB), SUB, LANES)
-
-
 def joint(tiles, echo, slant, angle, pairs):
     steps = echo.shape[2] // SUB
     columns = angle.shape[1]
@@ -511,13 +500,13 @@
     kept, given = range_call(echo, slant, 0, 1, order, 2, early=True)
     came = lax.ppermute(given, "high", [(h, h ^ (FAR // 2)) for h in range(FAR)])
     (sent,) = range_call(echo, slant, 1, steps - 1, order, 2)
-    array = by_block(turn(sent, axes))
+    array = turn(sent, axes)
     early = list(pair_call(kept, came))
     near = tiles // 2
     for s in range(1, tiles):
         flip = s // near * tiles + s % near
         early[s] = lax.ppermute(early[s], ("acq", "high", "low"), [(i, i ^ flip) for i in range(2 * tiles)])
-    early = by_block(jnp.stack(early))
+    early = jnp.stack(early)
     looked = joint_call(me, same, array, early, angle, other_angle, azimuth_tables(angle.shape[0]), order)
     sources = [half * tiles + order.index(t) for t in range(tiles) for half in range(2)]
     result = place_call(turn(looked, axes), sources, columns // 2 // LOOK_RG, 2)
@@ -528,7 +517,7 @@
     columns = angle.shape[1]
     rounds = pairs.shape[0]
     (sent,) = range_call(echo, slant, 0, echo.shape[2] // SUB, list(range(tiles)), 1)
-    mine = single_call(by_block(turn(sent, ("high", "low"))), angle, azimuth_tables(angle.shape[0]))
+    mine = single_call(turn(sent, ("high", "low")), angle, azimuth_tables(angle.shape[0]))
     every = lax.all_gather(mine, "acq", axis=0)
     partner = lax.dynamic_index_in_dim(pairs, lax.axis_index("acq"), 1, keepdims=False)
     partners = [lax.dynamic_index_in_dim(every, partner[r], 0, keepdims=False) for r in range(rounds)]

time: 141 us -> 141 us (level)
  no operation moved by 1% of the time
where the time goes in v3:
time: 141 us; the launch traced here: 140 us
  waiting for transfers between devices  58 us (41%)
  starting transfers between devices  31.8 us (23%)
  Pallas kernels  30 us (21%)
  blocking collectives  15.4 us (11%)
  local copies, waits for them, and re-layouts  3.61 us (3%)
    ppermute x15, waiting for transfers between devices, joint(): lax.ppermute(early[s], ('acq', 'high', 'low'), [(i, i ^ flip) for i in ra...  57.9 us
    ppermute x15, starting transfers between devices, joint(): lax.ppermute(early[s], ('acq', 'high', 'low'), [(i, i ^ flip) for i in ra...  22.1 us
    all_to_all x1, blocking collectives, turn(): return lax.all_to_all(array, axes, split_axis=0, concat_axis=0, tiled=True)  15.4 us
    pallas_call x2, Pallas kernels, range_call(): pl.pallas_call(functools.partial(range_kernel, outer, early), grid=(steps...  14.2 us
    pallas_call x1, Pallas kernels, joint_call(): pl.pallas_call(functools.partial(joint_kernel, order, rounds), grid_spec=...  12 us
    ppermute x1, starting transfers between devices, joint(): came = lax.ppermute(given, 'high', [(h, h ^ FAR // 2) for h in range(FAR)])  4.04 us
    all_to_all x1, starting transfers between devices, turn(): return lax.all_to_all(array, axes, split_axis=0, concat_axis=0, tiled=True)  3.94 us
  transfers between devices with their start and end apart: 18, of which 6 were waited for; matrix products, arithmetic and copies ran while one was open for 2% of the time, Pallas kernels for 9%

profile of v3, /device:TPU:0, one launch (start us, length us, event | category | flops | bytes accessed | tf_op | source)
XLA Modules:
  0.0 140.2 jit_solution(6312908784708930528)
XLA Ops:
  0.0 3.9 %range_compress_0.1 = (f32[16,3,1,16,128]{4,3,2,1,0:T(8,128)}, f32[16,3,1,16,128]{4,3,2,1,0:T(8,128)}) custom-call(f32[2,6,768,128]{3,2,1,0:T(8,128)} %bitcast.45, f32[2,1,12288]{2,1,0:T(1,128)} %slant_ref.3, bf16[3,128,128]{2,1,0:T(8,128)(2,1)} %constant.45.clone.a1_ref, bf16[768,256]{1,0:T(8,128)(2,1)} %constant.46.clone.b2_ref, ...), custom_call_target="tpu_custom_call" | custom-call | flops 1056964608 | bytes 1572864 | tf_op jit(solution)/shard_map/range_compress_0/pallas_call | solution.py:196
  3.9 4.0 %collective-permute-start = (f32[16,3,1,16,128]{4,3,2,1,0:T(8,128)}, f32[16,3,1,16,128]{4,3,2,1,0:T(8,128)S(1)}, u32[]{:S(2)}, u32[]{:S(2)}) collective-permute-start(f32[16,3,1,16,128]{4,3,2,1,0:T(8,128)} %get-tuple-element.24), channel_id=1, source_target_pairs={{0,8},{4,12},{8,0},{12,4},{1,9},{5,13},{9,1},{13,5},{2,10},{6,14},... | collective-permute-start | bytes 1179656 | tf_op jit(solution)/shard_map/ppermute | solution.py:501
  7.9 10.3 %range_compress_1.1 = f32[32,3,5,16,128]{4,3,2,1,0:T(8,128)} custom-call(f32[2,6,768,128]{3,2,1,0:T(8,128)} %bitcast.46, f32[2,1,12288]{2,1,0:T(1,128)} %slant_ref.3, bf16[3,128,128]{2,1,0:T(8,128)(2,1)} %constant.45.clone.a1_ref, bf16[768,256]{1,0:T(8,128)(2,1)} %constant.46.clone.b2_ref, bf16[768,256]{1,0:T(8,128)(2,1)} %constant.47.clone.b3_ref, ...), custom_call_target="tpu_custom_call" | custom-call | flops 5284823040 | bytes 7864320 | tf_op jit(solution)/shard_map/range_compress_1/pallas_call | solution.py:196
  18.2 3.9 %all-to-all-start = ((f32[32,3,5,16,128]{4,3,2,1,0:T(8,128)}), f32[32,3,5,16,128]{4,3,2,1,0:T(8,128)}, u32[]{:S(2)}, u32[]{:S(2)}) async-start(f32[32,3,5,16,128]{4,3,2,1,0:T(8,128)} %range_compress_1.1), calls=%async_computation | async-start | bytes 7864320 | tf_op jit(solution)/shard_map/all_to_all | solution.py:484
  22.2 1.1 dynamic-slice_bitcast_fusion
  23.3 1.7 %collective-permute-start.16 = (f32[768,384]{1,0:T(8,128)}, f32[768,384]{1,0:T(8,128)}, u32[]{:S(2)}, u32[]{:S(2)}) collective-permute-start(f32[768,384]{1,0:T(8,128)} %dynamic-slice_bitcast_fusion), channel_id=1, source_target_pairs={{0,16},{16,0},{1,17},{17,1},{2,18},{18,2},{3,19},{19,3},{4,20},{20... | collective-permute-start | bytes 3538952 | tf_op jit(solution)/shard_map/ppermute | solution.py:494
  26.3 0.8 copy-done.3
  27.1 2.0 %pair_halves.1 = (f32[2,3,16,128]{3,2,1,0:T(8,128)}, f32[2,3,16,128]{3,2,1,0:T(8,128)}, f32[2,3,16,128]{3,2,1,0:T(8,128)}, f32[2,3,16,128]{3,2,1,0:T(8,128)}, f3...) custom-call(f32[16,3,1,16,128]{4,3,2,1,0:T(8,128)} %get-tuple-elemen, ...), custom_call_target="tpu_custom_call" | custom-call | flops 999999995904 | bytes 393216 | tf_op jit(solution)/shard_map/pair_halves/pallas_call | solution.py:225
  29.1 0.8 bitcast_dynamic-update-slice_fusion.15
  29.9 1.5 %collective-permute-start.2 = (f32[2,3,16,128]{3,2,1,0:T(8,128)}, f32[2,3,16,128]{3,2,1,0:T(8,128)S(1)}, u32[]{:S(2)}, u32[]{:S(2)}) collective-permute-start(f32[2,3,16,128]{3,2,1,0:T(8,128)} %get-tuple-element.27), channel_id=1, source_target_pairs={{0,2},{1,3},{2,0},{3,1},{4,6},{5,7},{6,4},{7,5},{8,10},{9,11},{10,... | collective-permute-start | bytes 147464 | tf_op jit(solution)/shard_map/ppermute | solution.py:508
  31.8 1.5 %collective-permute-start.4 = (f32[2,3,16,128]{3,2,1,0:T(8,128)}, f32[2,3,16,128]{3,2,1,0:T(8,128)S(1)}, u32[]{:S(2)}, u32[]{:S(2)}) collective-permute-start(f32[2,3,16,128]{3,2,1,0:T(8,128)} %get-tuple-element.29), channel_id=1, source_target_pairs={{0,4},{1,5},{2,6},{3,7},{4,0},{5,1},{6,2},{7,3},{8,12},{9,13},{10,... | collective-permute-start | bytes 147464 | tf_op jit(solution)/shard_map/ppermute | solution.py:508
  33.4 18.1 %collective-permute-done.2 = f32[2,3,16,128]{3,2,1,0:T(8,128)S(1)} collective-permute-done((f32[2,3,16,128]{3,2,1,0:T(8,128)}, f32[2,3,16,128]{3,2,1,0:T(8,128)S(1)}, u32[]{:S(2)}, u32[]{:S(2)}) %collective-permute-start.2) | collective-permute-done | bytes 49184 | tf_op jit(solution)/shard_map/ppermute | solution.py:508
  51.7 1.2 collective-permute-start.7
  53.0 35.5 %collective-permute-done.4 = f32[2,3,16,128]{3,2,1,0:T(8,128)S(1)} collective-permute-done((f32[2,3,16,128]{3,2,1,0:T(8,128)}, f32[2,3,16,128]{3,2,1,0:T(8,128)S(1)}, u32[]{:S(2)}, u32[]{:S(2)}) %collective-permute-start.4) | collective-permute-done | bytes 49184 | tf_op jit(solution)/shard_map/ppermute | solution.py:508
  88.5 1.5 %collective-permute-start.8 = (f32[2,3,16,128]{3,2,1,0:T(8,128)}, f32[2,3,16,128]{3,2,1,0:T(8,128)S(1)}, u32[]{:S(2)}, u32[]{:S(2)}) collective-permute-start(f32[2,3,16,128]{3,2,1,0:T(8,128)} %get-tuple-element.33), channel_id=1, source_target_pairs={{0,16},{1,17},{2,18},{3,19},{4,20},{5,21},{6,22},{7,23},{8,24},{9,... | collective-permute-start | bytes 147464 | tf_op jit(solution)/shard_map/ppermute | solution.py:508
  90.6 4.0 %collective-permute-start.10 = (f32[2,3,16,128]{3,2,1,0:T(8,128)}, f32[2,3,16,128]{3,2,1,0:T(8,128)S(1)}, u32[]{:S(2)}, u32[]{:S(2)}) collective-permute-start(f32[2,3,16,128]{3,2,1,0:T(8,128)} %get-tuple-element.35), channel_id=1, source_target_pairs={{0,18},{1,19},{2,16},{3,17},{4,22},{5,23},{6,20},{7,21},{8,26},{9,... | collective-permute-start | bytes 147464 | tf_op jit(solution)/shard_map/ppermute | solution.py:508
  94.7 3.9 %collective-permute-start.12 = (f32[2,3,16,128]{3,2,1,0:T(8,128)}, f32[2,3,16,128]{3,2,1,0:T(8,128)S(1)}, u32[]{:S(2)}, u32[]{:S(2)}) collective-permute-start(f32[2,3,16,128]{3,2,1,0:T(8,128)} %get-tuple-element.37), channel_id=1, source_target_pairs={{0,20},{1,21},{2,22},{3,23},{4,16},{5,17},{6,18},{7,19},{8,28},{9,... | collective-permute-start | bytes 147464 | tf_op jit(solution)/shard_map/ppermute | solution.py:508
  99.4 4.8 %collective-permute-start.14 = (f32[2,3,16,128]{3,2,1,0:T(8,128)}, f32[2,3,16,128]{3,2,1,0:T(8,128)S(1)}, u32[]{:S(2)}, u32[]{:S(2)}) collective-permute-start(f32[2,3,16,128]{3,2,1,0:T(8,128)} %get-tuple-element.39), channel_id=1, source_target_pairs={{0,22},{1,23},{2,20},{3,21},{4,18},{5,19},{6,16},{7,17},{8,30},{9,... | collective-permute-start | bytes 147464 | tf_op jit(solution)/shard_map/ppermute | solution.py:508
  104.1 2.3 %collective-permute-start.15 = (f32[2,3,16,128]{3,2,1,0:T(8,128)}, f32[2,3,16,128]{3,2,1,0:T(8,128)S(1)}, u32[]{:S(2)}, u32[]{:S(2)}) collective-permute-start(f32[2,3,16,128]{3,2,1,0:T(8,128)} %get-tuple-element.40), channel_id=1, source_target_pairs={{0,23},{1,22},{2,21},{3,20},{4,19},{5,18},{6,17},{7,16},{8,31},{9,... | collective-permute-start | bytes 147464 | tf_op jit(solution)/shard_map/ppermute | solution.py:508
  106.7 3.4 %collective-permute-done.15 = f32[2,3,16,128]{3,2,1,0:T(8,128)S(1)} collective-permute-done((f32[2,3,16,128]{3,2,1,0:T(8,128)}, f32[2,3,16,128]{3,2,1,0:T(8,128)S(1)}, u32[]{:S(2)}, u32[]{:S(2)}) %collective-permute-start.15) | collective-permute-done | bytes 49184 | tf_op jit(solution)/shard_map/ppermute | solution.py:508
  110.1 0.9 copy-done.1
  111.0 12.0 %azimuth_interferogram.1 = f32[32,16,128]{2,1,0:T(8,128)} custom-call(s32[2]{0:T(128)} %pad_add_fusion.me_ref, s32[2]{0:T(128)} %fusion.same_ref, f32[32,3,5,16,128]{4,3,2,1,0:T(8,128)} %all-to-all-done.x_ref, f32[16,2,3,16,128]{4,3,2,1,0:T(8,128)} %copy-done.1, f32[768,768]{1,0:T(8,128)} %bitcast.47, f32[768,384]{1,0:T(8,128)} %collective-permute-done.16.other_angle, ...), custom_call_target="tpu_custom_call" | custom-call | flops 3623878656 | bytes 11796480 | tf_op jit(solution)/shard_map/azimuth_interferogram/pallas_call | solution.py:366
  123.0 15.4 %all_to_all.10.in_ref = f32[32,16,128]{2,1,0:T(8,128)} all-to-all(f32[32,16,128]{2,1,0:T(8,128)} %azimuth_interferogram.1), channel_id=1, replica_groups=mesh['acq'=2,'high'=4,'low'=4] {'acq','low','high'}, dimensions={0} | all-to-all | bytes 524288 | tf_op jit(solution)/shard_map/all_to_all | solution.py:484
  138.3 1.8 %place_samples.1 = f32[32,1536]{1,0:T(8,128)} custom-call(f32[32,16,128]{2,1,0:T(8,128)} %all_to_all.10.in_ref), custom_call_target="tpu_custom_call" | custom-call | tf_op jit(solution)/shard_map/place_samples/pallas_call | solution.py:473
  (45 shorter events, 3.7 us)
Async XLA Ops:
  3.9 22.5 %collective-permute-start = (f32[16,3,1,16,128]{4,3,2,1,0:T(8,128)}, f32[16,3,1,16,128]{4,3,2,1,0:T(8,128)S(1)}, u32[]{:S(2)}, u32[]{:S(2)}) collective-permute-start(f32[16,3,1,16,128]{4,3,2,1,0:T(8,128)} %get-tuple-element.24), channel_id=1, source_target_pairs={{0,8},{4,12},{8,0},{12,4},{1,9},{5,13},{9,1},{13,5},{2,10},{6,14},... | collective-permute-start | bytes 1179656 | tf_op jit(solution)/shard_map/ppermute | solution.py:501
  18.2 4.0 %copy-start = (f32[1,768,768]{2,1,0:T(8,128)S(1)}, f32[1,768,768]{2,1,0:T(8,128)}, u32[]{:S(2)}) copy-start(f32[1,768,768]{2,1,0:T(8,128)} %param.19) | copy-start | bytes 7077892
  18.2 91.9 %all-to-all-start = ((f32[32,3,5,16,128]{4,3,2,1,0:T(8,128)}), f32[32,3,5,16,128]{4,3,2,1,0:T(8,128)}, u32[]{:S(2)}, u32[]{:S(2)}) async-start(f32[32,3,5,16,128]{4,3,2,1,0:T(8,128)} %range_compress_1.1), calls=%async_computation | async-start | bytes 7864320 | tf_op jit(solution)/shard_map/all_to_all | solution.py:484
  22.2 2.8 %copy-start.2 = (s32[2,2]{1,0:T(2,128)S(1)}, s32[2,2]{1,0:T(2,128)}, u32[]{:S(2)}) copy-start(s32[2,2]{1,0:T(2,128)} %param.20) | copy-start | bytes 52
  23.3 86.8 %collective-permute-start.16 = (f32[768,384]{1,0:T(8,128)}, f32[768,384]{1,0:T(8,128)}, u32[]{:S(2)}, u32[]{:S(2)}) collective-permute-start(f32[768,384]{1,0:T(8,128)} %dynamic-slice_bitcast_fusion), channel_id=1, source_target_pairs={{0,16},{16,0},{1,17},{17,1},{2,18},{18,2},{3,19},{19,3},{4,20},{20... | collective-permute-start | bytes 3538952 | tf_op jit(solution)/shard_map/ppermute | solution.py:494
  26.3 0.8 copy-start.3
  29.1 4.2 %collective-permute-start.1 = (f32[2,3,16,128]{3,2,1,0:T(8,128)}, f32[2,3,16,128]{3,2,1,0:T(8,128)S(1)}, u32[]{:S(2)}, u32[]{:S(2)}) collective-permute-start(f32[2,3,16,128]{3,2,1,0:T(8,128)} %get-tuple-element.26), channel_id=1, source_target_pairs={{0,1},{1,0},{2,3},{3,2},{4,5},{5,4},{6,7},{7,6},{8,9},{9,8},{10,11... | collective-permute-start | bytes 147464 | tf_op jit(solution)/shard_map/ppermute | solution.py:508
  29.9 21.7 %collective-permute-start.2 = (f32[2,3,16,128]{3,2,1,0:T(8,128)}, f32[2,3,16,128]{3,2,1,0:T(8,128)S(1)}, u32[]{:S(2)}, u32[]{:S(2)}) collective-permute-start(f32[2,3,16,128]{3,2,1,0:T(8,128)} %get-tuple-element.27), channel_id=1, source_target_pairs={{0,2},{1,3},{2,0},{3,1},{4,6},{5,7},{6,4},{7,5},{8,10},{9,11},{10,... | collective-permute-start | bytes 147464 | tf_op jit(solution)/shard_map/ppermute | solution.py:508
  31.4 20.4 %collective-permute-start.3 = (f32[2,3,16,128]{3,2,1,0:T(8,128)}, f32[2,3,16,128]{3,2,1,0:T(8,128)S(1)}, u32[]{:S(2)}, u32[]{:S(2)}) collective-permute-start(f32[2,3,16,128]{3,2,1,0:T(8,128)} %get-tuple-element.28), channel_id=1, source_target_pairs={{0,3},{1,2},{2,1},{3,0},{4,7},{5,6},{6,5},{7,4},{8,11},{9,10},{10,... | collective-permute-start | bytes 147464 | tf_op jit(solution)/shard_map/ppermute | solution.py:508
  31.8 56.7 %collective-permute-start.4 = (f32[2,3,16,128]{3,2,1,0:T(8,128)}, f32[2,3,16,128]{3,2,1,0:T(8,128)S(1)}, u32[]{:S(2)}, u32[]{:S(2)}) collective-permute-start(f32[2,3,16,128]{3,2,1,0:T(8,128)} %get-tuple-element.29), channel_id=1, source_target_pairs={{0,4},{1,5},{2,6},{3,7},{4,0},{5,1},{6,2},{7,3},{8,12},{9,13},{10,... | collective-permute-start | bytes 147464 | tf_op jit(solution)/shard_map/ppermute | solution.py:508
  33.2 56.8 %collective-permute-start.5 = (f32[2,3,16,128]{3,2,1,0:T(8,128)}, f32[2,3,16,128]{3,2,1,0:T(8,128)S(1)}, u32[]{:S(2)}, u32[]{:S(2)}) collective-permute-start(f32[2,3,16,128]{3,2,1,0:T(8,128)} %get-tuple-element.30), channel_id=1, source_target_pairs={{0,5},{1,4},{2,7},{3,6},{4,1},{5,0},{6,3},{7,2},{8,13},{9,12},{10,... | collective-permute-start | bytes 147464 | tf_op jit(solution)/shard_map/ppermute | solution.py:508
  51.6 39.0 %collective-permute-start.6 = (f32[2,3,16,128]{3,2,1,0:T(8,128)}, f32[2,3,16,128]{3,2,1,0:T(8,128)S(1)}, u32[]{:S(2)}, u32[]{:S(2)}) collective-permute-start(f32[2,3,16,128]{3,2,1,0:T(8,128)} %get-tuple-element.31), channel_id=1, source_target_pairs={{0,6},{1,7},{2,4},{3,5},{4,2},{5,3},{6,0},{7,1},{8,14},{9,15},{10,... | collective-permute-start | bytes 147464 | tf_op jit(solution)/shard_map/ppermute | solution.py:508
  51.7 42.9 %collective-permute-start.7 = (f32[2,3,16,128]{3,2,1,0:T(8,128)}, f32[2,3,16,128]{3,2,1,0:T(8,128)S(1)}, u32[]{:S(2)}, u32[]{:S(2)}) collective-permute-start(f32[2,3,16,128]{3,2,1,0:T(8,128)} %get-tuple-element.32), channel_id=1, source_target_pairs={{0,7},{1,6},{2,5},{3,4},{4,3},{5,2},{6,1},{7,0},{8,15},{9,14},{10,... | collective-permute-start | bytes 147464 | tf_op jit(solution)/shard_map/ppermute | solution.py:508
  88.5 6.2 %collective-permute-start.8 = (f32[2,3,16,128]{3,2,1,0:T(8,128)}, f32[2,3,16,128]{3,2,1,0:T(8,128)S(1)}, u32[]{:S(2)}, u32[]{:S(2)}) collective-permute-start(f32[2,3,16,128]{3,2,1,0:T(8,128)} %get-tuple-element.33), channel_id=1, source_target_pairs={{0,16},{1,17},{2,18},{3,19},{4,20},{5,21},{6,22},{7,23},{8,24},{9,... | collective-permute-start | bytes 147464 | tf_op jit(solution)/shard_map/ppermute | solution.py:508
  90.1 8.6 %collective-permute-start.9 = (f32[2,3,16,128]{3,2,1,0:T(8,128)}, f32[2,3,16,128]{3,2,1,0:T(8,128)S(1)}, u32[]{:S(2)}, u32[]{:S(2)}) collective-permute-start(f32[2,3,16,128]{3,2,1,0:T(8,128)} %get-tuple-element.34), channel_id=1, source_target_pairs={{0,17},{1,16},{2,19},{3,18},{4,21},{5,20},{6,23},{7,22},{8,25},{9,... | collective-permute-start | bytes 147464 | tf_op jit(solution)/shard_map/ppermute | solution.py:508
  90.6 8.7 %collective-permute-start.10 = (f32[2,3,16,128]{3,2,1,0:T(8,128)}, f32[2,3,16,128]{3,2,1,0:T(8,128)S(1)}, u32[]{:S(2)}, u32[]{:S(2)}) collective-permute-start(f32[2,3,16,128]{3,2,1,0:T(8,128)} %get-tuple-element.35), channel_id=1, source_target_pairs={{0,18},{1,19},{2,16},{3,17},{4,22},{5,23},{6,20},{7,21},{8,26},{9,... | collective-permute-start | bytes 147464 | tf_op jit(solution)/shard_map/ppermute | solution.py:508
  94.6 9.5 %collective-permute-start.11 = (f32[2,3,16,128]{3,2,1,0:T(8,128)}, f32[2,3,16,128]{3,2,1,0:T(8,128)S(1)}, u32[]{:S(2)}, u32[]{:S(2)}) collective-permute-start(f32[2,3,16,128]{3,2,1,0:T(8,128)} %get-tuple-element.36), channel_id=1, source_target_pairs={{0,19},{1,18},{2,17},{3,16},{4,23},{5,22},{6,21},{7,20},{8,27},{9,... | collective-permute-start | bytes 147464 | tf_op jit(solution)/shard_map/ppermute | solution.py:508
  94.7 11.7 %collective-permute-start.12 = (f32[2,3,16,128]{3,2,1,0:T(8,128)}, f32[2,3,16,128]{3,2,1,0:T(8,128)S(1)}, u32[]{:S(2)}, u32[]{:S(2)}) collective-permute-start(f32[2,3,16,128]{3,2,1,0:T(8,128)} %get-tuple-element.37), channel_id=1, source_target_pairs={{0,20},{1,21},{2,22},{3,23},{4,16},{5,17},{6,18},{7,19},{8,28},{9,... | collective-permute-start | bytes 147464 | tf_op jit(solution)/shard_map/ppermute | solution.py:508
  98.6 7.8 %collective-permute-start.13 = (f32[2,3,16,128]{3,2,1,0:T(8,128)}, f32[2,3,16,128]{3,2,1,0:T(8,128)S(1)}, u32[]{:S(2)}, u32[]{:S(2)}) collective-permute-start(f32[2,3,16,128]{3,2,1,0:T(8,128)} %get-tuple-element.38), channel_id=1, source_target_pairs={{0,21},{1,20},{2,23},{3,22},{4,17},{5,16},{6,19},{7,18},{8,29},{9,... | collective-permute-start | bytes 147464 | tf_op jit(solution)/shard_map/ppermute | solution.py:508
  99.4 7.3 %collective-permute-start.14 = (f32[2,3,16,128]{3,2,1,0:T(8,128)}, f32[2,3,16,128]{3,2,1,0:T(8,128)S(1)}, u32[]{:S(2)}, u32[]{:S(2)}) collective-permute-start(f32[2,3,16,128]{3,2,1,0:T(8,128)} %get-tuple-element.39), channel_id=1, source_target_pairs={{0,22},{1,23},{2,20},{3,21},{4,18},{5,19},{6,16},{7,17},{8,30},{9,... | collective-permute-start | bytes 147464 | tf_op jit(solution)/shard_map/ppermute | solution.py:508
  104.1 6.0 %collective-permute-start.15 = (f32[2,3,16,128]{3,2,1,0:T(8,128)}, f32[2,3,16,128]{3,2,1,0:T(8,128)S(1)}, u32[]{:S(2)}, u32[]{:S(2)}) collective-permute-start(f32[2,3,16,128]{3,2,1,0:T(8,128)} %get-tuple-element.40), channel_id=1, source_target_pairs={{0,23},{1,22},{2,21},{3,20},{4,19},{5,18},{6,17},{7,16},{8,31},{9,... | collective-permute-start | bytes 147464 | tf_op jit(solution)/shard_map/ppermute | solution.py:508
  110.1 0.9 copy-start.1

commit v4 on v3

--- a/solution.py
+++ b/solution.py
@@ -16,6 +16,8 @@
 LANES = 128
 SUB = 8
 FAR = 4
+SPARE = 32
+USED = LANES - SPARE
 CLASSES = 12
 BATCH = 4
 VMEM_LIMIT = 56 * 1024 * 1024
@@ -46,6 +48,13 @@
     both = dot(table, jnp.concatenate([high, low], axis=0))
     rows = table.shape[0] // 2
     return both[:rows] + both[rows:]
+
+
+def dot_parts(table, value):
+    rows = table.shape[0] // 2
+    high, low = table[:rows], table[rows:]
+    left = [jnp.concatenate(pair, axis=1) for pair in ((high, high), (low, jnp.zeros_like(low)))]
+    return dot_stacked(jnp.concatenate(left, axis=0), value)
 
 
 def thirds(a, b, c, sign):
@@ -57,8 +66,13 @@
 
 
 def dot_table_right(value, table):
+    rows = table.shape[0] // 2
+    high_table, low_table = table[:rows], table[rows:]
     high, low = split(value)
-    return dot(jnp.concatenate([high, low, high], axis=1), table)
+    return dot(
+        jnp.concatenate([high, low, high], axis=1),
+        jnp.concatenate([high_table, high_table, low_table], axis=0),
+    )
 
 
 def stacked(table):
@@ -90,18 +104,17 @@
         a4.append(stacked(np.block([[c, -s], [s, c]])[np.array(rows)] / length))
     c2, s2 = trig(np.outer(q, q), inner)
     b2 = np.block([[c2, -s2], [s2, c2]])
-    b3 = np.block([[c2, s2], [-s2, c2]])
     ct, st = trig(np.outer(k1, q), length)
     twiddle = np.stack([ct, st]).astype(np.float32)
-    b2, b3 = [np.concatenate(high_low(t)[[0, 0, 1]]) for t in (b2, b3)]
-    return np.stack(a1), b2, b3, np.stack(a4), twiddle
+    b2 = np.concatenate(high_low(b2))
+    return np.stack(a1), b2, np.stack(a4), twiddle
 
 
 def spot(tile, low):
     return lax.rem(tile, low) * FAR + lax.div(tile, low)
 
 
-def range_kernel(outer, early, x_ref, slant_ref, a1_ref, b2_ref, b3_ref, a4_ref, t_ref, *rest):
+def range_kernel(outer, early, x_ref, slant_ref, a1_ref, b2_ref, a4_ref, t_ref, *rest):
     outs, (rows_ref, h_ref), held = rest[: 1 + early], rest[1 + early : 3 + early], rest[3 + early :]
     part = outer // 3
 
@@ -143,14 +156,14 @@
         for b in range(BATCH):
             yr = y[b * outer : (b + 1) * outer, :LANES]
             yi = y[b * outer : (b + 1) * outer, LANES:]
-            z.append(jnp.concatenate([yr * hr - yi * hi, yr * hi + yi * hr], axis=1))
-        y = dot_table_right(jnp.concatenate(z, axis=0), b3_ref[...])
+            z.append(jnp.concatenate([yr * hr - yi * hi, -yr * hi - yi * hr], axis=1))
+        y = dot_table_right(jnp.concatenate(z, axis=0), b2_ref[...])
         yield
         z = []
         for b in range(BATCH):
             yr = y[b * outer : (b + 1) * outer, :LANES]
             yi = y[b * outer : (b + 1) * outer, LANES:]
-            zr, zi = yr * ct - yi * st, yi * ct + yr * st
+            zr, zi = yr * ct + yi * st, yr * st - yi * ct
             z.append(thirds(*[(zr[k * part : (k + 1) * part], zi[k * part : (k + 1) * part]) for k in range(3)], 1.0))
         y = []
         for p0 in range(3):
@@ -242,9 +255,9 @@
     lines = (first + u[None, :] * LOOK_AZ + s[:, None]).reshape(-1)
     for f0 in range(CLASSES):
         c, s = trig(np.outer(CLASSES * f1 + f0, np.arange(part)), length)
-        ahead.append(stacked(np.block([[c, s], [-s, c]])))
+        ahead.append(np.concatenate(high_low(np.block([[c, s], [-s, c]]))))
         c, s = trig(np.outer(lines, CLASSES * f1 + f0), length)
-        back.append(stacked(np.block([[c, -s], [s, c]]) / length))
+        back.append(np.concatenate(high_low(np.block([[c, -s], [s, c]]) / length)))
     return [np.stack(ahead), np.stack(back)]
 
 
@@ -285,13 +298,13 @@
     z, forward = [], []
     for f0 in range(CLASSES + 1):
         if f0 < CLASSES:
-            forward.append(dot_stacked(fw[f0], jnp.concatenate(classes[f0], axis=0)))
+            forward.append(dot_parts(fw[f0], jnp.concatenate(classes[f0], axis=0)))
         if f0 > 0:
             y, k = forward[f0 - 1], f0 - 1
             dr, di = y[:part], y[part:]
             pc, ps = phases(k)
             e = jnp.concatenate([dr * pc - di * ps, dr * ps + di * pc], axis=0)
-            y = dot_stacked(bw[k], e)
+            y = dot_parts(bw[k], e)
             z.append((y[:part], y[part:]))
     sums = [fours(*[z[class_of(e, g)] for g in range(4)]) for e in range(3)]
     outs = []
@@ -309,7 +322,7 @@
     return dot(high, look) + dot(low, look)
 
 
-def joint_kernel(order, rounds, me_ref, same_ref, x_ref, early_ref, own_angle, other_angle, fw, bw, look_ref, out, stage):
+def joint_kernel(order, rounds, me_ref, same_ref, x_ref, early_ref, own_angle, other_angle, fw, bw, look_ref, out, stage, looked):
     acq = me_ref[0]
     tiles = len(order)
     near = tiles // 2
@@ -335,19 +348,43 @@
     own_imag = looked_at(mi * mr - mr * mi, look[1])
     other_real = looked_at(pr * pr + pi * pi, look[0])
     other_imag = looked_at(pi * pr - pr * pi, look[1])
-    per = AOI // LOOK_AZ // tiles
-
-    @pl.when(pl.program_id(0) == 0)
+    block = pl.program_id(0)
+
+    @pl.when(block == 0)
     def _():
-        out[...] = jnp.zeros_like(out)
+        looked[...] = jnp.zeros_like(looked)
 
     for r in range(rounds):
         same = same_ref[r] != 0
-        own = jnp.where(same, own_real + own_imag, cross_real + cross_imag)
-        other = jnp.where(same, other_real + other_imag, cross_real - cross_imag)
-        for first, value in zip(firsts, (own, other)):
+        looked[0, r] += jnp.where(same, own_real + own_imag, cross_real + cross_imag)
+        looked[1, r] += jnp.where(same, other_real + other_imag, cross_real - cross_imag)
+
+    @pl.when(block == pl.num_programs(0) - 1)
+    def _():
+        for k, first in enumerate(firsts):
+            groups = pack(looked[k, 0], looked[k, 1])
             for place, t in enumerate(order):
-                out[first + place, r * per : (r + 1) * per, :] += value[t * per : (t + 1) * per]
+                for j, (value, at) in enumerate(groups):
+                    out[first + place, j] = value[t * SUB + at : t * SUB + at + SUB // 2]
+
+
+def pack(even, odd):
+    half = SUB // 2
+    free = lax.broadcasted_iota(jnp.int32, even.shape, 1) >= USED
+    rest = [pltpu.roll(odd, (USED - SPARE * j) % LANES, 1) for j in range(3)]
+    up = lambda value: pltpu.roll(value, value.shape[0] - half, 0)
+    return (
+        (jnp.where(free, up(rest[0]), even), 0),
+        (jnp.where(free, rest[1], even), half),
+        (jnp.where(free, up(rest[2]), odd), 0),
+    )
+
+
+def unpack(parts):
+    lane = lax.broadcasted_iota(jnp.int32, parts[0].shape, 1)
+    rest = [pltpu.roll(part, (SPARE * j - USED) % LANES, 1) for j, part in enumerate(parts)]
+    last = jnp.where(lane < SPARE, rest[0], jnp.where(lane < 2 * SPARE, rest[1], rest[2]))
+    return jnp.concatenate([parts[0], parts[1], parts[2], last], axis=0)
 
 
 def joint_call(me, same, array, early, angle, other_angle, tables, order):
@@ -355,7 +392,6 @@
     tiles = len(order)
     lines = angle.shape[0]
     rounds = same.shape[0]
-    rows = rounds * (AOI // LOOK_AZ // tiles)
     wide = blocks * LANES // LOOK_RG
     look = np.stack(
         [
@@ -376,10 +412,13 @@
                 *[pl.BlockSpec(t.shape, lambda b, me, same: (0, 0, 0)) for t in tables],
                 pl.BlockSpec((1,) + look.shape[1:], lambda b, me, same: (b, 0, 0, 0)),
             ],
-            out_specs=pl.BlockSpec((dests, rows, LANES), lambda b, me, same: (0, 0, 0)),
-            scratch_shapes=[pltpu.VMEM((2, tiles, steps + 1, SUB, 2 * LANES), jnp.float32)],
+            out_specs=pl.BlockSpec((dests, 3, SUB // 2, LANES), lambda b, me, same: (0, 0, 0, 0)),
+            scratch_shapes=[
+                pltpu.VMEM((2, tiles, steps + 1, SUB, 2 * LANES), jnp.float32),
+                pltpu.VMEM((2, rounds, AOI // LOOK_AZ, LANES), jnp.float32),
+            ],
         ),
-        out_shape=jax.ShapeDtypeStruct((dests, rows, LANES), jnp.float32),
+        out_shape=jax.ShapeDtypeStruct((dests, 3, SUB // 2, LANES), jnp.float32),
         compiler_params=pltpu.CompilerParams(vmem_limit_bytes=VMEM_LIMIT),
         cost_estimate=pl.CostEstimate(
             flops=2 * 2 * 3 * 6 * 256 * 256 * 2 * LANES * blocks,
@@ -451,7 +490,11 @@
 
 
 def place_kernel(sources, valid, parts, in_ref, out):
-    rows = in_ref.shape[1]
+    if in_ref.shape[1:] == (3, SUB // 2, LANES):
+        values = {k: unpack([in_ref[k, j] for j in range(3)]) for k in sources}
+    else:
+        values = {k: in_ref[k] for k in sources}
+    rows = values[sources[0]].shape[0]
     lane = lax.broadcasted_iota(jnp.int32, (rows, LANES), 1)
     for c in range(parts):
         for o in range(len(sources) * valid // LANES):
@@ -460,7 +503,7 @@
                 shift = place * valid - o * LANES
                 if shift + valid <= 0 or shift >= LANES:
                     continue
-                value = in_ref[source]
+                value = values[source]
                 turn_by = (shift - c * valid) % LANES
                 if turn_by:
                     value = pltpu.roll(value, turn_by, 1)
@@ -468,8 +511,7 @@
             out[c * rows : (c + 1) * rows, o * LANES : (o + 1) * LANES] = acc
 
 
-def place_call(received, sources, valid, parts):
-    _, rows, _ = received.shape
+def place_call(received, rows, sources, valid, parts):
     return pl.pallas_call(
         functools.partial(place_kernel, sources, valid, parts),
         in_specs=[pl.BlockSpec(memory_space=pltpu.VMEM)],
@@ -509,7 +551,7 @@
     early = jnp.stack(early)
     looked = joint_call(me, same, array, early, angle, other_angle, azimuth_tables(angle.shape[0]), order)
     sources = [half * tiles + order.index(t) for t in range(tiles) for half in range(2)]
-    result = place_call(turn(looked, axes), sources, columns // 2 // LOOK_RG, 2)
+    result = place_call(turn(looked, axes), rounds * SUB, sources, columns // 2 // LOOK_RG, 2)
     return result.reshape(2, rounds, 1, -1, result.shape[1])
 
 
@@ -522,12 +564,13 @@
     partner = lax.dynamic_index_in_dim(pairs, lax.axis_index("acq"), 1, keepdims=False)
     partners = [lax.dynamic_index_in_dim(every, partner[r], 0, keepdims=False) for r in range(rounds)]
     looked = turn(cross_call(mine, partners, tiles), ("high", "low"))
-    result = place_call(looked, list(range(tiles)), columns // LOOK_RG, 1)
+    result = place_call(looked, looked.shape[1], list(range(tiles)), columns // LOOK_RG, 1)
     return result.reshape(2, rounds, 1, -1, result.shape[1])
 
 
 def shards(tiles, acqs, echo, slant, angle, pairs):
-    fits = echo.shape[2] > SUB and tiles == FAR * FAR and angle.shape[2] % (6 * LANES) == 0 and AOI // LOOK_AZ % (tiles * SUB) == 0
+    fits = echo.shape[2] > SUB and tiles == FAR * FAR and AOI // LOOK_AZ == tiles * SUB
+    fits = fits and angle.shape[2] // LOOK_RG == USED and pairs.shape[0] == 2
     program = joint if acqs == 2 and fits else separate
     return program(tiles, echo, slant, angle[0], pairs)
 

time: 141 us -> 139 us (0.986)
  no operation moved by 1% of the time
where the time goes in v4:
time: 139 us
  waiting for transfers between devices  57.9 us (42%)
  starting transfers between devices  31.9 us (23%)
  Pallas kernels  29.3 us (21%)
  blocking collectives  14.6 us (11%)
  local copies, waits for them, and re-layouts  3.61 us (3%)
    ppermute x15, waiting for transfers between devices, joint(): lax.ppermute(early[s], ('acq', 'high', 'low'), [(i, i ^ flip) for i in ra...  57.9 us
    ppermute x15, starting transfers between devices, joint(): lax.ppermute(early[s], ('acq', 'high', 'low'), [(i, i ^ flip) for i in ra...  22.2 us
    all_to_all x1, blocking collectives, turn(): return lax.all_to_all(array, axes, split_axis=0, concat_axis=0, tiled=True)  14.6 us
    pallas_call x2, Pallas kernels, range_call(): pl.pallas_call(functools.partial(range_kernel, outer, early), grid=(steps...  13.9 us
    pallas_call x1, Pallas kernels, joint_call(): pl.pallas_call(functools.partial(joint_kernel, order, rounds), grid_spec=...  11.6 us
    ppermute x1, starting transfers between devices, joint(): came = lax.ppermute(given, 'high', [(h, h ^ FAR // 2) for h in range(FAR)])  4.04 us
    all_to_all x1, starting transfers between devices, turn(): return lax.all_to_all(array, axes, split_axis=0, concat_axis=0, tiled=True)  3.94 us
  transfers between devices with their start and end apart: 18, of which 6 were waited for; matrix products, arithmetic and copies ran while one was open for 2% of the time, Pallas kernels for 9%

profile of v4, /device:TPU:0, one launch (start us, length us, event | category | flops | bytes accessed | tf_op | source)
XLA Modules:
  0.0 138.8 jit_solution(8009277975666038468)
XLA Ops:
  0.0 3.7 %range_compress_0.1 = (f32[16,3,1,16,128]{4,3,2,1,0:T(8,128)}, f32[16,3,1,16,128]{4,3,2,1,0:T(8,128)}) custom-call(f32[2,6,768,128]{3,2,1,0:T(8,128)} %bitcast.45, f32[2,1,12288]{2,1,0:T(1,128)} %slant_ref.3, bf16[3,128,128]{2,1,0:T(8,128)(2,1)} %constant.43.clone.a1_ref, bf16[512,256]{1,0:T(8,128)(2,1)} %constant.44.clone.b2_ref, ...), custom_call_target="tpu_custom_call" | custom-call | flops 1056964608 | bytes 1572864 | tf_op jit(solution)/shard_map/range_compress_0/pallas_call | solution.py:209
  3.7 4.0 %collective-permute-start = (f32[16,3,1,16,128]{4,3,2,1,0:T(8,128)}, f32[16,3,1,16,128]{4,3,2,1,0:T(8,128)S(1)}, u32[]{:S(2)}, u32[]{:S(2)}) collective-permute-start(f32[16,3,1,16,128]{4,3,2,1,0:T(8,128)} %get-tuple-element.24), channel_id=1, source_target_pairs={{0,8},{4,12},{8,0},{12,4},{1,9},{5,13},{9,1},{13,5},{2,10},{6,14},... | collective-permute-start | bytes 1179656 | tf_op jit(solution)/shard_map/ppermute | solution.py:543
  7.7 10.2 %range_compress_1.1 = f32[32,3,5,16,128]{4,3,2,1,0:T(8,128)} custom-call(f32[2,6,768,128]{3,2,1,0:T(8,128)} %bitcast.46, f32[2,1,12288]{2,1,0:T(1,128)} %slant_ref.3, bf16[3,128,128]{2,1,0:T(8,128)(2,1)} %constant.43.clone.a1_ref, bf16[512,256]{1,0:T(8,128)(2,1)} %constant.44.clone.b2_ref, bf16[3,128,128]{2,1,0:T(8,128)(2,1)} %constant.45.clone.a4_ref, ...), custom_call_target="tpu_custom_call" | custom-call | flops 5284823040 | bytes 7864320 | tf_op jit(solution)/shard_map/range_compress_1/pallas_call | solution.py:209
  17.9 3.9 %all-to-all-start = ((f32[32,3,5,16,128]{4,3,2,1,0:T(8,128)}), f32[32,3,5,16,128]{4,3,2,1,0:T(8,128)}, u32[]{:S(2)}, u32[]{:S(2)}) async-start(f32[32,3,5,16,128]{4,3,2,1,0:T(8,128)} %range_compress_1.1), calls=%async_computation | async-start | bytes 7864320 | tf_op jit(solution)/shard_map/all_to_all | solution.py:526
  21.9 1.1 dynamic-slice_bitcast_fusion
  23.0 1.7 %collective-permute-start.16 = (f32[768,384]{1,0:T(8,128)}, f32[768,384]{1,0:T(8,128)}, u32[]{:S(2)}, u32[]{:S(2)}) collective-permute-start(f32[768,384]{1,0:T(8,128)} %dynamic-slice_bitcast_fusion), channel_id=1, source_target_pairs={{0,16},{16,0},{1,17},{17,1},{2,18},{18,2},{3,19},{19,3},{4,20},{20... | collective-permute-start | bytes 3538952 | tf_op jit(solution)/shard_map/ppermute | solution.py:536
  26.0 0.8 copy-done.3
  26.8 2.0 %pair_halves.1 = (f32[2,3,16,128]{3,2,1,0:T(8,128)}, f32[2,3,16,128]{3,2,1,0:T(8,128)}, f32[2,3,16,128]{3,2,1,0:T(8,128)}, f32[2,3,16,128]{3,2,1,0:T(8,128)}, f3...) custom-call(f32[16,3,1,16,128]{4,3,2,1,0:T(8,128)} %get-tuple-elemen, ...), custom_call_target="tpu_custom_call" | custom-call | flops 999999995904 | bytes 393216 | tf_op jit(solution)/shard_map/pair_halves/pallas_call | solution.py:238
  28.8 0.8 bitcast_dynamic-update-slice_fusion.15
  29.6 1.5 %collective-permute-start.2 = (f32[2,3,16,128]{3,2,1,0:T(8,128)}, f32[2,3,16,128]{3,2,1,0:T(8,128)S(1)}, u32[]{:S(2)}, u32[]{:S(2)}) collective-permute-start(f32[2,3,16,128]{3,2,1,0:T(8,128)} %get-tuple-element.27), channel_id=1, source_target_pairs={{0,2},{1,3},{2,0},{3,1},{4,6},{5,7},{6,4},{7,5},{8,10},{9,11},{10,... | collective-permute-start | bytes 147464 | tf_op jit(solution)/shard_map/ppermute | solution.py:550
  31.4 1.5 %collective-permute-start.4 = (f32[2,3,16,128]{3,2,1,0:T(8,128)}, f32[2,3,16,128]{3,2,1,0:T(8,128)S(1)}, u32[]{:S(2)}, u32[]{:S(2)}) collective-permute-start(f32[2,3,16,128]{3,2,1,0:T(8,128)} %get-tuple-element.29), channel_id=1, source_target_pairs={{0,4},{1,5},{2,6},{3,7},{4,0},{5,1},{6,2},{7,3},{8,12},{9,13},{10,... | collective-permute-start | bytes 147464 | tf_op jit(solution)/shard_map/ppermute | solution.py:550
  33.1 17.7 %collective-permute-done.2 = f32[2,3,16,128]{3,2,1,0:T(8,128)S(1)} collective-permute-done((f32[2,3,16,128]{3,2,1,0:T(8,128)}, f32[2,3,16,128]{3,2,1,0:T(8,128)S(1)}, u32[]{:S(2)}, u32[]{:S(2)}) %collective-permute-start.2) | collective-permute-done | bytes 49184 | tf_op jit(solution)/shard_map/ppermute | solution.py:550
  51.0 1.4 collective-permute-start.7
  52.4 35.7 %collective-permute-done.4 = f32[2,3,16,128]{3,2,1,0:T(8,128)S(1)} collective-permute-done((f32[2,3,16,128]{3,2,1,0:T(8,128)}, f32[2,3,16,128]{3,2,1,0:T(8,128)S(1)}, u32[]{:S(2)}, u32[]{:S(2)}) %collective-permute-start.4) | collective-permute-done | bytes 49184 | tf_op jit(solution)/shard_map/ppermute | solution.py:550
  88.1 1.6 %collective-permute-start.8 = (f32[2,3,16,128]{3,2,1,0:T(8,128)}, f32[2,3,16,128]{3,2,1,0:T(8,128)S(1)}, u32[]{:S(2)}, u32[]{:S(2)}) collective-permute-start(f32[2,3,16,128]{3,2,1,0:T(8,128)} %get-tuple-element.33), channel_id=1, source_target_pairs={{0,16},{1,17},{2,18},{3,19},{4,20},{5,21},{6,22},{7,23},{8,24},{9,... | collective-permute-start | bytes 147464 | tf_op jit(solution)/shard_map/ppermute | solution.py:550
  90.2 4.1 %collective-permute-start.10 = (f32[2,3,16,128]{3,2,1,0:T(8,128)}, f32[2,3,16,128]{3,2,1,0:T(8,128)S(1)}, u32[]{:S(2)}, u32[]{:S(2)}) collective-permute-start(f32[2,3,16,128]{3,2,1,0:T(8,128)} %get-tuple-element.35), channel_id=1, source_target_pairs={{0,18},{1,19},{2,16},{3,17},{4,22},{5,23},{6,20},{7,21},{8,26},{9,... | collective-permute-start | bytes 147464 | tf_op jit(solution)/shard_map/ppermute | solution.py:550
  94.5 3.8 %collective-permute-start.12 = (f32[2,3,16,128]{3,2,1,0:T(8,128)}, f32[2,3,16,128]{3,2,1,0:T(8,128)S(1)}, u32[]{:S(2)}, u32[]{:S(2)}) collective-permute-start(f32[2,3,16,128]{3,2,1,0:T(8,128)} %get-tuple-element.37), channel_id=1, source_target_pairs={{0,20},{1,21},{2,22},{3,23},{4,16},{5,17},{6,18},{7,19},{8,28},{9,... | collective-permute-start | bytes 147464 | tf_op jit(solution)/shard_map/ppermute | solution.py:550
  99.1 2.9 %collective-permute-start.14 = (f32[2,3,16,128]{3,2,1,0:T(8,128)}, f32[2,3,16,128]{3,2,1,0:T(8,128)S(1)}, u32[]{:S(2)}, u32[]{:S(2)}) collective-permute-start(f32[2,3,16,128]{3,2,1,0:T(8,128)} %get-tuple-element.39), channel_id=1, source_target_pairs={{0,22},{1,23},{2,20},{3,21},{4,18},{5,19},{6,16},{7,17},{8,30},{9,... | collective-permute-start | bytes 147464 | tf_op jit(solution)/shard_map/ppermute | solution.py:550
  101.9 4.0 %collective-permute-start.15 = (f32[2,3,16,128]{3,2,1,0:T(8,128)}, f32[2,3,16,128]{3,2,1,0:T(8,128)S(1)}, u32[]{:S(2)}, u32[]{:S(2)}) collective-permute-start(f32[2,3,16,128]{3,2,1,0:T(8,128)} %get-tuple-element.40), channel_id=1, source_target_pairs={{0,23},{1,22},{2,21},{3,20},{4,19},{5,18},{6,17},{7,16},{8,31},{9,... | collective-permute-start | bytes 147464 | tf_op jit(solution)/shard_map/ppermute | solution.py:550
  106.2 3.6 %collective-permute-done.15 = f32[2,3,16,128]{3,2,1,0:T(8,128)S(1)} collective-permute-done((f32[2,3,16,128]{3,2,1,0:T(8,128)}, f32[2,3,16,128]{3,2,1,0:T(8,128)S(1)}, u32[]{:S(2)}, u32[]{:S(2)}) %collective-permute-start.15) | collective-permute-done | bytes 49184 | tf_op jit(solution)/shard_map/ppermute | solution.py:550
  109.8 0.9 copy-done.1
  110.7 11.6 %azimuth_interferogram.1 = f32[32,3,4,128]{3,2,1,0:T(4,128)} custom-call(s32[2]{0:T(128)} %pad_add_fusion.me_ref, s32[2]{0:T(128)} %fusion.same_ref, f32[32,3,5,16,128]{4,3,2,1,0:T(8,128)} %all-to-all-done.x_ref, f32[16,2,3,16,128]{4,3,2,1,0:T(8,128)} %copy-done.1, f32[768,768]{1,0:T(8,128)} %bitcast.47, f32[768,384]{1,0:T(8,128)} %collective-permute-done.16.other_angle, ...), custom_call_target="tpu_custom_call" | custom-call | flops 3623878656 | bytes 11796480 | tf_op jit(solution)/shard_map/azimuth_interferogram/pallas_call | solution.py:402
  122.3 14.6 %all_to_all.10.in_ref = f32[32,3,4,128]{3,2,1,0:T(4,128)} all-to-all(f32[32,3,4,128]{3,2,1,0:T(4,128)} %azimuth_interferogram.1), channel_id=1, replica_groups=mesh['acq'=2,'high'=4,'low'=4] {'acq','low','high'}, dimensions={0} | all-to-all | bytes 393216 | tf_op jit(solution)/shard_map/all_to_all | solution.py:526
  136.9 1.9 %place_samples.1 = f32[32,1536]{1,0:T(8,128)} custom-call(f32[32,3,4,128]{3,2,1,0:T(4,128)} %all_to_all.10.in_ref), custom_call_target="tpu_custom_call" | custom-call | tf_op jit(solution)/shard_map/place_samples/pallas_call | solution.py:515
  (45 shorter events, 3.7 us)
Async XLA Ops:
  3.7 22.3 %collective-permute-start = (f32[16,3,1,16,128]{4,3,2,1,0:T(8,128)}, f32[16,3,1,16,128]{4,3,2,1,0:T(8,128)S(1)}, u32[]{:S(2)}, u32[]{:S(2)}) collective-permute-start(f32[16,3,1,16,128]{4,3,2,1,0:T(8,128)} %get-tuple-element.24), channel_id=1, source_target_pairs={{0,8},{4,12},{8,0},{12,4},{1,9},{5,13},{9,1},{13,5},{2,10},{6,14},... | collective-permute-start | bytes 1179656 | tf_op jit(solution)/shard_map/ppermute | solution.py:543
  17.9 4.0 %copy-start = (f32[1,768,768]{2,1,0:T(8,128)S(1)}, f32[1,768,768]{2,1,0:T(8,128)}, u32[]{:S(2)}) copy-start(f32[1,768,768]{2,1,0:T(8,128)} %param.17) | copy-start | bytes 7077892
  17.9 91.9 %all-to-all-start = ((f32[32,3,5,16,128]{4,3,2,1,0:T(8,128)}), f32[32,3,5,16,128]{4,3,2,1,0:T(8,128)}, u32[]{:S(2)}, u32[]{:S(2)}) async-start(f32[32,3,5,16,128]{4,3,2,1,0:T(8,128)} %range_compress_1.1), calls=%async_computation | async-start | bytes 7864320 | tf_op jit(solution)/shard_map/all_to_all | solution.py:526
  21.9 2.8 %copy-start.2 = (s32[2,2]{1,0:T(2,128)S(1)}, s32[2,2]{1,0:T(2,128)}, u32[]{:S(2)}) copy-start(s32[2,2]{1,0:T(2,128)} %param.18) | copy-start | bytes 52
  23.0 86.9 %collective-permute-start.16 = (f32[768,384]{1,0:T(8,128)}, f32[768,384]{1,0:T(8,128)}, u32[]{:S(2)}, u32[]{:S(2)}) collective-permute-start(f32[768,384]{1,0:T(8,128)} %dynamic-slice_bitcast_fusion), channel_id=1, source_target_pairs={{0,16},{16,0},{1,17},{17,1},{2,18},{18,2},{3,19},{19,3},{4,20},{20... | collective-permute-start | bytes 3538952 | tf_op jit(solution)/shard_map/ppermute | solution.py:536
  26.0 0.8 copy-start.3
  28.7 4.2 %collective-permute-start.1 = (f32[2,3,16,128]{3,2,1,0:T(8,128)}, f32[2,3,16,128]{3,2,1,0:T(8,128)S(1)}, u32[]{:S(2)}, u32[]{:S(2)}) collective-permute-start(f32[2,3,16,128]{3,2,1,0:T(8,128)} %get-tuple-element.26), channel_id=1, source_target_pairs={{0,1},{1,0},{2,3},{3,2},{4,5},{5,4},{6,7},{7,6},{8,9},{9,8},{10,11... | collective-permute-start | bytes 147464 | tf_op jit(solution)/shard_map/ppermute | solution.py:550
  29.6 21.2 %collective-permute-start.2 = (f32[2,3,16,128]{3,2,1,0:T(8,128)}, f32[2,3,16,128]{3,2,1,0:T(8,128)S(1)}, u32[]{:S(2)}, u32[]{:S(2)}) collective-permute-start(f32[2,3,16,128]{3,2,1,0:T(8,128)} %get-tuple-element.27), channel_id=1, source_target_pairs={{0,2},{1,3},{2,0},{3,1},{4,6},{5,7},{6,4},{7,5},{8,10},{9,11},{10,... | collective-permute-start | bytes 147464 | tf_op jit(solution)/shard_map/ppermute | solution.py:550
  31.0 20.0 %collective-permute-start.3 = (f32[2,3,16,128]{3,2,1,0:T(8,128)}, f32[2,3,16,128]{3,2,1,0:T(8,128)S(1)}, u32[]{:S(2)}, u32[]{:S(2)}) collective-permute-start(f32[2,3,16,128]{3,2,1,0:T(8,128)} %get-tuple-element.28), channel_id=1, source_target_pairs={{0,3},{1,2},{2,1},{3,0},{4,7},{5,6},{6,5},{7,4},{8,11},{9,10},{10,... | collective-permute-start | bytes 147464 | tf_op jit(solution)/shard_map/ppermute | solution.py:550
  31.4 56.7 %collective-permute-start.4 = (f32[2,3,16,128]{3,2,1,0:T(8,128)}, f32[2,3,16,128]{3,2,1,0:T(8,128)S(1)}, u32[]{:S(2)}, u32[]{:S(2)}) collective-permute-start(f32[2,3,16,128]{3,2,1,0:T(8,128)} %get-tuple-element.29), channel_id=1, source_target_pairs={{0,4},{1,5},{2,6},{3,7},{4,0},{5,1},{6,2},{7,3},{8,12},{9,13},{10,... | collective-permute-start | bytes 147464 | tf_op jit(solution)/shard_map/ppermute | solution.py:550
  32.9 56.8 %collective-permute-start.5 = (f32[2,3,16,128]{3,2,1,0:T(8,128)}, f32[2,3,16,128]{3,2,1,0:T(8,128)S(1)}, u32[]{:S(2)}, u32[]{:S(2)}) collective-permute-start(f32[2,3,16,128]{3,2,1,0:T(8,128)} %get-tuple-element.30), channel_id=1, source_target_pairs={{0,5},{1,4},{2,7},{3,6},{4,1},{5,0},{6,3},{7,2},{8,13},{9,12},{10,... | collective-permute-start | bytes 147464 | tf_op jit(solution)/shard_map/ppermute | solution.py:550
  50.8 39.4 %collective-permute-start.6 = (f32[2,3,16,128]{3,2,1,0:T(8,128)}, f32[2,3,16,128]{3,2,1,0:T(8,128)S(1)}, u32[]{:S(2)}, u32[]{:S(2)}) collective-permute-start(f32[2,3,16,128]{3,2,1,0:T(8,128)} %get-tuple-element.31), channel_id=1, source_target_pairs={{0,6},{1,7},{2,4},{3,5},{4,2},{5,3},{6,0},{7,1},{8,14},{9,15},{10,... | collective-permute-start | bytes 147464 | tf_op jit(solution)/shard_map/ppermute | solution.py:550
  51.0 43.3 %collective-permute-start.7 = (f32[2,3,16,128]{3,2,1,0:T(8,128)}, f32[2,3,16,128]{3,2,1,0:T(8,128)S(1)}, u32[]{:S(2)}, u32[]{:S(2)}) collective-permute-start(f32[2,3,16,128]{3,2,1,0:T(8,128)} %get-tuple-element.32), channel_id=1, source_target_pairs={{0,7},{1,6},{2,5},{3,4},{4,3},{5,2},{6,1},{7,0},{8,15},{9,14},{10,... | collective-permute-start | bytes 147464 | tf_op jit(solution)/shard_map/ppermute | solution.py:550
  88.1 6.3 %collective-permute-start.8 = (f32[2,3,16,128]{3,2,1,0:T(8,128)}, f32[2,3,16,128]{3,2,1,0:T(8,128)S(1)}, u32[]{:S(2)}, u32[]{:S(2)}) collective-permute-start(f32[2,3,16,128]{3,2,1,0:T(8,128)} %get-tuple-element.33), channel_id=1, source_target_pairs={{0,16},{1,17},{2,18},{3,19},{4,20},{5,21},{6,22},{7,23},{8,24},{9,... | collective-permute-start | bytes 147464 | tf_op jit(solution)/shard_map/ppermute | solution.py:550
  89.7 8.6 %collective-permute-start.9 = (f32[2,3,16,128]{3,2,1,0:T(8,128)}, f32[2,3,16,128]{3,2,1,0:T(8,128)S(1)}, u32[]{:S(2)}, u32[]{:S(2)}) collective-permute-start(f32[2,3,16,128]{3,2,1,0:T(8,128)} %get-tuple-element.34), channel_id=1, source_target_pairs={{0,17},{1,16},{2,19},{3,18},{4,21},{5,20},{6,23},{7,22},{8,25},{9,... | collective-permute-start | bytes 147464 | tf_op jit(solution)/shard_map/ppermute | solution.py:550
  90.2 8.8 %collective-permute-start.10 = (f32[2,3,16,128]{3,2,1,0:T(8,128)}, f32[2,3,16,128]{3,2,1,0:T(8,128)S(1)}, u32[]{:S(2)}, u32[]{:S(2)}) collective-permute-start(f32[2,3,16,128]{3,2,1,0:T(8,128)} %get-tuple-element.35), channel_id=1, source_target_pairs={{0,18},{1,19},{2,16},{3,17},{4,22},{5,23},{6,20},{7,21},{8,26},{9,... | collective-permute-start | bytes 147464 | tf_op jit(solution)/shard_map/ppermute | solution.py:550
  94.4 7.6 %collective-permute-start.11 = (f32[2,3,16,128]{3,2,1,0:T(8,128)}, f32[2,3,16,128]{3,2,1,0:T(8,128)S(1)}, u32[]{:S(2)}, u32[]{:S(2)}) collective-permute-start(f32[2,3,16,128]{3,2,1,0:T(8,128)} %get-tuple-element.36), channel_id=1, source_target_pairs={{0,19},{1,18},{2,17},{3,16},{4,23},{5,22},{6,21},{7,20},{8,27},{9,... | collective-permute-start | bytes 147464 | tf_op jit(solution)/shard_map/ppermute | solution.py:550
  94.5 11.5 %collective-permute-start.12 = (f32[2,3,16,128]{3,2,1,0:T(8,128)}, f32[2,3,16,128]{3,2,1,0:T(8,128)S(1)}, u32[]{:S(2)}, u32[]{:S(2)}) collective-permute-start(f32[2,3,16,128]{3,2,1,0:T(8,128)} %get-tuple-element.37), channel_id=1, source_target_pairs={{0,20},{1,21},{2,22},{3,23},{4,16},{5,17},{6,18},{7,19},{8,28},{9,... | collective-permute-start | bytes 147464 | tf_op jit(solution)/shard_map/ppermute | solution.py:550
  98.3 7.7 %collective-permute-start.13 = (f32[2,3,16,128]{3,2,1,0:T(8,128)}, f32[2,3,16,128]{3,2,1,0:T(8,128)S(1)}, u32[]{:S(2)}, u32[]{:S(2)}) collective-permute-start(f32[2,3,16,128]{3,2,1,0:T(8,128)} %get-tuple-element.38), channel_id=1, source_target_pairs={{0,21},{1,20},{2,23},{3,22},{4,17},{5,16},{6,19},{7,18},{8,29},{9,... | collective-permute-start | bytes 147464 | tf_op jit(solution)/shard_map/ppermute | solution.py:550
  99.1 7.1 %collective-permute-start.14 = (f32[2,3,16,128]{3,2,1,0:T(8,128)}, f32[2,3,16,128]{3,2,1,0:T(8,128)S(1)}, u32[]{:S(2)}, u32[]{:S(2)}) collective-permute-start(f32[2,3,16,128]{3,2,1,0:T(8,128)} %get-tuple-element.39), channel_id=1, source_target_pairs={{0,22},{1,23},{2,20},{3,21},{4,18},{5,19},{6,16},{7,17},{8,30},{9,... | collective-permute-start | bytes 147464 | tf_op jit(solution)/shard_map/ppermute | solution.py:550
  101.9 7.9 %collective-permute-start.15 = (f32[2,3,16,128]{3,2,1,0:T(8,128)}, f32[2,3,16,128]{3,2,1,0:T(8,128)S(1)}, u32[]{:S(2)}, u32[]{:S(2)}) collective-permute-start(f32[2,3,16,128]{3,2,1,0:T(8,128)} %get-tuple-element.40), channel_id=1, source_target_pairs={{0,23},{1,22},{2,21},{3,20},{4,19},{5,18},{6,17},{7,16},{8,31},{9,... | collective-permute-start | bytes 147464 | tf_op jit(solution)/shard_map/ppermute | solution.py:550
  109.8 0.9 copy-start.1

commit v5 on v4

--- a/solution.py
+++ b/solution.py
@@ -314,40 +314,51 @@
     return [jnp.concatenate([pair[c] for pair in outs], axis=0) for c in range(2)]
 
 
-def looked_at(field, look):
+def looked_at(fields, look):
     lines = AOI // 4 // LOOK_AZ
-    groups = [field[k * lines : (k + 1) * lines] for k in range(AOI // lines)]
-    added = [groups[k] + groups[k + 1] for k in range(0, len(groups), LOOK_AZ)]
+    added = []
+    for field in fields:
+        groups = [field[k * lines : (k + 1) * lines] for k in range(AOI // lines)]
+        added += [groups[k] + groups[k + 1] for k in range(0, len(groups), LOOK_AZ)]
     high, low = split(jnp.concatenate(added, axis=0))
-    return dot(high, look) + dot(low, look)
-
-
-def joint_kernel(order, rounds, me_ref, same_ref, x_ref, early_ref, own_angle, other_angle, fw, bw, look_ref, out, stage, looked):
+    looked = dot(high, look) + dot(low, look)
+    rows = AOI // LOOK_AZ
+    return [looked[k * rows : (k + 1) * rows] for k in range(len(fields))]
+
+
+def joint_kernel(order, rounds, me_ref, same_ref, x_ref, early_ref, own_angle, other_angle, fw, bw, look_ref, out, looked):
     acq = me_ref[0]
     tiles = len(order)
     near = tiles // 2
     firsts = [acq * tiles, (1 - acq) * tiles]
-    for part in range(2):
-        for k, first in enumerate(firsts):
-            lanes = slice(k * LANES, (k + 1) * LANES)
-            for place, t in enumerate(order):
-                stage[part, t, 1:, :, lanes] = x_ref[first + place, 0, :, part * SUB : (part + 1) * SUB, :]
-            for s in range(near):
-                for side in range(2):
-                    tile = jnp.bitwise_xor(me_ref[1], s + side * near)
-                    stage[part, tile, 0, :, lanes] = early_ref[k * near + s, side, 0, part * SUB : (part + 1) * SUB, :]
-    xr, xi = [stage[part].reshape(-1, 2 * LANES) for part in range(2)]
+    steps = x_ref.shape[2] + 1
+    places = [jnp.bitwise_xor(me_ref[1], t) for t in range(tiles)]
+
+    def piece(k, t, step, part):
+        rows = slice(part * SUB, (part + 1) * SUB)
+        if step:
+            return x_ref[firsts[k] + order.index(t), 0, step - 1, rows, :]
+        return early_ref[k * near + lax.rem(places[t], near), lax.div(places[t], near), 0, rows, :]
+
+    xr, xi = [
+        jnp.concatenate(
+            [
+                jnp.concatenate([piece(k, t, step, part) for t in range(tiles) for step in range(steps)], axis=0)
+                for k in range(2)
+            ],
+            axis=1,
+        )
+        for part in range(2)
+    ]
     rows_of = lambda k: pl.ds(k, own_angle.shape[0] // CLASSES, stride=CLASSES)
     phases = lambda k: cos_sin(jnp.concatenate([a[rows_of(k), :] for a in (own_angle, other_angle)], axis=1))
     fr, fi = focus(xr, xi, phases, [fw, bw])
     mr, mi, pr, pi = fr[:, :LANES], fi[:, :LANES], fr[:, LANES:], fi[:, LANES:]
     look = look_ref[0]
-    cross_real = looked_at(mr * pr + mi * pi, look[0])
-    cross_imag = looked_at(mi * pr - mr * pi, look[1])
-    own_real = looked_at(mr * mr + mi * mi, look[0])
-    own_imag = looked_at(mi * mr - mr * mi, look[1])
-    other_real = looked_at(pr * pr + pi * pi, look[0])
-    other_imag = looked_at(pi * pr - pr * pi, look[1])
+    reals = [mr * pr + mi * pi, mr * mr + mi * mi, pr * pr + pi * pi]
+    imags = [mi * pr - mr * pi, mi * mr - mr * mi, pi * pr - pr * pi]
+    cross_real, own_real, other_real = looked_at(reals, look[0])
+    cross_imag, own_imag, other_imag = looked_at(imags, look[1])
     block = pl.program_id(0)
 
     @pl.when(block == 0)
@@ -414,7 +425,6 @@
             ],
             out_specs=pl.BlockSpec((dests, 3, SUB // 2, LANES), lambda b, me, same: (0, 0, 0, 0)),
             scratch_shapes=[
-                pltpu.VMEM((2, tiles, steps + 1, SUB, 2 * LANES), jnp.float32),
                 pltpu.VMEM((2, rounds, AOI // LOOK_AZ, LANES), jnp.float32),
             ],
         ),
@@ -467,7 +477,7 @@
     for r in range(rounds):
         pr, pi = partner_refs[r][:AOI], partner_refs[r][AOI:]
         for c, field in enumerate((mr * pr + mi * pi, mi * pr - mr * pi)):
-            looked = looked_at(field, look_ref[...])
+            (looked,) = looked_at([field], look_ref[...])
             at = (c * rounds + r) * per
             for t in range(tiles):
                 out[t, at : at + per, :] = looked[t * per : (t + 1) * per]

time: 139 us -> 139 us (level)
  no operation moved by 1% of the time
where the time goes in v5:
time: 139 us
  waiting for transfers between devices  57.9 us (42%)
  starting transfers between devices  31.9 us (23%)
  Pallas kernels  29.4 us (21%)
  blocking collectives  14.6 us (11%)
  local copies, waits for them, and re-layouts  3.61 us (3%)
    ppermute x15, waiting for transfers between devices, joint(): lax.ppermute(early[s], ('acq', 'high', 'low'), [(i, i ^ flip) for i in ra...  57.9 us
    ppermute x15, starting transfers between devices, joint(): lax.ppermute(early[s], ('acq', 'high', 'low'), [(i, i ^ flip) for i in ra...  22.2 us
    all_to_all x1, blocking collectives, turn(): return lax.all_to_all(array, axes, split_axis=0, concat_axis=0, tiled=True)  14.6 us
    pallas_call x2, Pallas kernels, range_call(): pl.pallas_call(functools.partial(range_kernel, outer, early), grid=(steps...  13.9 us
    pallas_call x1, Pallas kernels, joint_call(): pl.pallas_call(functools.partial(joint_kernel, order, rounds), grid_spec=...  11.7 us
    ppermute x1, starting transfers between devices, joint(): came = lax.ppermute(given, 'high', [(h, h ^ FAR // 2) for h in range(FAR)])  4.04 us
    all_to_all x1, starting transfers between devices, turn(): return lax.all_to_all(array, axes, split_axis=0, concat_axis=0, tiled=True)  3.94 us
  transfers between devices with their start and end apart: 18, of which 6 were waited for; matrix products, arithmetic and copies ran while one was open for 2% of the time, Pallas kernels for 9%

profile of v5, /device:TPU:0, one launch (start us, length us, event | category | flops | bytes accessed | tf_op | source)
XLA Modules:
  0.0 138.9 jit_solution(9185486136269868920)
XLA Ops:
  0.0 3.7 %range_compress_0.1 = (f32[16,3,1,16,128]{4,3,2,1,0:T(8,128)}, f32[16,3,1,16,128]{4,3,2,1,0:T(8,128)}) custom-call(f32[2,6,768,128]{3,2,1,0:T(8,128)} %bitcast.45, f32[2,1,12288]{2,1,0:T(1,128)} %slant_ref.3, bf16[3,128,128]{2,1,0:T(8,128)(2,1)} %constant.43.clone.a1_ref, bf16[512,256]{1,0:T(8,128)(2,1)} %constant.44.clone.b2_ref, ...), custom_call_target="tpu_custom_call" | custom-call | flops 1056964608 | bytes 1572864 | tf_op jit(solution)/shard_map/range_compress_0/pallas_call | solution.py:209
  3.7 4.0 %collective-permute-start = (f32[16,3,1,16,128]{4,3,2,1,0:T(8,128)}, f32[16,3,1,16,128]{4,3,2,1,0:T(8,128)S(1)}, u32[]{:S(2)}, u32[]{:S(2)}) collective-permute-start(f32[16,3,1,16,128]{4,3,2,1,0:T(8,128)} %get-tuple-element.24), channel_id=1, source_target_pairs={{0,8},{4,12},{8,0},{12,4},{1,9},{5,13},{9,1},{13,5},{2,10},{6,14},... | collective-permute-start | bytes 1179656 | tf_op jit(solution)/shard_map/ppermute | solution.py:553
  7.7 10.2 %range_compress_1.1 = f32[32,3,5,16,128]{4,3,2,1,0:T(8,128)} custom-call(f32[2,6,768,128]{3,2,1,0:T(8,128)} %bitcast.46, f32[2,1,12288]{2,1,0:T(1,128)} %slant_ref.3, bf16[3,128,128]{2,1,0:T(8,128)(2,1)} %constant.43.clone.a1_ref, bf16[512,256]{1,0:T(8,128)(2,1)} %constant.44.clone.b2_ref, bf16[3,128,128]{2,1,0:T(8,128)(2,1)} %constant.45.clone.a4_ref, ...), custom_call_target="tpu_custom_call" | custom-call | flops 5284823040 | bytes 7864320 | tf_op jit(solution)/shard_map/range_compress_1/pallas_call | solution.py:209
  17.9 3.9 %all-to-all-start = ((f32[32,3,5,16,128]{4,3,2,1,0:T(8,128)}), f32[32,3,5,16,128]{4,3,2,1,0:T(8,128)}, u32[]{:S(2)}, u32[]{:S(2)}) async-start(f32[32,3,5,16,128]{4,3,2,1,0:T(8,128)} %range_compress_1.1), calls=%async_computation | async-start | bytes 7864320 | tf_op jit(solution)/shard_map/all_to_all | solution.py:536
  21.9 1.1 dynamic-slice_bitcast_fusion
  23.0 1.7 %collective-permute-start.16 = (f32[768,384]{1,0:T(8,128)}, f32[768,384]{1,0:T(8,128)}, u32[]{:S(2)}, u32[]{:S(2)}) collective-permute-start(f32[768,384]{1,0:T(8,128)} %dynamic-slice_bitcast_fusion), channel_id=1, source_target_pairs={{0,16},{16,0},{1,17},{17,1},{2,18},{18,2},{3,19},{19,3},{4,20},{20... | collective-permute-start | bytes 3538952 | tf_op jit(solution)/shard_map/ppermute | solution.py:546
  26.0 0.8 copy-done.3
  26.8 2.0 %pair_halves.1 = (f32[2,3,16,128]{3,2,1,0:T(8,128)}, f32[2,3,16,128]{3,2,1,0:T(8,128)}, f32[2,3,16,128]{3,2,1,0:T(8,128)}, f32[2,3,16,128]{3,2,1,0:T(8,128)}, f3...) custom-call(f32[16,3,1,16,128]{4,3,2,1,0:T(8,128)} %get-tuple-elemen, ...), custom_call_target="tpu_custom_call" | custom-call | flops 999999995904 | bytes 393216 | tf_op jit(solution)/shard_map/pair_halves/pallas_call | solution.py:238
  28.8 0.8 bitcast_dynamic-update-slice_fusion.15
  29.6 1.5 %collective-permute-start.2 = (f32[2,3,16,128]{3,2,1,0:T(8,128)}, f32[2,3,16,128]{3,2,1,0:T(8,128)S(1)}, u32[]{:S(2)}, u32[]{:S(2)}) collective-permute-start(f32[2,3,16,128]{3,2,1,0:T(8,128)} %get-tuple-element.27), channel_id=1, source_target_pairs={{0,2},{1,3},{2,0},{3,1},{4,6},{5,7},{6,4},{7,5},{8,10},{9,11},{10,... | collective-permute-start | bytes 147464 | tf_op jit(solution)/shard_map/ppermute | solution.py:560
  31.4 1.5 %collective-permute-start.4 = (f32[2,3,16,128]{3,2,1,0:T(8,128)}, f32[2,3,16,128]{3,2,1,0:T(8,128)S(1)}, u32[]{:S(2)}, u32[]{:S(2)}) collective-permute-start(f32[2,3,16,128]{3,2,1,0:T(8,128)} %get-tuple-element.29), channel_id=1, source_target_pairs={{0,4},{1,5},{2,6},{3,7},{4,0},{5,1},{6,2},{7,3},{8,12},{9,13},{10,... | collective-permute-start | bytes 147464 | tf_op jit(solution)/shard_map/ppermute | solution.py:560
  33.1 17.7 %collective-permute-done.2 = f32[2,3,16,128]{3,2,1,0:T(8,128)S(1)} collective-permute-done((f32[2,3,16,128]{3,2,1,0:T(8,128)}, f32[2,3,16,128]{3,2,1,0:T(8,128)S(1)}, u32[]{:S(2)}, u32[]{:S(2)}) %collective-permute-start.2) | collective-permute-done | bytes 49184 | tf_op jit(solution)/shard_map/ppermute | solution.py:560
  51.0 1.4 collective-permute-start.7
  52.4 35.7 %collective-permute-done.4 = f32[2,3,16,128]{3,2,1,0:T(8,128)S(1)} collective-permute-done((f32[2,3,16,128]{3,2,1,0:T(8,128)}, f32[2,3,16,128]{3,2,1,0:T(8,128)S(1)}, u32[]{:S(2)}, u32[]{:S(2)}) %collective-permute-start.4) | collective-permute-done | bytes 49184 | tf_op jit(solution)/shard_map/ppermute | solution.py:560
  88.1 1.6 %collective-permute-start.8 = (f32[2,3,16,128]{3,2,1,0:T(8,128)}, f32[2,3,16,128]{3,2,1,0:T(8,128)S(1)}, u32[]{:S(2)}, u32[]{:S(2)}) collective-permute-start(f32[2,3,16,128]{3,2,1,0:T(8,128)} %get-tuple-element.33), channel_id=1, source_target_pairs={{0,16},{1,17},{2,18},{3,19},{4,20},{5,21},{6,22},{7,23},{8,24},{9,... | collective-permute-start | bytes 147464 | tf_op jit(solution)/shard_map/ppermute | solution.py:560
  90.2 4.1 %collective-permute-start.10 = (f32[2,3,16,128]{3,2,1,0:T(8,128)}, f32[2,3,16,128]{3,2,1,0:T(8,128)S(1)}, u32[]{:S(2)}, u32[]{:S(2)}) collective-permute-start(f32[2,3,16,128]{3,2,1,0:T(8,128)} %get-tuple-element.35), channel_id=1, source_target_pairs={{0,18},{1,19},{2,16},{3,17},{4,22},{5,23},{6,20},{7,21},{8,26},{9,... | collective-permute-start | bytes 147464 | tf_op jit(solution)/shard_map/ppermute | solution.py:560
  94.5 3.8 %collective-permute-start.12 = (f32[2,3,16,128]{3,2,1,0:T(8,128)}, f32[2,3,16,128]{3,2,1,0:T(8,128)S(1)}, u32[]{:S(2)}, u32[]{:S(2)}) collective-permute-start(f32[2,3,16,128]{3,2,1,0:T(8,128)} %get-tuple-element.37), channel_id=1, source_target_pairs={{0,20},{1,21},{2,22},{3,23},{4,16},{5,17},{6,18},{7,19},{8,28},{9,... | collective-permute-start | bytes 147464 | tf_op jit(solution)/shard_map/ppermute | solution.py:560
  99.1 2.9 %collective-permute-start.14 = (f32[2,3,16,128]{3,2,1,0:T(8,128)}, f32[2,3,16,128]{3,2,1,0:T(8,128)S(1)}, u32[]{:S(2)}, u32[]{:S(2)}) collective-permute-start(f32[2,3,16,128]{3,2,1,0:T(8,128)} %get-tuple-element.39), channel_id=1, source_target_pairs={{0,22},{1,23},{2,20},{3,21},{4,18},{5,19},{6,16},{7,17},{8,30},{9,... | collective-permute-start | bytes 147464 | tf_op jit(solution)/shard_map/ppermute | solution.py:560
  101.9 4.0 %collective-permute-start.15 = (f32[2,3,16,128]{3,2,1,0:T(8,128)}, f32[2,3,16,128]{3,2,1,0:T(8,128)S(1)}, u32[]{:S(2)}, u32[]{:S(2)}) collective-permute-start(f32[2,3,16,128]{3,2,1,0:T(8,128)} %get-tuple-element.40), channel_id=1, source_target_pairs={{0,23},{1,22},{2,21},{3,20},{4,19},{5,18},{6,17},{7,16},{8,31},{9,... | collective-permute-start | bytes 147464 | tf_op jit(solution)/shard_map/ppermute | solution.py:560
  106.2 3.6 %collective-permute-done.15 = f32[2,3,16,128]{3,2,1,0:T(8,128)S(1)} collective-permute-done((f32[2,3,16,128]{3,2,1,0:T(8,128)}, f32[2,3,16,128]{3,2,1,0:T(8,128)S(1)}, u32[]{:S(2)}, u32[]{:S(2)}) %collective-permute-start.15) | collective-permute-done | bytes 49184 | tf_op jit(solution)/shard_map/ppermute | solution.py:560
  109.8 0.9 copy-done.1
  110.7 11.7 %azimuth_interferogram.1 = f32[32,3,4,128]{3,2,1,0:T(4,128)} custom-call(s32[2]{0:T(128)} %pad_add_fusion.me_ref, s32[2]{0:T(128)} %fusion.same_ref, f32[32,3,5,16,128]{4,3,2,1,0:T(8,128)} %all-to-all-done.x_ref, f32[16,2,3,16,128]{4,3,2,1,0:T(8,128)} %copy-done.1, f32[768,768]{1,0:T(8,128)} %bitcast.47, f32[768,384]{1,0:T(8,128)} %collective-permute-done.16.other_angle, ...), custom_call_target="tpu_custom_call" | custom-call | flops 3623878656 | bytes 11796480 | tf_op jit(solution)/shard_map/azimuth_interferogram/pallas_call | solution.py:413
  122.4 14.6 %all_to_all.10.in_ref = f32[32,3,4,128]{3,2,1,0:T(4,128)} all-to-all(f32[32,3,4,128]{3,2,1,0:T(4,128)} %azimuth_interferogram.1), channel_id=1, replica_groups=mesh['acq'=2,'high'=4,'low'=4] {'acq','low','high'}, dimensions={0} | all-to-all | bytes 393216 | tf_op jit(solution)/shard_map/all_to_all | solution.py:536
  137.0 1.9 %place_samples.1 = f32[32,1536]{1,0:T(8,128)} custom-call(f32[32,3,4,128]{3,2,1,0:T(4,128)} %all_to_all.10.in_ref), custom_call_target="tpu_custom_call" | custom-call | tf_op jit(solution)/shard_map/place_samples/pallas_call | solution.py:525
  (45 shorter events, 3.7 us)
Async XLA Ops:
  3.7 22.3 %collective-permute-start = (f32[16,3,1,16,128]{4,3,2,1,0:T(8,128)}, f32[16,3,1,16,128]{4,3,2,1,0:T(8,128)S(1)}, u32[]{:S(2)}, u32[]{:S(2)}) collective-permute-start(f32[16,3,1,16,128]{4,3,2,1,0:T(8,128)} %get-tuple-element.24), channel_id=1, source_target_pairs={{0,8},{4,12},{8,0},{12,4},{1,9},{5,13},{9,1},{13,5},{2,10},{6,14},... | collective-permute-start | bytes 1179656 | tf_op jit(solution)/shard_map/ppermute | solution.py:553
  17.9 4.0 %copy-start = (f32[1,768,768]{2,1,0:T(8,128)S(1)}, f32[1,768,768]{2,1,0:T(8,128)}, u32[]{:S(2)}) copy-start(f32[1,768,768]{2,1,0:T(8,128)} %param.17) | copy-start | bytes 7077892
  17.9 91.9 %all-to-all-start = ((f32[32,3,5,16,128]{4,3,2,1,0:T(8,128)}), f32[32,3,5,16,128]{4,3,2,1,0:T(8,128)}, u32[]{:S(2)}, u32[]{:S(2)}) async-start(f32[32,3,5,16,128]{4,3,2,1,0:T(8,128)} %range_compress_1.1), calls=%async_computation | async-start | bytes 7864320 | tf_op jit(solution)/shard_map/all_to_all | solution.py:536
  21.9 2.8 %copy-start.2 = (s32[2,2]{1,0:T(2,128)S(1)}, s32[2,2]{1,0:T(2,128)}, u32[]{:S(2)}) copy-start(s32[2,2]{1,0:T(2,128)} %param.18) | copy-start | bytes 52
  23.0 86.9 %collective-permute-start.16 = (f32[768,384]{1,0:T(8,128)}, f32[768,384]{1,0:T(8,128)}, u32[]{:S(2)}, u32[]{:S(2)}) collective-permute-start(f32[768,384]{1,0:T(8,128)} %dynamic-slice_bitcast_fusion), channel_id=1, source_target_pairs={{0,16},{16,0},{1,17},{17,1},{2,18},{18,2},{3,19},{19,3},{4,20},{20... | collective-permute-start | bytes 3538952 | tf_op jit(solution)/shard_map/ppermute | solution.py:546
  26.0 0.8 copy-start.3
  28.7 4.2 %collective-permute-start.1 = (f32[2,3,16,128]{3,2,1,0:T(8,128)}, f32[2,3,16,128]{3,2,1,0:T(8,128)S(1)}, u32[]{:S(2)}, u32[]{:S(2)}) collective-permute-start(f32[2,3,16,128]{3,2,1,0:T(8,128)} %get-tuple-element.26), channel_id=1, source_target_pairs={{0,1},{1,0},{2,3},{3,2},{4,5},{5,4},{6,7},{7,6},{8,9},{9,8},{10,11... | collective-permute-start | bytes 147464 | tf_op jit(solution)/shard_map/ppermute | solution.py:560
  29.6 21.2 %collective-permute-start.2 = (f32[2,3,16,128]{3,2,1,0:T(8,128)}, f32[2,3,16,128]{3,2,1,0:T(8,128)S(1)}, u32[]{:S(2)}, u32[]{:S(2)}) collective-permute-start(f32[2,3,16,128]{3,2,1,0:T(8,128)} %get-tuple-element.27), channel_id=1, source_target_pairs={{0,2},{1,3},{2,0},{3,1},{4,6},{5,7},{6,4},{7,5},{8,10},{9,11},{10,... | collective-permute-start | bytes 147464 | tf_op jit(solution)/shard_map/ppermute | solution.py:560
  31.0 20.0 %collective-permute-start.3 = (f32[2,3,16,128]{3,2,1,0:T(8,128)}, f32[2,3,16,128]{3,2,1,0:T(8,128)S(1)}, u32[]{:S(2)}, u32[]{:S(2)}) collective-permute-start(f32[2,3,16,128]{3,2,1,0:T(8,128)} %get-tuple-element.28), channel_id=1, source_target_pairs={{0,3},{1,2},{2,1},{3,0},{4,7},{5,6},{6,5},{7,4},{8,11},{9,10},{10,... | collective-permute-start | bytes 147464 | tf_op jit(solution)/shard_map/ppermute | solution.py:560
  31.4 56.7 %collective-permute-start.4 = (f32[2,3,16,128]{3,2,1,0:T(8,128)}, f32[2,3,16,128]{3,2,1,0:T(8,128)S(1)}, u32[]{:S(2)}, u32[]{:S(2)}) collective-permute-start(f32[2,3,16,128]{3,2,1,0:T(8,128)} %get-tuple-element.29), channel_id=1, source_target_pairs={{0,4},{1,5},{2,6},{3,7},{4,0},{5,1},{6,2},{7,3},{8,12},{9,13},{10,... | collective-permute-start | bytes 147464 | tf_op jit(solution)/shard_map/ppermute | solution.py:560
  32.9 56.8 %collective-permute-start.5 = (f32[2,3,16,128]{3,2,1,0:T(8,128)}, f32[2,3,16,128]{3,2,1,0:T(8,128)S(1)}, u32[]{:S(2)}, u32[]{:S(2)}) collective-permute-start(f32[2,3,16,128]{3,2,1,0:T(8,128)} %get-tuple-element.30), channel_id=1, source_target_pairs={{0,5},{1,4},{2,7},{3,6},{4,1},{5,0},{6,3},{7,2},{8,13},{9,12},{10,... | collective-permute-start | bytes 147464 | tf_op jit(solution)/shard_map/ppermute | solution.py:560
  50.8 39.4 %collective-permute-start.6 = (f32[2,3,16,128]{3,2,1,0:T(8,128)}, f32[2,3,16,128]{3,2,1,0:T(8,128)S(1)}, u32[]{:S(2)}, u32[]{:S(2)}) collective-permute-start(f32[2,3,16,128]{3,2,1,0:T(8,128)} %get-tuple-element.31), channel_id=1, source_target_pairs={{0,6},{1,7},{2,4},{3,5},{4,2},{5,3},{6,0},{7,1},{8,14},{9,15},{10,... | collective-permute-start | bytes 147464 | tf_op jit(solution)/shard_map/ppermute | solution.py:560
  51.0 43.3 %collective-permute-start.7 = (f32[2,3,16,128]{3,2,1,0:T(8,128)}, f32[2,3,16,128]{3,2,1,0:T(8,128)S(1)}, u32[]{:S(2)}, u32[]{:S(2)}) collective-permute-start(f32[2,3,16,128]{3,2,1,0:T(8,128)} %get-tuple-element.32), channel_id=1, source_target_pairs={{0,7},{1,6},{2,5},{3,4},{4,3},{5,2},{6,1},{7,0},{8,15},{9,14},{10,... | collective-permute-start | bytes 147464 | tf_op jit(solution)/shard_map/ppermute | solution.py:560
  88.1 6.3 %collective-permute-start.8 = (f32[2,3,16,128]{3,2,1,0:T(8,128)}, f32[2,3,16,128]{3,2,1,0:T(8,128)S(1)}, u32[]{:S(2)}, u32[]{:S(2)}) collective-permute-start(f32[2,3,16,128]{3,2,1,0:T(8,128)} %get-tuple-element.33), channel_id=1, source_target_pairs={{0,16},{1,17},{2,18},{3,19},{4,20},{5,21},{6,22},{7,23},{8,24},{9,... | collective-permute-start | bytes 147464 | tf_op jit(solution)/shard_map/ppermute | solution.py:560
  89.7 8.6 %collective-permute-start.9 = (f32[2,3,16,128]{3,2,1,0:T(8,128)}, f32[2,3,16,128]{3,2,1,0:T(8,128)S(1)}, u32[]{:S(2)}, u32[]{:S(2)}) collective-permute-start(f32[2,3,16,128]{3,2,1,0:T(8,128)} %get-tuple-element.34), channel_id=1, source_target_pairs={{0,17},{1,16},{2,19},{3,18},{4,21},{5,20},{6,23},{7,22},{8,25},{9,... | collective-permute-start | bytes 147464 | tf_op jit(solution)/shard_map/ppermute | solution.py:560
  90.2 8.8 %collective-permute-start.10 = (f32[2,3,16,128]{3,2,1,0:T(8,128)}, f32[2,3,16,128]{3,2,1,0:T(8,128)S(1)}, u32[]{:S(2)}, u32[]{:S(2)}) collective-permute-start(f32[2,3,16,128]{3,2,1,0:T(8,128)} %get-tuple-element.35), channel_id=1, source_target_pairs={{0,18},{1,19},{2,16},{3,17},{4,22},{5,23},{6,20},{7,21},{8,26},{9,... | collective-permute-start | bytes 147464 | tf_op jit(solution)/shard_map/ppermute | solution.py:560
  94.4 7.6 %collective-permute-start.11 = (f32[2,3,16,128]{3,2,1,0:T(8,128)}, f32[2,3,16,128]{3,2,1,0:T(8,128)S(1)}, u32[]{:S(2)}, u32[]{:S(2)}) collective-permute-start(f32[2,3,16,128]{3,2,1,0:T(8,128)} %get-tuple-element.36), channel_id=1, source_target_pairs={{0,19},{1,18},{2,17},{3,16},{4,23},{5,22},{6,21},{7,20},{8,27},{9,... | collective-permute-start | bytes 147464 | tf_op jit(solution)/shard_map/ppermute | solution.py:560
  94.5 11.5 %collective-permute-start.12 = (f32[2,3,16,128]{3,2,1,0:T(8,128)}, f32[2,3,16,128]{3,2,1,0:T(8,128)S(1)}, u32[]{:S(2)}, u32[]{:S(2)}) collective-permute-start(f32[2,3,16,128]{3,2,1,0:T(8,128)} %get-tuple-element.37), channel_id=1, source_target_pairs={{0,20},{1,21},{2,22},{3,23},{4,16},{5,17},{6,18},{7,19},{8,28},{9,... | collective-permute-start | bytes 147464 | tf_op jit(solution)/shard_map/ppermute | solution.py:560
  98.3 7.7 %collective-permute-start.13 = (f32[2,3,16,128]{3,2,1,0:T(8,128)}, f32[2,3,16,128]{3,2,1,0:T(8,128)S(1)}, u32[]{:S(2)}, u32[]{:S(2)}) collective-permute-start(f32[2,3,16,128]{3,2,1,0:T(8,128)} %get-tuple-element.38), channel_id=1, source_target_pairs={{0,21},{1,20},{2,23},{3,22},{4,17},{5,16},{6,19},{7,18},{8,29},{9,... | collective-permute-start | bytes 147464 | tf_op jit(solution)/shard_map/ppermute | solution.py:560
  99.1 7.1 %collective-permute-start.14 = (f32[2,3,16,128]{3,2,1,0:T(8,128)}, f32[2,3,16,128]{3,2,1,0:T(8,128)S(1)}, u32[]{:S(2)}, u32[]{:S(2)}) collective-permute-start(f32[2,3,16,128]{3,2,1,0:T(8,128)} %get-tuple-element.39), channel_id=1, source_target_pairs={{0,22},{1,23},{2,20},{3,21},{4,18},{5,19},{6,16},{7,17},{8,30},{9,... | collective-permute-start | bytes 147464 | tf_op jit(solution)/shard_map/ppermute | solution.py:560
  101.9 7.9 %collective-permute-start.15 = (f32[2,3,16,128]{3,2,1,0:T(8,128)}, f32[2,3,16,128]{3,2,1,0:T(8,128)S(1)}, u32[]{:S(2)}, u32[]{:S(2)}) collective-permute-start(f32[2,3,16,128]{3,2,1,0:T(8,128)} %get-tuple-element.40), channel_id=1, source_target_pairs={{0,23},{1,22},{2,21},{3,20},{4,19},{5,18},{6,17},{7,16},{8,31},{9,... | collective-permute-start | bytes 147464 | tf_op jit(solution)/shard_map/ppermute | solution.py:560
  109.8 0.9 copy-start.1

commit v6 on v4

--- a/solution.py
+++ b/solution.py
@@ -291,22 +291,25 @@
     part = xr.shape[0] // CLASSES
     x = [(xr[k * part : (k + 1) * part], xi[k * part : (k + 1) * part]) for k in range(CLASSES)]
     columns = [thirds(*[x[(4 * i + 3 * j) % CLASSES] for i in range(3)], -1.0) for j in range(4)]
-    classes = [None] * CLASSES
-    for e in range(3):
-        for g, pair in enumerate(fours(*[columns[j][e] for j in range(4)])):
-            classes[class_of(e, g)] = pair
-    z, forward = [], []
-    for f0 in range(CLASSES + 1):
-        if f0 < CLASSES:
-            forward.append(dot_parts(fw[f0], jnp.concatenate(classes[f0], axis=0)))
-        if f0 > 0:
-            y, k = forward[f0 - 1], f0 - 1
+    made, ahead, done, sums = [], [], [], []
+    make = lambda e: made.append(fours(*[columns[j][e] for j in range(4)]))
+    make(0)
+    for i in range(CLASSES + 1):
+        e, g = divmod(i, 4)
+        if g == 2 and e < 2:
+            make(e + 1)
+        if i < CLASSES:
+            ahead.append(dot_parts(fw[class_of(e, g)], jnp.concatenate(made[e][g], axis=0)))
+        if i > 0:
+            y, k = ahead[i - 1], class_of(*divmod(i - 1, 4))
             dr, di = y[:part], y[part:]
             pc, ps = phases(k)
-            e = jnp.concatenate([dr * pc - di * ps, dr * ps + di * pc], axis=0)
-            y = dot_parts(bw[k], e)
-            z.append((y[:part], y[part:]))
-    sums = [fours(*[z[class_of(e, g)] for g in range(4)]) for e in range(3)]
+            value = jnp.concatenate([dr * pc - di * ps, dr * ps + di * pc], axis=0)
+            y = dot_parts(bw[k], value)
+            done.append((y[:part], y[part:]))
+            if i > 4 and g == 1:
+                sums.append(fours(*done[i - 5 : i - 1]))
+    sums.append(fours(*done[8:]))
     outs = []
     for h in range(AOI // part):
         terms = [sums[e][h] for e in range(3)]

time: 139 us -> 139 us (level)
  no operation moved by 1% of the time
where the time goes in v6:
time: 139 us
  waiting for transfers between devices  57.9 us (42%)
  starting transfers between devices  31.9 us (23%)
  Pallas kernels  29.6 us (21%)
  blocking collectives  14.6 us (11%)
  local copies, waits for them, and re-layouts  3.61 us (3%)
    ppermute x15, waiting for transfers between devices, joint(): lax.ppermute(early[s], ('acq', 'high', 'low'), [(i, i ^ flip) for i in ra...  57.9 us
    ppermute x15, starting transfers between devices, joint(): lax.ppermute(early[s], ('acq', 'high', 'low'), [(i, i ^ flip) for i in ra...  22.2 us
    all_to_all x1, blocking collectives, turn(): return lax.all_to_all(array, axes, split_axis=0, concat_axis=0, tiled=True)  14.6 us
    pallas_call x2, Pallas kernels, range_call(): pl.pallas_call(functools.partial(range_kernel, outer, early), grid=(steps...  13.9 us
    pallas_call x1, Pallas kernels, joint_call(): pl.pallas_call(functools.partial(joint_kernel, order, rounds), grid_spec=...  11.8 us
    ppermute x1, starting transfers between devices, joint(): came = lax.ppermute(given, 'high', [(h, h ^ FAR // 2) for h in range(FAR)])  4.04 us
    all_to_all x1, starting transfers between devices, turn(): return lax.all_to_all(array, axes, split_axis=0, concat_axis=0, tiled=True)  3.94 us
  transfers between devices with their start and end apart: 18, of which 6 were waited for; matrix products, arithmetic and copies ran while one was open for 2% of the time, Pallas kernels for 9%

profile of v6, /device:TPU:0, one launch (start us, length us, event | category | flops | bytes accessed | tf_op | source)
XLA Modules:
  0.0 139.1 jit_solution(17727728177371106395)
XLA Ops:
  0.0 3.7 %range_compress_0.1 = (f32[16,3,1,16,128]{4,3,2,1,0:T(8,128)}, f32[16,3,1,16,128]{4,3,2,1,0:T(8,128)}) custom-call(f32[2,6,768,128]{3,2,1,0:T(8,128)} %bitcast.45, f32[2,1,12288]{2,1,0:T(1,128)} %slant_ref.3, bf16[3,128,128]{2,1,0:T(8,128)(2,1)} %constant.43.clone.a1_ref, bf16[512,256]{1,0:T(8,128)(2,1)} %constant.44.clone.b2_ref, ...), custom_call_target="tpu_custom_call" | custom-call | flops 1056964608 | bytes 1572864 | tf_op jit(solution)/shard_map/range_compress_0/pallas_call | solution.py:209
  3.7 4.0 %collective-permute-start = (f32[16,3,1,16,128]{4,3,2,1,0:T(8,128)}, f32[16,3,1,16,128]{4,3,2,1,0:T(8,128)S(1)}, u32[]{:S(2)}, u32[]{:S(2)}) collective-permute-start(f32[16,3,1,16,128]{4,3,2,1,0:T(8,128)} %get-tuple-element.24), channel_id=1, source_target_pairs={{0,8},{4,12},{8,0},{12,4},{1,9},{5,13},{9,1},{13,5},{2,10},{6,14},... | collective-permute-start | bytes 1179656 | tf_op jit(solution)/shard_map/ppermute | solution.py:546
  7.7 10.2 %range_compress_1.1 = f32[32,3,5,16,128]{4,3,2,1,0:T(8,128)} custom-call(f32[2,6,768,128]{3,2,1,0:T(8,128)} %bitcast.46, f32[2,1,12288]{2,1,0:T(1,128)} %slant_ref.3, bf16[3,128,128]{2,1,0:T(8,128)(2,1)} %constant.43.clone.a1_ref, bf16[512,256]{1,0:T(8,128)(2,1)} %constant.44.clone.b2_ref, bf16[3,128,128]{2,1,0:T(8,128)(2,1)} %constant.45.clone.a4_ref, ...), custom_call_target="tpu_custom_call" | custom-call | flops 5284823040 | bytes 7864320 | tf_op jit(solution)/shard_map/range_compress_1/pallas_call | solution.py:209
  17.9 3.9 %all-to-all-start = ((f32[32,3,5,16,128]{4,3,2,1,0:T(8,128)}), f32[32,3,5,16,128]{4,3,2,1,0:T(8,128)}, u32[]{:S(2)}, u32[]{:S(2)}) async-start(f32[32,3,5,16,128]{4,3,2,1,0:T(8,128)} %range_compress_1.1), calls=%async_computation | async-start | bytes 7864320 | tf_op jit(solution)/shard_map/all_to_all | solution.py:529
  21.9 1.1 dynamic-slice_bitcast_fusion
  23.0 1.7 %collective-permute-start.16 = (f32[768,384]{1,0:T(8,128)}, f32[768,384]{1,0:T(8,128)}, u32[]{:S(2)}, u32[]{:S(2)}) collective-permute-start(f32[768,384]{1,0:T(8,128)} %dynamic-slice_bitcast_fusion), channel_id=1, source_target_pairs={{0,16},{16,0},{1,17},{17,1},{2,18},{18,2},{3,19},{19,3},{4,20},{20... | collective-permute-start | bytes 3538952 | tf_op jit(solution)/shard_map/ppermute | solution.py:539
  26.0 0.8 copy-done.3
  26.8 2.0 %pair_halves.1 = (f32[2,3,16,128]{3,2,1,0:T(8,128)}, f32[2,3,16,128]{3,2,1,0:T(8,128)}, f32[2,3,16,128]{3,2,1,0:T(8,128)}, f32[2,3,16,128]{3,2,1,0:T(8,128)}, f3...) custom-call(f32[16,3,1,16,128]{4,3,2,1,0:T(8,128)} %get-tuple-elemen, ...), custom_call_target="tpu_custom_call" | custom-call | flops 999999995904 | bytes 393216 | tf_op jit(solution)/shard_map/pair_halves/pallas_call | solution.py:238
  28.8 0.8 bitcast_dynamic-update-slice_fusion.15
  29.6 1.5 %collective-permute-start.2 = (f32[2,3,16,128]{3,2,1,0:T(8,128)}, f32[2,3,16,128]{3,2,1,0:T(8,128)S(1)}, u32[]{:S(2)}, u32[]{:S(2)}) collective-permute-start(f32[2,3,16,128]{3,2,1,0:T(8,128)} %get-tuple-element.27), channel_id=1, source_target_pairs={{0,2},{1,3},{2,0},{3,1},{4,6},{5,7},{6,4},{7,5},{8,10},{9,11},{10,... | collective-permute-start | bytes 147464 | tf_op jit(solution)/shard_map/ppermute | solution.py:553
  31.4 1.5 %collective-permute-start.4 = (f32[2,3,16,128]{3,2,1,0:T(8,128)}, f32[2,3,16,128]{3,2,1,0:T(8,128)S(1)}, u32[]{:S(2)}, u32[]{:S(2)}) collective-permute-start(f32[2,3,16,128]{3,2,1,0:T(8,128)} %get-tuple-element.29), channel_id=1, source_target_pairs={{0,4},{1,5},{2,6},{3,7},{4,0},{5,1},{6,2},{7,3},{8,12},{9,13},{10,... | collective-permute-start | bytes 147464 | tf_op jit(solution)/shard_map/ppermute | solution.py:553
  33.1 17.7 %collective-permute-done.2 = f32[2,3,16,128]{3,2,1,0:T(8,128)S(1)} collective-permute-done((f32[2,3,16,128]{3,2,1,0:T(8,128)}, f32[2,3,16,128]{3,2,1,0:T(8,128)S(1)}, u32[]{:S(2)}, u32[]{:S(2)}) %collective-permute-start.2) | collective-permute-done | bytes 49184 | tf_op jit(solution)/shard_map/ppermute | solution.py:553
  51.0 1.4 collective-permute-start.7
  52.4 35.7 %collective-permute-done.4 = f32[2,3,16,128]{3,2,1,0:T(8,128)S(1)} collective-permute-done((f32[2,3,16,128]{3,2,1,0:T(8,128)}, f32[2,3,16,128]{3,2,1,0:T(8,128)S(1)}, u32[]{:S(2)}, u32[]{:S(2)}) %collective-permute-start.4) | collective-permute-done | bytes 49184 | tf_op jit(solution)/shard_map/ppermute | solution.py:553
  88.1 1.6 %collective-permute-start.8 = (f32[2,3,16,128]{3,2,1,0:T(8,128)}, f32[2,3,16,128]{3,2,1,0:T(8,128)S(1)}, u32[]{:S(2)}, u32[]{:S(2)}) collective-permute-start(f32[2,3,16,128]{3,2,1,0:T(8,128)} %get-tuple-element.33), channel_id=1, source_target_pairs={{0,16},{1,17},{2,18},{3,19},{4,20},{5,21},{6,22},{7,23},{8,24},{9,... | collective-permute-start | bytes 147464 | tf_op jit(solution)/shard_map/ppermute | solution.py:553
  90.2 4.1 %collective-permute-start.10 = (f32[2,3,16,128]{3,2,1,0:T(8,128)}, f32[2,3,16,128]{3,2,1,0:T(8,128)S(1)}, u32[]{:S(2)}, u32[]{:S(2)}) collective-permute-start(f32[2,3,16,128]{3,2,1,0:T(8,128)} %get-tuple-element.35), channel_id=1, source_target_pairs={{0,18},{1,19},{2,16},{3,17},{4,22},{5,23},{6,20},{7,21},{8,26},{9,... | collective-permute-start | bytes 147464 | tf_op jit(solution)/shard_map/ppermute | solution.py:553
  94.5 3.8 %collective-permute-start.12 = (f32[2,3,16,128]{3,2,1,0:T(8,128)}, f32[2,3,16,128]{3,2,1,0:T(8,128)S(1)}, u32[]{:S(2)}, u32[]{:S(2)}) collective-permute-start(f32[2,3,16,128]{3,2,1,0:T(8,128)} %get-tuple-element.37), channel_id=1, source_target_pairs={{0,20},{1,21},{2,22},{3,23},{4,16},{5,17},{6,18},{7,19},{8,28},{9,... | collective-permute-start | bytes 147464 | tf_op jit(solution)/shard_map/ppermute | solution.py:553
  99.1 2.9 %collective-permute-start.14 = (f32[2,3,16,128]{3,2,1,0:T(8,128)}, f32[2,3,16,128]{3,2,1,0:T(8,128)S(1)}, u32[]{:S(2)}, u32[]{:S(2)}) collective-permute-start(f32[2,3,16,128]{3,2,1,0:T(8,128)} %get-tuple-element.39), channel_id=1, source_target_pairs={{0,22},{1,23},{2,20},{3,21},{4,18},{5,19},{6,16},{7,17},{8,30},{9,... | collective-permute-start | bytes 147464 | tf_op jit(solution)/shard_map/ppermute | solution.py:553
  101.9 4.0 %collective-permute-start.15 = (f32[2,3,16,128]{3,2,1,0:T(8,128)}, f32[2,3,16,128]{3,2,1,0:T(8,128)S(1)}, u32[]{:S(2)}, u32[]{:S(2)}) collective-permute-start(f32[2,3,16,128]{3,2,1,0:T(8,128)} %get-tuple-element.40), channel_id=1, source_target_pairs={{0,23},{1,22},{2,21},{3,20},{4,19},{5,18},{6,17},{7,16},{8,31},{9,... | collective-permute-start | bytes 147464 | tf_op jit(solution)/shard_map/ppermute | solution.py:553
  106.2 3.6 %collective-permute-done.15 = f32[2,3,16,128]{3,2,1,0:T(8,128)S(1)} collective-permute-done((f32[2,3,16,128]{3,2,1,0:T(8,128)}, f32[2,3,16,128]{3,2,1,0:T(8,128)S(1)}, u32[]{:S(2)}, u32[]{:S(2)}) %collective-permute-start.15) | collective-permute-done | bytes 49184 | tf_op jit(solution)/shard_map/ppermute | solution.py:553
  109.8 0.9 copy-done.1
  110.7 11.8 %azimuth_interferogram.1 = f32[32,3,4,128]{3,2,1,0:T(4,128)} custom-call(s32[2]{0:T(128)} %pad_add_fusion.me_ref, s32[2]{0:T(128)} %fusion.same_ref, f32[32,3,5,16,128]{4,3,2,1,0:T(8,128)} %all-to-all-done.x_ref, f32[16,2,3,16,128]{4,3,2,1,0:T(8,128)} %copy-done.1, f32[768,768]{1,0:T(8,128)} %bitcast.47, f32[768,384]{1,0:T(8,128)} %collective-permute-done.16.other_angle, ...), custom_call_target="tpu_custom_call" | custom-call | flops 3623878656 | bytes 11796480 | tf_op jit(solution)/shard_map/azimuth_interferogram/pallas_call | solution.py:405
  122.6 14.6 %all_to_all.10.in_ref = f32[32,3,4,128]{3,2,1,0:T(4,128)} all-to-all(f32[32,3,4,128]{3,2,1,0:T(4,128)} %azimuth_interferogram.1), channel_id=1, replica_groups=mesh['acq'=2,'high'=4,'low'=4] {'acq','low','high'}, dimensions={0} | all-to-all | bytes 393216 | tf_op jit(solution)/shard_map/all_to_all | solution.py:529
  137.2 1.9 %place_samples.1 = f32[32,1536]{1,0:T(8,128)} custom-call(f32[32,3,4,128]{3,2,1,0:T(4,128)} %all_to_all.10.in_ref), custom_call_target="tpu_custom_call" | custom-call | tf_op jit(solution)/shard_map/place_samples/pallas_call | solution.py:518
  (45 shorter events, 3.7 us)
Async XLA Ops:
  3.7 22.3 %collective-permute-start = (f32[16,3,1,16,128]{4,3,2,1,0:T(8,128)}, f32[16,3,1,16,128]{4,3,2,1,0:T(8,128)S(1)}, u32[]{:S(2)}, u32[]{:S(2)}) collective-permute-start(f32[16,3,1,16,128]{4,3,2,1,0:T(8,128)} %get-tuple-element.24), channel_id=1, source_target_pairs={{0,8},{4,12},{8,0},{12,4},{1,9},{5,13},{9,1},{13,5},{2,10},{6,14},... | collective-permute-start | bytes 1179656 | tf_op jit(solution)/shard_map/ppermute | solution.py:546
  17.9 4.0 %copy-start = (f32[1,768,768]{2,1,0:T(8,128)S(1)}, f32[1,768,768]{2,1,0:T(8,128)}, u32[]{:S(2)}) copy-start(f32[1,768,768]{2,1,0:T(8,128)} %param.17) | copy-start | bytes 7077892
  17.9 91.9 %all-to-all-start = ((f32[32,3,5,16,128]{4,3,2,1,0:T(8,128)}), f32[32,3,5,16,128]{4,3,2,1,0:T(8,128)}, u32[]{:S(2)}, u32[]{:S(2)}) async-start(f32[32,3,5,16,128]{4,3,2,1,0:T(8,128)} %range_compress_1.1), calls=%async_computation | async-start | bytes 7864320 | tf_op jit(solution)/shard_map/all_to_all | solution.py:529
  21.9 2.8 %copy-start.2 = (s32[2,2]{1,0:T(2,128)S(1)}, s32[2,2]{1,0:T(2,128)}, u32[]{:S(2)}) copy-start(s32[2,2]{1,0:T(2,128)} %param.18) | copy-start | bytes 52
  23.0 86.9 %collective-permute-start.16 = (f32[768,384]{1,0:T(8,128)}, f32[768,384]{1,0:T(8,128)}, u32[]{:S(2)}, u32[]{:S(2)}) collective-permute-start(f32[768,384]{1,0:T(8,128)} %dynamic-slice_bitcast_fusion), channel_id=1, source_target_pairs={{0,16},{16,0},{1,17},{17,1},{2,18},{18,2},{3,19},{19,3},{4,20},{20... | collective-permute-start | bytes 3538952 | tf_op jit(solution)/shard_map/ppermute | solution.py:539
  26.0 0.8 copy-start.3
  28.7 4.2 %collective-permute-start.1 = (f32[2,3,16,128]{3,2,1,0:T(8,128)}, f32[2,3,16,128]{3,2,1,0:T(8,128)S(1)}, u32[]{:S(2)}, u32[]{:S(2)}) collective-permute-start(f32[2,3,16,128]{3,2,1,0:T(8,128)} %get-tuple-element.26), channel_id=1, source_target_pairs={{0,1},{1,0},{2,3},{3,2},{4,5},{5,4},{6,7},{7,6},{8,9},{9,8},{10,11... | collective-permute-start | bytes 147464 | tf_op jit(solution)/shard_map/ppermute | solution.py:553
  29.6 21.2 %collective-permute-start.2 = (f32[2,3,16,128]{3,2,1,0:T(8,128)}, f32[2,3,16,128]{3,2,1,0:T(8,128)S(1)}, u32[]{:S(2)}, u32[]{:S(2)}) collective-permute-start(f32[2,3,16,128]{3,2,1,0:T(8,128)} %get-tuple-element.27), channel_id=1, source_target_pairs={{0,2},{1,3},{2,0},{3,1},{4,6},{5,7},{6,4},{7,5},{8,10},{9,11},{10,... | collective-permute-start | bytes 147464 | tf_op jit(solution)/shard_map/ppermute | solution.py:553
  31.0 20.0 %collective-permute-start.3 = (f32[2,3,16,128]{3,2,1,0:T(8,128)}, f32[2,3,16,128]{3,2,1,0:T(8,128)S(1)}, u32[]{:S(2)}, u32[]{:S(2)}) collective-permute-start(f32[2,3,16,128]{3,2,1,0:T(8,128)} %get-tuple-element.28), channel_id=1, source_target_pairs={{0,3},{1,2},{2,1},{3,0},{4,7},{5,6},{6,5},{7,4},{8,11},{9,10},{10,... | collective-permute-start | bytes 147464 | tf_op jit(solution)/shard_map/ppermute | solution.py:553
  31.4 56.7 %collective-permute-start.4 = (f32[2,3,16,128]{3,2,1,0:T(8,128)}, f32[2,3,16,128]{3,2,1,0:T(8,128)S(1)}, u32[]{:S(2)}, u32[]{:S(2)}) collective-permute-start(f32[2,3,16,128]{3,2,1,0:T(8,128)} %get-tuple-element.29), channel_id=1, source_target_pairs={{0,4},{1,5},{2,6},{3,7},{4,0},{5,1},{6,2},{7,3},{8,12},{9,13},{10,... | collective-permute-start | bytes 147464 | tf_op jit(solution)/shard_map/ppermute | solution.py:553
  32.9 56.8 %collective-permute-start.5 = (f32[2,3,16,128]{3,2,1,0:T(8,128)}, f32[2,3,16,128]{3,2,1,0:T(8,128)S(1)}, u32[]{:S(2)}, u32[]{:S(2)}) collective-permute-start(f32[2,3,16,128]{3,2,1,0:T(8,128)} %get-tuple-element.30), channel_id=1, source_target_pairs={{0,5},{1,4},{2,7},{3,6},{4,1},{5,0},{6,3},{7,2},{8,13},{9,12},{10,... | collective-permute-start | bytes 147464 | tf_op jit(solution)/shard_map/ppermute | solution.py:553
  50.8 39.4 %collective-permute-start.6 = (f32[2,3,16,128]{3,2,1,0:T(8,128)}, f32[2,3,16,128]{3,2,1,0:T(8,128)S(1)}, u32[]{:S(2)}, u32[]{:S(2)}) collective-permute-start(f32[2,3,16,128]{3,2,1,0:T(8,128)} %get-tuple-element.31), channel_id=1, source_target_pairs={{0,6},{1,7},{2,4},{3,5},{4,2},{5,3},{6,0},{7,1},{8,14},{9,15},{10,... | collective-permute-start | bytes 147464 | tf_op jit(solution)/shard_map/ppermute | solution.py:553
  51.0 43.3 %collective-permute-start.7 = (f32[2,3,16,128]{3,2,1,0:T(8,128)}, f32[2,3,16,128]{3,2,1,0:T(8,128)S(1)}, u32[]{:S(2)}, u32[]{:S(2)}) collective-permute-start(f32[2,3,16,128]{3,2,1,0:T(8,128)} %get-tuple-element.32), channel_id=1, source_target_pairs={{0,7},{1,6},{2,5},{3,4},{4,3},{5,2},{6,1},{7,0},{8,15},{9,14},{10,... | collective-permute-start | bytes 147464 | tf_op jit(solution)/shard_map/ppermute | solution.py:553
  88.1 6.3 %collective-permute-start.8 = (f32[2,3,16,128]{3,2,1,0:T(8,128)}, f32[2,3,16,128]{3,2,1,0:T(8,128)S(1)}, u32[]{:S(2)}, u32[]{:S(2)}) collective-permute-start(f32[2,3,16,128]{3,2,1,0:T(8,128)} %get-tuple-element.33), channel_id=1, source_target_pairs={{0,16},{1,17},{2,18},{3,19},{4,20},{5,21},{6,22},{7,23},{8,24},{9,... | collective-permute-start | bytes 147464 | tf_op jit(solution)/shard_map/ppermute | solution.py:553
  89.7 8.6 %collective-permute-start.9 = (f32[2,3,16,128]{3,2,1,0:T(8,128)}, f32[2,3,16,128]{3,2,1,0:T(8,128)S(1)}, u32[]{:S(2)}, u32[]{:S(2)}) collective-permute-start(f32[2,3,16,128]{3,2,1,0:T(8,128)} %get-tuple-element.34), channel_id=1, source_target_pairs={{0,17},{1,16},{2,19},{3,18},{4,21},{5,20},{6,23},{7,22},{8,25},{9,... | collective-permute-start | bytes 147464 | tf_op jit(solution)/shard_map/ppermute | solution.py:553
  90.2 8.8 %collective-permute-start.10 = (f32[2,3,16,128]{3,2,1,0:T(8,128)}, f32[2,3,16,128]{3,2,1,0:T(8,128)S(1)}, u32[]{:S(2)}, u32[]{:S(2)}) collective-permute-start(f32[2,3,16,128]{3,2,1,0:T(8,128)} %get-tuple-element.35), channel_id=1, source_target_pairs={{0,18},{1,19},{2,16},{3,17},{4,22},{5,23},{6,20},{7,21},{8,26},{9,... | collective-permute-start | bytes 147464 | tf_op jit(solution)/shard_map/ppermute | solution.py:553
  94.4 7.6 %collective-permute-start.11 = (f32[2,3,16,128]{3,2,1,0:T(8,128)}, f32[2,3,16,128]{3,2,1,0:T(8,128)S(1)}, u32[]{:S(2)}, u32[]{:S(2)}) collective-permute-start(f32[2,3,16,128]{3,2,1,0:T(8,128)} %get-tuple-element.36), channel_id=1, source_target_pairs={{0,19},{1,18},{2,17},{3,16},{4,23},{5,22},{6,21},{7,20},{8,27},{9,... | collective-permute-start | bytes 147464 | tf_op jit(solution)/shard_map/ppermute | solution.py:553
  94.5 11.5 %collective-permute-start.12 = (f32[2,3,16,128]{3,2,1,0:T(8,128)}, f32[2,3,16,128]{3,2,1,0:T(8,128)S(1)}, u32[]{:S(2)}, u32[]{:S(2)}) collective-permute-start(f32[2,3,16,128]{3,2,1,0:T(8,128)} %get-tuple-element.37), channel_id=1, source_target_pairs={{0,20},{1,21},{2,22},{3,23},{4,16},{5,17},{6,18},{7,19},{8,28},{9,... | collective-permute-start | bytes 147464 | tf_op jit(solution)/shard_map/ppermute | solution.py:553
  98.3 7.7 %collective-permute-start.13 = (f32[2,3,16,128]{3,2,1,0:T(8,128)}, f32[2,3,16,128]{3,2,1,0:T(8,128)S(1)}, u32[]{:S(2)}, u32[]{:S(2)}) collective-permute-start(f32[2,3,16,128]{3,2,1,0:T(8,128)} %get-tuple-element.38), channel_id=1, source_target_pairs={{0,21},{1,20},{2,23},{3,22},{4,17},{5,16},{6,19},{7,18},{8,29},{9,... | collective-permute-start | bytes 147464 | tf_op jit(solution)/shard_map/ppermute | solution.py:553
  99.1 7.1 %collective-permute-start.14 = (f32[2,3,16,128]{3,2,1,0:T(8,128)}, f32[2,3,16,128]{3,2,1,0:T(8,128)S(1)}, u32[]{:S(2)}, u32[]{:S(2)}) collective-permute-start(f32[2,3,16,128]{3,2,1,0:T(8,128)} %get-tuple-element.39), channel_id=1, source_target_pairs={{0,22},{1,23},{2,20},{3,21},{4,18},{5,19},{6,16},{7,17},{8,30},{9,... | collective-permute-start | bytes 147464 | tf_op jit(solution)/shard_map/ppermute | solution.py:553
  101.9 7.9 %collective-permute-start.15 = (f32[2,3,16,128]{3,2,1,0:T(8,128)}, f32[2,3,16,128]{3,2,1,0:T(8,128)S(1)}, u32[]{:S(2)}, u32[]{:S(2)}) collective-permute-start(f32[2,3,16,128]{3,2,1,0:T(8,128)} %get-tuple-element.40), channel_id=1, source_target_pairs={{0,23},{1,22},{2,21},{3,20},{4,19},{5,18},{6,17},{7,16},{8,31},{9,... | collective-permute-start | bytes 147464 | tf_op jit(solution)/shard_map/ppermute | solution.py:553
  109.8 0.9 copy-start.1

commit v7 on v4

--- a/solution.py
+++ b/solution.py
@@ -118,17 +118,18 @@
     outs, (rows_ref, h_ref), held = rest[: 1 + early], rest[1 + early : 3 + early], rest[3 + early :]
     part = outer // 3
 
-    @pl.when(pl.program_id(0) == 0)
-    def _():
+    def arrange():
         for c in range(2):
             for k2 in range(LANES):
                 rows_ref[c, k2 : k2 + 1, :outer] = slant_ref[c, :, k2 * outer : (k2 + 1) * outer]
             h_ref[c] = rows_ref[c].T[:outer]
 
+    if not early:
+        pl.when(pl.program_id(0) == 0)(arrange)
+
     rows = outs[0].shape[1] * outs[0].shape[3]
     turned = held[0] if early else outs[0].reshape(outs[0].shape[0] * rows, LANES)
     ct, st = t_ref[0], t_ref[1]
-    hr, hi = h_ref[0], h_ref[1]
 
     def batch(first):
         lines = range(first, first + BATCH)
@@ -152,6 +153,7 @@
             z.append(jnp.concatenate([yr * ct + yi * st, yi * ct - yr * st], axis=1))
         y = dot_table_right(jnp.concatenate(z, axis=0), b2_ref[...])
         yield
+        hr, hi = h_ref[0], h_ref[1]
         z = []
         for b in range(BATCH):
             yr = y[b * outer : (b + 1) * outer, :LANES]
@@ -179,9 +181,11 @@
         yield
 
     batches = [batch(first) for first in range(0, SUB, BATCH)]
-    for _ in range(5):
+    for stage in range(5):
         for work in batches:
             next(work)
+        if early and stage == 0:
+            arrange()
     if not early:
         return
     near = outs[0].shape[0] // 2

time: 139 us -> 139 us (level)
  no operation moved by 1% of the time
where the time goes in v7:
time: 139 us
  waiting for transfers between devices  57.9 us (42%)
  starting transfers between devices  31.9 us (23%)
  Pallas kernels  29.3 us (21%)
  blocking collectives  14.6 us (11%)
  local copies, waits for them, and re-layouts  3.61 us (3%)
    ppermute x15, waiting for transfers between devices, joint(): lax.ppermute(early[s], ('acq', 'high', 'low'), [(i, i ^ flip) for i in ra...  57.8 us
    ppermute x15, starting transfers between devices, joint(): lax.ppermute(early[s], ('acq', 'high', 'low'), [(i, i ^ flip) for i in ra...  22.3 us
    all_to_all x1, blocking collectives, turn(): return lax.all_to_all(array, axes, split_axis=0, concat_axis=0, tiled=True)  14.6 us
    pallas_call x2, Pallas kernels, range_call(): pl.pallas_call(functools.partial(range_kernel, outer, early), grid=(steps...  13.9 us
    pallas_call x1, Pallas kernels, joint_call(): pl.pallas_call(functools.partial(joint_kernel, order, rounds), grid_spec=...  11.6 us
    ppermute x1, starting transfers between devices, joint(): came = lax.ppermute(given, 'high', [(h, h ^ FAR // 2) for h in range(FAR)])  4.04 us
    all_to_all x1, starting transfers between devices, turn(): return lax.all_to_all(array, axes, split_axis=0, concat_axis=0, tiled=True)  3.94 us
  transfers between devices with their start and end apart: 18, of which 6 were waited for; matrix products, arithmetic and copies ran while one was open for 2% of the time, Pallas kernels for 9%

profile of v7, /device:TPU:0, one launch (start us, length us, event | category | flops | bytes accessed | tf_op | source)
XLA Modules:
  0.0 138.8 jit_solution(1267979867991805488)
XLA Ops:
  0.0 3.7 %range_compress_0.1 = (f32[16,3,1,16,128]{4,3,2,1,0:T(8,128)}, f32[16,3,1,16,128]{4,3,2,1,0:T(8,128)}) custom-call(f32[2,6,768,128]{3,2,1,0:T(8,128)} %bitcast.45, f32[2,1,12288]{2,1,0:T(1,128)} %slant_ref.3, bf16[3,128,128]{2,1,0:T(8,128)(2,1)} %constant.43.clone.a1_ref, bf16[512,256]{1,0:T(8,128)(2,1)} %constant.44.clone.b2_ref, ...), custom_call_target="tpu_custom_call" | custom-call | flops 1056964608 | bytes 1572864 | tf_op jit(solution)/shard_map/range_compress_0/pallas_call | solution.py:213
  3.7 4.0 %collective-permute-start = (f32[16,3,1,16,128]{4,3,2,1,0:T(8,128)}, f32[16,3,1,16,128]{4,3,2,1,0:T(8,128)S(1)}, u32[]{:S(2)}, u32[]{:S(2)}) collective-permute-start(f32[16,3,1,16,128]{4,3,2,1,0:T(8,128)} %get-tuple-element.24), channel_id=1, source_target_pairs={{0,8},{4,12},{8,0},{12,4},{1,9},{5,13},{9,1},{13,5},{2,10},{6,14},... | collective-permute-start | bytes 1179656 | tf_op jit(solution)/shard_map/ppermute | solution.py:547
  7.7 10.2 %range_compress_1.1 = f32[32,3,5,16,128]{4,3,2,1,0:T(8,128)} custom-call(f32[2,6,768,128]{3,2,1,0:T(8,128)} %bitcast.46, f32[2,1,12288]{2,1,0:T(1,128)} %slant_ref.3, bf16[3,128,128]{2,1,0:T(8,128)(2,1)} %constant.43.clone.a1_ref, bf16[512,256]{1,0:T(8,128)(2,1)} %constant.44.clone.b2_ref, bf16[3,128,128]{2,1,0:T(8,128)(2,1)} %constant.45.clone.a4_ref, ...), custom_call_target="tpu_custom_call" | custom-call | flops 5284823040 | bytes 7864320 | tf_op jit(solution)/shard_map/range_compress_1/pallas_call | solution.py:213
  17.9 3.9 %all-to-all-start = ((f32[32,3,5,16,128]{4,3,2,1,0:T(8,128)}), f32[32,3,5,16,128]{4,3,2,1,0:T(8,128)}, u32[]{:S(2)}, u32[]{:S(2)}) async-start(f32[32,3,5,16,128]{4,3,2,1,0:T(8,128)} %range_compress_1.1), calls=%async_computation | async-start | bytes 7864320 | tf_op jit(solution)/shard_map/all_to_all | solution.py:530
  21.9 1.1 dynamic-slice_bitcast_fusion
  23.0 1.7 %collective-permute-start.16 = (f32[768,384]{1,0:T(8,128)}, f32[768,384]{1,0:T(8,128)}, u32[]{:S(2)}, u32[]{:S(2)}) collective-permute-start(f32[768,384]{1,0:T(8,128)} %dynamic-slice_bitcast_fusion), channel_id=1, source_target_pairs={{0,16},{16,0},{1,17},{17,1},{2,18},{18,2},{3,19},{19,3},{4,20},{20... | collective-permute-start | bytes 3538952 | tf_op jit(solution)/shard_map/ppermute | solution.py:540
  26.0 0.8 copy-done.3
  26.8 2.0 %pair_halves.1 = (f32[2,3,16,128]{3,2,1,0:T(8,128)}, f32[2,3,16,128]{3,2,1,0:T(8,128)}, f32[2,3,16,128]{3,2,1,0:T(8,128)}, f32[2,3,16,128]{3,2,1,0:T(8,128)}, f3...) custom-call(f32[16,3,1,16,128]{4,3,2,1,0:T(8,128)} %get-tuple-elemen, ...), custom_call_target="tpu_custom_call" | custom-call | flops 999999995904 | bytes 393216 | tf_op jit(solution)/shard_map/pair_halves/pallas_call | solution.py:242
  28.8 0.8 bitcast_dynamic-update-slice_fusion.15
  29.6 1.5 %collective-permute-start.2 = (f32[2,3,16,128]{3,2,1,0:T(8,128)}, f32[2,3,16,128]{3,2,1,0:T(8,128)S(1)}, u32[]{:S(2)}, u32[]{:S(2)}) collective-permute-start(f32[2,3,16,128]{3,2,1,0:T(8,128)} %get-tuple-element.27), channel_id=1, source_target_pairs={{0,2},{1,3},{2,0},{3,1},{4,6},{5,7},{6,4},{7,5},{8,10},{9,11},{10,... | collective-permute-start | bytes 147464 | tf_op jit(solution)/shard_map/ppermute | solution.py:554
  31.4 1.5 %collective-permute-start.4 = (f32[2,3,16,128]{3,2,1,0:T(8,128)}, f32[2,3,16,128]{3,2,1,0:T(8,128)S(1)}, u32[]{:S(2)}, u32[]{:S(2)}) collective-permute-start(f32[2,3,16,128]{3,2,1,0:T(8,128)} %get-tuple-element.29), channel_id=1, source_target_pairs={{0,4},{1,5},{2,6},{3,7},{4,0},{5,1},{6,2},{7,3},{8,12},{9,13},{10,... | collective-permute-start | bytes 147464 | tf_op jit(solution)/shard_map/ppermute | solution.py:554
  33.1 17.7 %collective-permute-done.2 = f32[2,3,16,128]{3,2,1,0:T(8,128)S(1)} collective-permute-done((f32[2,3,16,128]{3,2,1,0:T(8,128)}, f32[2,3,16,128]{3,2,1,0:T(8,128)S(1)}, u32[]{:S(2)}, u32[]{:S(2)}) %collective-permute-start.2) | collective-permute-done | bytes 49184 | tf_op jit(solution)/shard_map/ppermute | solution.py:554
  51.0 1.4 %collective-permute-start.7 = (f32[2,3,16,128]{3,2,1,0:T(8,128)}, f32[2,3,16,128]{3,2,1,0:T(8,128)S(1)}, u32[]{:S(2)}, u32[]{:S(2)}) collective-permute-start(f32[2,3,16,128]{3,2,1,0:T(8,128)} %get-tuple-element.32), channel_id=1, source_target_pairs={{0,7},{1,6},{2,5},{3,4},{4,3},{5,2},{6,1},{7,0},{8,15},{9,14},{10,... | collective-permute-start | bytes 147464 | tf_op jit(solution)/shard_map/ppermute | solution.py:554
  52.4 35.7 %collective-permute-done.4 = f32[2,3,16,128]{3,2,1,0:T(8,128)S(1)} collective-permute-done((f32[2,3,16,128]{3,2,1,0:T(8,128)}, f32[2,3,16,128]{3,2,1,0:T(8,128)S(1)}, u32[]{:S(2)}, u32[]{:S(2)}) %collective-permute-start.4) | collective-permute-done | bytes 49184 | tf_op jit(solution)/shard_map/ppermute | solution.py:554
  88.1 1.6 %collective-permute-start.8 = (f32[2,3,16,128]{3,2,1,0:T(8,128)}, f32[2,3,16,128]{3,2,1,0:T(8,128)S(1)}, u32[]{:S(2)}, u32[]{:S(2)}) collective-permute-start(f32[2,3,16,128]{3,2,1,0:T(8,128)} %get-tuple-element.33), channel_id=1, source_target_pairs={{0,16},{1,17},{2,18},{3,19},{4,20},{5,21},{6,22},{7,23},{8,24},{9,... | collective-permute-start | bytes 147464 | tf_op jit(solution)/shard_map/ppermute | solution.py:554
  90.2 4.1 %collective-permute-start.10 = (f32[2,3,16,128]{3,2,1,0:T(8,128)}, f32[2,3,16,128]{3,2,1,0:T(8,128)S(1)}, u32[]{:S(2)}, u32[]{:S(2)}) collective-permute-start(f32[2,3,16,128]{3,2,1,0:T(8,128)} %get-tuple-element.35), channel_id=1, source_target_pairs={{0,18},{1,19},{2,16},{3,17},{4,22},{5,23},{6,20},{7,21},{8,26},{9,... | collective-permute-start | bytes 147464 | tf_op jit(solution)/shard_map/ppermute | solution.py:554
  94.5 3.9 %collective-permute-start.12 = (f32[2,3,16,128]{3,2,1,0:T(8,128)}, f32[2,3,16,128]{3,2,1,0:T(8,128)S(1)}, u32[]{:S(2)}, u32[]{:S(2)}) collective-permute-start(f32[2,3,16,128]{3,2,1,0:T(8,128)} %get-tuple-element.37), channel_id=1, source_target_pairs={{0,20},{1,21},{2,22},{3,23},{4,16},{5,17},{6,18},{7,19},{8,28},{9,... | collective-permute-start | bytes 147464 | tf_op jit(solution)/shard_map/ppermute | solution.py:554
  99.1 2.9 %collective-permute-start.14 = (f32[2,3,16,128]{3,2,1,0:T(8,128)}, f32[2,3,16,128]{3,2,1,0:T(8,128)S(1)}, u32[]{:S(2)}, u32[]{:S(2)}) collective-permute-start(f32[2,3,16,128]{3,2,1,0:T(8,128)} %get-tuple-element.39), channel_id=1, source_target_pairs={{0,22},{1,23},{2,20},{3,21},{4,18},{5,19},{6,16},{7,17},{8,30},{9,... | collective-permute-start | bytes 147464 | tf_op jit(solution)/shard_map/ppermute | solution.py:554
  101.9 4.1 %collective-permute-start.15 = (f32[2,3,16,128]{3,2,1,0:T(8,128)}, f32[2,3,16,128]{3,2,1,0:T(8,128)S(1)}, u32[]{:S(2)}, u32[]{:S(2)}) collective-permute-start(f32[2,3,16,128]{3,2,1,0:T(8,128)} %get-tuple-element.40), channel_id=1, source_target_pairs={{0,23},{1,22},{2,21},{3,20},{4,19},{5,18},{6,17},{7,16},{8,31},{9,... | collective-permute-start | bytes 147464 | tf_op jit(solution)/shard_map/ppermute | solution.py:554
  106.2 3.6 %collective-permute-done.15 = f32[2,3,16,128]{3,2,1,0:T(8,128)S(1)} collective-permute-done((f32[2,3,16,128]{3,2,1,0:T(8,128)}, f32[2,3,16,128]{3,2,1,0:T(8,128)S(1)}, u32[]{:S(2)}, u32[]{:S(2)}) %collective-permute-start.15) | collective-permute-done | bytes 49184 | tf_op jit(solution)/shard_map/ppermute | solution.py:554
  109.8 0.9 copy-done.1
  110.7 11.6 %azimuth_interferogram.1 = f32[32,3,4,128]{3,2,1,0:T(4,128)} custom-call(s32[2]{0:T(128)} %pad_add_fusion.me_ref, s32[2]{0:T(128)} %fusion.same_ref, f32[32,3,5,16,128]{4,3,2,1,0:T(8,128)} %all-to-all-done.x_ref, f32[16,2,3,16,128]{4,3,2,1,0:T(8,128)} %copy-done.1, f32[768,768]{1,0:T(8,128)} %bitcast.47, f32[768,384]{1,0:T(8,128)} %collective-permute-done.16.other_angle, ...), custom_call_target="tpu_custom_call" | custom-call | flops 3623878656 | bytes 11796480 | tf_op jit(solution)/shard_map/azimuth_interferogram/pallas_call | solution.py:406
  122.3 14.6 %all_to_all.10.in_ref = f32[32,3,4,128]{3,2,1,0:T(4,128)} all-to-all(f32[32,3,4,128]{3,2,1,0:T(4,128)} %azimuth_interferogram.1), channel_id=1, replica_groups=mesh['acq'=2,'high'=4,'low'=4] {'acq','low','high'}, dimensions={0} | all-to-all | bytes 393216 | tf_op jit(solution)/shard_map/all_to_all | solution.py:530
  136.9 1.9 %place_samples.1 = f32[32,1536]{1,0:T(8,128)} custom-call(f32[32,3,4,128]{3,2,1,0:T(4,128)} %all_to_all.10.in_ref), custom_call_target="tpu_custom_call" | custom-call | tf_op jit(solution)/shard_map/place_samples/pallas_call | solution.py:519
  (45 shorter events, 3.7 us)
Async XLA Ops:
  3.7 22.3 %collective-permute-start = (f32[16,3,1,16,128]{4,3,2,1,0:T(8,128)}, f32[16,3,1,16,128]{4,3,2,1,0:T(8,128)S(1)}, u32[]{:S(2)}, u32[]{:S(2)}) collective-permute-start(f32[16,3,1,16,128]{4,3,2,1,0:T(8,128)} %get-tuple-element.24), channel_id=1, source_target_pairs={{0,8},{4,12},{8,0},{12,4},{1,9},{5,13},{9,1},{13,5},{2,10},{6,14},... | collective-permute-start | bytes 1179656 | tf_op jit(solution)/shard_map/ppermute | solution.py:547
  17.9 4.0 %copy-start = (f32[1,768,768]{2,1,0:T(8,128)S(1)}, f32[1,768,768]{2,1,0:T(8,128)}, u32[]{:S(2)}) copy-start(f32[1,768,768]{2,1,0:T(8,128)} %param.17) | copy-start | bytes 7077892
  17.9 91.9 %all-to-all-start = ((f32[32,3,5,16,128]{4,3,2,1,0:T(8,128)}), f32[32,3,5,16,128]{4,3,2,1,0:T(8,128)}, u32[]{:S(2)}, u32[]{:S(2)}) async-start(f32[32,3,5,16,128]{4,3,2,1,0:T(8,128)} %range_compress_1.1), calls=%async_computation | async-start | bytes 7864320 | tf_op jit(solution)/shard_map/all_to_all | solution.py:530
  21.9 2.8 %copy-start.2 = (s32[2,2]{1,0:T(2,128)S(1)}, s32[2,2]{1,0:T(2,128)}, u32[]{:S(2)}) copy-start(s32[2,2]{1,0:T(2,128)} %param.18) | copy-start | bytes 52
  23.0 86.9 %collective-permute-start.16 = (f32[768,384]{1,0:T(8,128)}, f32[768,384]{1,0:T(8,128)}, u32[]{:S(2)}, u32[]{:S(2)}) collective-permute-start(f32[768,384]{1,0:T(8,128)} %dynamic-slice_bitcast_fusion), channel_id=1, source_target_pairs={{0,16},{16,0},{1,17},{17,1},{2,18},{18,2},{3,19},{19,3},{4,20},{20... | collective-permute-start | bytes 3538952 | tf_op jit(solution)/shard_map/ppermute | solution.py:540
  26.0 0.8 copy-start.3
  28.7 4.2 %collective-permute-start.1 = (f32[2,3,16,128]{3,2,1,0:T(8,128)}, f32[2,3,16,128]{3,2,1,0:T(8,128)S(1)}, u32[]{:S(2)}, u32[]{:S(2)}) collective-permute-start(f32[2,3,16,128]{3,2,1,0:T(8,128)} %get-tuple-element.26), channel_id=1, source_target_pairs={{0,1},{1,0},{2,3},{3,2},{4,5},{5,4},{6,7},{7,6},{8,9},{9,8},{10,11... | collective-permute-start | bytes 147464 | tf_op jit(solution)/shard_map/ppermute | solution.py:554
  29.6 21.2 %collective-permute-start.2 = (f32[2,3,16,128]{3,2,1,0:T(8,128)}, f32[2,3,16,128]{3,2,1,0:T(8,128)S(1)}, u32[]{:S(2)}, u32[]{:S(2)}) collective-permute-start(f32[2,3,16,128]{3,2,1,0:T(8,128)} %get-tuple-element.27), channel_id=1, source_target_pairs={{0,2},{1,3},{2,0},{3,1},{4,6},{5,7},{6,4},{7,5},{8,10},{9,11},{10,... | collective-permute-start | bytes 147464 | tf_op jit(solution)/shard_map/ppermute | solution.py:554
  31.1 20.0 %collective-permute-start.3 = (f32[2,3,16,128]{3,2,1,0:T(8,128)}, f32[2,3,16,128]{3,2,1,0:T(8,128)S(1)}, u32[]{:S(2)}, u32[]{:S(2)}) collective-permute-start(f32[2,3,16,128]{3,2,1,0:T(8,128)} %get-tuple-element.28), channel_id=1, source_target_pairs={{0,3},{1,2},{2,1},{3,0},{4,7},{5,6},{6,5},{7,4},{8,11},{9,10},{10,... | collective-permute-start | bytes 147464 | tf_op jit(solution)/shard_map/ppermute | solution.py:554
  31.4 56.7 %collective-permute-start.4 = (f32[2,3,16,128]{3,2,1,0:T(8,128)}, f32[2,3,16,128]{3,2,1,0:T(8,128)S(1)}, u32[]{:S(2)}, u32[]{:S(2)}) collective-permute-start(f32[2,3,16,128]{3,2,1,0:T(8,128)} %get-tuple-element.29), channel_id=1, source_target_pairs={{0,4},{1,5},{2,6},{3,7},{4,0},{5,1},{6,2},{7,3},{8,12},{9,13},{10,... | collective-permute-start | bytes 147464 | tf_op jit(solution)/shard_map/ppermute | solution.py:554
  32.9 56.8 %collective-permute-start.5 = (f32[2,3,16,128]{3,2,1,0:T(8,128)}, f32[2,3,16,128]{3,2,1,0:T(8,128)S(1)}, u32[]{:S(2)}, u32[]{:S(2)}) collective-permute-start(f32[2,3,16,128]{3,2,1,0:T(8,128)} %get-tuple-element.30), channel_id=1, source_target_pairs={{0,5},{1,4},{2,7},{3,6},{4,1},{5,0},{6,3},{7,2},{8,13},{9,12},{10,... | collective-permute-start | bytes 147464 | tf_op jit(solution)/shard_map/ppermute | solution.py:554
  50.8 39.4 %collective-permute-start.6 = (f32[2,3,16,128]{3,2,1,0:T(8,128)}, f32[2,3,16,128]{3,2,1,0:T(8,128)S(1)}, u32[]{:S(2)}, u32[]{:S(2)}) collective-permute-start(f32[2,3,16,128]{3,2,1,0:T(8,128)} %get-tuple-element.31), channel_id=1, source_target_pairs={{0,6},{1,7},{2,4},{3,5},{4,2},{5,3},{6,0},{7,1},{8,14},{9,15},{10,... | collective-permute-start | bytes 147464 | tf_op jit(solution)/shard_map/ppermute | solution.py:554
  51.0 43.3 %collective-permute-start.7 = (f32[2,3,16,128]{3,2,1,0:T(8,128)}, f32[2,3,16,128]{3,2,1,0:T(8,128)S(1)}, u32[]{:S(2)}, u32[]{:S(2)}) collective-permute-start(f32[2,3,16,128]{3,2,1,0:T(8,128)} %get-tuple-element.32), channel_id=1, source_target_pairs={{0,7},{1,6},{2,5},{3,4},{4,3},{5,2},{6,1},{7,0},{8,15},{9,14},{10,... | collective-permute-start | bytes 147464 | tf_op jit(solution)/shard_map/ppermute | solution.py:554
  88.1 6.3 %collective-permute-start.8 = (f32[2,3,16,128]{3,2,1,0:T(8,128)}, f32[2,3,16,128]{3,2,1,0:T(8,128)S(1)}, u32[]{:S(2)}, u32[]{:S(2)}) collective-permute-start(f32[2,3,16,128]{3,2,1,0:T(8,128)} %get-tuple-element.33), channel_id=1, source_target_pairs={{0,16},{1,17},{2,18},{3,19},{4,20},{5,21},{6,22},{7,23},{8,24},{9,... | collective-permute-start | bytes 147464 | tf_op jit(solution)/shard_map/ppermute | solution.py:554
  89.7 8.6 %collective-permute-start.9 = (f32[2,3,16,128]{3,2,1,0:T(8,128)}, f32[2,3,16,128]{3,2,1,0:T(8,128)S(1)}, u32[]{:S(2)}, u32[]{:S(2)}) collective-permute-start(f32[2,3,16,128]{3,2,1,0:T(8,128)} %get-tuple-element.34), channel_id=1, source_target_pairs={{0,17},{1,16},{2,19},{3,18},{4,21},{5,20},{6,23},{7,22},{8,25},{9,... | collective-permute-start | bytes 147464 | tf_op jit(solution)/shard_map/ppermute | solution.py:554
  90.2 8.8 %collective-permute-start.10 = (f32[2,3,16,128]{3,2,1,0:T(8,128)}, f32[2,3,16,128]{3,2,1,0:T(8,128)S(1)}, u32[]{:S(2)}, u32[]{:S(2)}) collective-permute-start(f32[2,3,16,128]{3,2,1,0:T(8,128)} %get-tuple-element.35), channel_id=1, source_target_pairs={{0,18},{1,19},{2,16},{3,17},{4,22},{5,23},{6,20},{7,21},{8,26},{9,... | collective-permute-start | bytes 147464 | tf_op jit(solution)/shard_map/ppermute | solution.py:554
  94.3 7.6 %collective-permute-start.11 = (f32[2,3,16,128]{3,2,1,0:T(8,128)}, f32[2,3,16,128]{3,2,1,0:T(8,128)S(1)}, u32[]{:S(2)}, u32[]{:S(2)}) collective-permute-start(f32[2,3,16,128]{3,2,1,0:T(8,128)} %get-tuple-element.36), channel_id=1, source_target_pairs={{0,19},{1,18},{2,17},{3,16},{4,23},{5,22},{6,21},{7,20},{8,27},{9,... | collective-permute-start | bytes 147464 | tf_op jit(solution)/shard_map/ppermute | solution.py:554
  94.5 11.6 %collective-permute-start.12 = (f32[2,3,16,128]{3,2,1,0:T(8,128)}, f32[2,3,16,128]{3,2,1,0:T(8,128)S(1)}, u32[]{:S(2)}, u32[]{:S(2)}) collective-permute-start(f32[2,3,16,128]{3,2,1,0:T(8,128)} %get-tuple-element.37), channel_id=1, source_target_pairs={{0,20},{1,21},{2,22},{3,23},{4,16},{5,17},{6,18},{7,19},{8,28},{9,... | collective-permute-start | bytes 147464 | tf_op jit(solution)/shard_map/ppermute | solution.py:554
  98.3 7.7 %collective-permute-start.13 = (f32[2,3,16,128]{3,2,1,0:T(8,128)}, f32[2,3,16,128]{3,2,1,0:T(8,128)S(1)}, u32[]{:S(2)}, u32[]{:S(2)}) collective-permute-start(f32[2,3,16,128]{3,2,1,0:T(8,128)} %get-tuple-element.38), channel_id=1, source_target_pairs={{0,21},{1,20},{2,23},{3,22},{4,17},{5,16},{6,19},{7,18},{8,29},{9,... | collective-permute-start | bytes 147464 | tf_op jit(solution)/shard_map/ppermute | solution.py:554
  99.1 7.1 %collective-permute-start.14 = (f32[2,3,16,128]{3,2,1,0:T(8,128)}, f32[2,3,16,128]{3,2,1,0:T(8,128)S(1)}, u32[]{:S(2)}, u32[]{:S(2)}) collective-permute-start(f32[2,3,16,128]{3,2,1,0:T(8,128)} %get-tuple-element.39), channel_id=1, source_target_pairs={{0,22},{1,23},{2,20},{3,21},{4,18},{5,19},{6,16},{7,17},{8,30},{9,... | collective-permute-start | bytes 147464 | tf_op jit(solution)/shard_map/ppermute | solution.py:554
  101.9 7.9 %collective-permute-start.15 = (f32[2,3,16,128]{3,2,1,0:T(8,128)}, f32[2,3,16,128]{3,2,1,0:T(8,128)S(1)}, u32[]{:S(2)}, u32[]{:S(2)}) collective-permute-start(f32[2,3,16,128]{3,2,1,0:T(8,128)} %get-tuple-element.40), channel_id=1, source_target_pairs={{0,23},{1,22},{2,21},{3,20},{4,19},{5,18},{6,17},{7,16},{8,31},{9,... | collective-permute-start | bytes 147464 | tf_op jit(solution)/shard_map/ppermute | solution.py:554
  109.8 0.9 copy-start.1

commit v8 on v4

--- a/solution.py
+++ b/solution.py
@@ -108,10 +108,6 @@
     twiddle = np.stack([ct, st]).astype(np.float32)
     b2 = np.concatenate(high_low(b2))
     return np.stack(a1), b2, np.stack(a4), twiddle
-
-
-def spot(tile, low):
-    return lax.rem(tile, low) * FAR + lax.div(tile, low)
 
 
 def range_kernel(outer, early, x_ref, slant_ref, a1_ref, b2_ref, a4_ref, t_ref, *rest):
@@ -190,7 +186,7 @@
     for k, out in enumerate(outs):
         for s in range(2 * near):
             tile = jnp.bitwise_xor(place, s % near + k * near)
-            dest = jnp.bitwise_xor(acq, s // near) * 2 * near + spot(tile, 2 * near // FAR)
+            dest = jnp.bitwise_xor(acq, s // near) * 2 * near + tile
             value = turned[pl.ds(pl.multiple_of(dest * rows, SUB), rows), :]
             out[s, :, 0] = value.reshape(out.shape[1], out.shape[3], LANES)
 
@@ -535,8 +531,8 @@
     theirs = lax.dynamic_slice_in_dim(angle, (1 - acq) * (columns // 2), columns // 2, 1)
     other_angle = lax.ppermute(theirs, "acq", [(0, 1), (1, 0)])
     low = lax.axis_size("low")
-    order = [h * low + k for k in range(low) for h in range(tiles // low)]
-    axes = ("acq", "low", "high")
+    order = list(range(tiles))
+    axes = ("acq", "high", "low")
     tile = lax.axis_index("high") * low + lax.axis_index("low")
     me = jnp.stack([acq, tile]).astype(jnp.int32)
     kept, given = range_call(echo, slant, 0, 1, order, 2, early=True)

time: 139 us -> 139 us (level)
  blocking collectives: 14.6 us -> 12.2 us
  waiting for transfers between devices: 57.9 us -> 59.4 us
    all_to_all x1, blocking collectives: 14.6 us -> 12.2 us  [turn(): return lax.all_to_all(array, axes, split_axis=0, concat_axis=0, tiled=True)]
    ppermute x15, waiting for transfers between devices: 57.9 us -> 59.4 us  [joint(): lax.ppermute(early[s], ('acq', 'high', 'low'), [(i, i ^ flip) for i in ra...]
  transfers between devices with their start and end apart: 18 -> 18, of which waited for: 6 -> 8; matrix products, arithmetic and copies ran while one was open for 2% -> 2% of each run, Pallas kernels for 9% -> 9%
where the time goes in v8:
time: 139 us
  waiting for transfers between devices  59.4 us (43%)
  starting transfers between devices  32.6 us (23%)
  Pallas kernels  29.3 us (21%)
  blocking collectives  12.2 us (9%)
  local copies, waits for them, and re-layouts  3.6 us (3%)
    ppermute x15, waiting for transfers between devices, joint(): lax.ppermute(early[s], ('acq', 'high', 'low'), [(i, i ^ flip) for i in ra...  59.4 us
    ppermute x15, starting transfers between devices, joint(): lax.ppermute(early[s], ('acq', 'high', 'low'), [(i, i ^ flip) for i in ra...  22.9 us
    pallas_call x2, Pallas kernels, range_call(): pl.pallas_call(functools.partial(range_kernel, outer, early), grid=(steps...  13.9 us
    all_to_all x1, blocking collectives, turn(): return lax.all_to_all(array, axes, split_axis=0, concat_axis=0, tiled=True)  12.2 us
    pallas_call x1, Pallas kernels, joint_call(): pl.pallas_call(functools.partial(joint_kernel, order, rounds), grid_spec=...  11.6 us
    ppermute x1, starting transfers between devices, joint(): came = lax.ppermute(given, 'high', [(h, h ^ FAR // 2) for h in range(FAR)])  4.04 us
    all_to_all x1, starting transfers between devices, turn(): return lax.all_to_all(array, axes, split_axis=0, concat_axis=0, tiled=True)  3.94 us
  transfers between devices with their start and end apart: 18, of which 8 were waited for; matrix products, arithmetic and copies ran while one was open for 2% of the time, Pallas kernels for 9%

profile of v8, /device:TPU:0, one launch (start us, length us, event | category | flops | bytes accessed | tf_op | source)
XLA Modules:
  0.0 138.6 jit_solution(14104669249707766143)
XLA Ops:
  0.0 3.7 %range_compress_0.1 = (f32[16,3,1,16,128]{4,3,2,1,0:T(8,128)}, f32[16,3,1,16,128]{4,3,2,1,0:T(8,128)}) custom-call(f32[2,6,768,128]{3,2,1,0:T(8,128)} %bitcast.45, f32[2,1,12288]{2,1,0:T(1,128)} %slant_ref.3, bf16[3,128,128]{2,1,0:T(8,128)(2,1)} %constant.43.clone.a1_ref, bf16[512,256]{1,0:T(8,128)(2,1)} %constant.44.clone.b2_ref, ...), custom_call_target="tpu_custom_call" | custom-call | flops 1056964608 | bytes 1572864 | tf_op jit(solution)/shard_map/range_compress_0/pallas_call | solution.py:205
  3.7 4.0 %collective-permute-start = (f32[16,3,1,16,128]{4,3,2,1,0:T(8,128)}, f32[16,3,1,16,128]{4,3,2,1,0:T(8,128)S(1)}, u32[]{:S(2)}, u32[]{:S(2)}) collective-permute-start(f32[16,3,1,16,128]{4,3,2,1,0:T(8,128)} %get-tuple-element.24), channel_id=1, source_target_pairs={{0,8},{4,12},{8,0},{12,4},{1,9},{5,13},{9,1},{13,5},{2,10},{6,14},... | collective-permute-start | bytes 1179656 | tf_op jit(solution)/shard_map/ppermute | solution.py:539
  7.7 10.2 %range_compress_1.1 = f32[32,3,5,16,128]{4,3,2,1,0:T(8,128)} custom-call(f32[2,6,768,128]{3,2,1,0:T(8,128)} %bitcast.46, f32[2,1,12288]{2,1,0:T(1,128)} %slant_ref.3, bf16[3,128,128]{2,1,0:T(8,128)(2,1)} %constant.43.clone.a1_ref, bf16[512,256]{1,0:T(8,128)(2,1)} %constant.44.clone.b2_ref, bf16[3,128,128]{2,1,0:T(8,128)(2,1)} %constant.45.clone.a4_ref, ...), custom_call_target="tpu_custom_call" | custom-call | flops 5284823040 | bytes 7864320 | tf_op jit(solution)/shard_map/range_compress_1/pallas_call | solution.py:205
  17.9 3.9 %all-to-all-start = ((f32[32,3,5,16,128]{4,3,2,1,0:T(8,128)}), f32[32,3,5,16,128]{4,3,2,1,0:T(8,128)}, u32[]{:S(2)}, u32[]{:S(2)}) async-start(f32[32,3,5,16,128]{4,3,2,1,0:T(8,128)} %range_compress_1.1), calls=%async_computation | async-start | bytes 7864320 | tf_op jit(solution)/shard_map/all_to_all | solution.py:522
  21.9 1.1 dynamic-slice_bitcast_fusion
  23.0 1.7 %collective-permute-start.16 = (f32[768,384]{1,0:T(8,128)}, f32[768,384]{1,0:T(8,128)}, u32[]{:S(2)}, u32[]{:S(2)}) collective-permute-start(f32[768,384]{1,0:T(8,128)} %dynamic-slice_bitcast_fusion), channel_id=1, source_target_pairs={{0,16},{16,0},{1,17},{17,1},{2,18},{18,2},{3,19},{19,3},{4,20},{20... | collective-permute-start | bytes 3538952 | tf_op jit(solution)/shard_map/ppermute | solution.py:532
  26.8 2.0 %pair_halves.1 = (f32[2,3,16,128]{3,2,1,0:T(8,128)}, f32[2,3,16,128]{3,2,1,0:T(8,128)}, f32[2,3,16,128]{3,2,1,0:T(8,128)}, f32[2,3,16,128]{3,2,1,0:T(8,128)}, f3...) custom-call(f32[16,3,1,16,128]{4,3,2,1,0:T(8,128)} %get-tuple-elemen, ...), custom_call_target="tpu_custom_call" | custom-call | flops 999999995904 | bytes 393216 | tf_op jit(solution)/shard_map/pair_halves/pallas_call | solution.py:234
  29.6 1.5 %collective-permute-start.2 = (f32[2,3,16,128]{3,2,1,0:T(8,128)}, f32[2,3,16,128]{3,2,1,0:T(8,128)S(1)}, u32[]{:S(2)}, u32[]{:S(2)}) collective-permute-start(f32[2,3,16,128]{3,2,1,0:T(8,128)} %get-tuple-element.27), channel_id=1, source_target_pairs={{0,2},{1,3},{2,0},{3,1},{4,6},{5,7},{6,4},{7,5},{8,10},{9,11},{10,... | collective-permute-start | bytes 147464 | tf_op jit(solution)/shard_map/ppermute | solution.py:546
  31.4 9.4 %collective-permute-start.4 = (f32[2,3,16,128]{3,2,1,0:T(8,128)}, f32[2,3,16,128]{3,2,1,0:T(8,128)S(1)}, u32[]{:S(2)}, u32[]{:S(2)}) collective-permute-start(f32[2,3,16,128]{3,2,1,0:T(8,128)} %get-tuple-element.29), channel_id=1, source_target_pairs={{0,4},{1,5},{2,6},{3,7},{4,0},{5,1},{6,2},{7,3},{8,12},{9,13},{10,... | collective-permute-start | bytes 147464 | tf_op jit(solution)/shard_map/ppermute | solution.py:546
  40.8 7.3 %collective-permute-done.2 = f32[2,3,16,128]{3,2,1,0:T(8,128)S(1)} collective-permute-done((f32[2,3,16,128]{3,2,1,0:T(8,128)}, f32[2,3,16,128]{3,2,1,0:T(8,128)S(1)}, u32[]{:S(2)}, u32[]{:S(2)}) %collective-permute-start.2) | collective-permute-done | bytes 49184 | tf_op jit(solution)/shard_map/ppermute | solution.py:546
  48.1 1.5 %collective-permute-done.3 = f32[2,3,16,128]{3,2,1,0:T(8,128)S(1)} collective-permute-done((f32[2,3,16,128]{3,2,1,0:T(8,128)}, f32[2,3,16,128]{3,2,1,0:T(8,128)S(1)}, u32[]{:S(2)}, u32[]{:S(2)}) %collective-permute-start.3) | collective-permute-done | bytes 49184 | tf_op jit(solution)/shard_map/ppermute | solution.py:546
  49.7 1.1 collective-permute-start.7
  50.8 37.9 %collective-permute-done.4 = f32[2,3,16,128]{3,2,1,0:T(8,128)S(1)} collective-permute-done((f32[2,3,16,128]{3,2,1,0:T(8,128)}, f32[2,3,16,128]{3,2,1,0:T(8,128)S(1)}, u32[]{:S(2)}, u32[]{:S(2)}) %collective-permute-start.4) | collective-permute-done | bytes 49184 | tf_op jit(solution)/shard_map/ppermute | solution.py:546
  88.7 1.9 %collective-permute-start.8 = (f32[2,3,16,128]{3,2,1,0:T(8,128)}, f32[2,3,16,128]{3,2,1,0:T(8,128)S(1)}, u32[]{:S(2)}, u32[]{:S(2)}) collective-permute-start(f32[2,3,16,128]{3,2,1,0:T(8,128)} %get-tuple-element.33), channel_id=1, source_target_pairs={{0,16},{1,17},{2,18},{3,19},{4,20},{5,21},{6,22},{7,23},{8,24},{9,... | collective-permute-start | bytes 147464 | tf_op jit(solution)/shard_map/ppermute | solution.py:546
  90.8 1.9 %collective-permute-start.10 = (f32[2,3,16,128]{3,2,1,0:T(8,128)}, f32[2,3,16,128]{3,2,1,0:T(8,128)S(1)}, u32[]{:S(2)}, u32[]{:S(2)}) collective-permute-start(f32[2,3,16,128]{3,2,1,0:T(8,128)} %get-tuple-element.35), channel_id=1, source_target_pairs={{0,18},{1,19},{2,16},{3,17},{4,22},{5,23},{6,20},{7,21},{8,26},{9,... | collective-permute-start | bytes 147464 | tf_op jit(solution)/shard_map/ppermute | solution.py:546
  92.7 1.5 %collective-permute-start.11 = (f32[2,3,16,128]{3,2,1,0:T(8,128)}, f32[2,3,16,128]{3,2,1,0:T(8,128)S(1)}, u32[]{:S(2)}, u32[]{:S(2)}) collective-permute-start(f32[2,3,16,128]{3,2,1,0:T(8,128)} %get-tuple-element.36), channel_id=1, source_target_pairs={{0,19},{1,18},{2,17},{3,16},{4,23},{5,22},{6,21},{7,20},{8,27},{9,... | collective-permute-start | bytes 147464 | tf_op jit(solution)/shard_map/ppermute | solution.py:546
  94.2 2.7 %collective-permute-done.8 = f32[2,3,16,128]{3,2,1,0:T(8,128)S(1)} collective-permute-done((f32[2,3,16,128]{3,2,1,0:T(8,128)}, f32[2,3,16,128]{3,2,1,0:T(8,128)S(1)}, u32[]{:S(2)}, u32[]{:S(2)}) %collective-permute-start.8) | collective-permute-done | bytes 49184 | tf_op jit(solution)/shard_map/ppermute | solution.py:546
  97.6 1.2 collective-permute-done.9
  98.8 3.8 %collective-permute-start.13 = (f32[2,3,16,128]{3,2,1,0:T(8,128)}, f32[2,3,16,128]{3,2,1,0:T(8,128)S(1)}, u32[]{:S(2)}, u32[]{:S(2)}) collective-permute-start(f32[2,3,16,128]{3,2,1,0:T(8,128)} %get-tuple-element.38), channel_id=1, source_target_pairs={{0,21},{1,20},{2,23},{3,22},{4,17},{5,16},{6,19},{7,18},{8,29},{9,... | collective-permute-start | bytes 147464 | tf_op jit(solution)/shard_map/ppermute | solution.py:546
  103.3 1.5 %collective-permute-done.13 = f32[2,3,16,128]{3,2,1,0:T(8,128)S(1)} collective-permute-done((f32[2,3,16,128]{3,2,1,0:T(8,128)}, f32[2,3,16,128]{3,2,1,0:T(8,128)S(1)}, u32[]{:S(2)}, u32[]{:S(2)}) %collective-permute-start.13) | collective-permute-done | bytes 49184 | tf_op jit(solution)/shard_map/ppermute | solution.py:546
  104.8 7.1 %collective-permute-done.14 = f32[2,3,16,128]{3,2,1,0:T(8,128)S(1)} collective-permute-done((f32[2,3,16,128]{3,2,1,0:T(8,128)}, f32[2,3,16,128]{3,2,1,0:T(8,128)S(1)}, u32[]{:S(2)}, u32[]{:S(2)}) %collective-permute-start.14) | collective-permute-done | bytes 49184 | tf_op jit(solution)/shard_map/ppermute | solution.py:546
  112.9 11.6 %azimuth_interferogram.1 = f32[32,3,4,128]{3,2,1,0:T(4,128)} custom-call(s32[2]{0:T(128)} %pad_add_fusion.me_ref, s32[2]{0:T(128)} %fusion.same_ref, f32[32,3,5,16,128]{4,3,2,1,0:T(8,128)} %all-to-all-done.x_ref, f32[16,2,3,16,128]{4,3,2,1,0:T(8,128)} %copy-done.1, f32[768,768]{1,0:T(8,128)} %bitcast.47, f32[768,384]{1,0:T(8,128)} %collective-permute-done.16.other_angle, ...), custom_call_target="tpu_custom_call" | custom-call | flops 3623878656 | bytes 11796480 | tf_op jit(solution)/shard_map/azimuth_interferogram/pallas_call | solution.py:398
  124.5 12.2 %all_to_all.10.in_ref = f32[32,3,4,128]{3,2,1,0:T(4,128)} all-to-all(f32[32,3,4,128]{3,2,1,0:T(4,128)} %azimuth_interferogram.1), channel_id=1, replica_groups=mesh['acq'=2,'high'=4,'low'=4] {'acq','high','low'}, dimensions={0} | all-to-all | bytes 393216 | tf_op jit(solution)/shard_map/all_to_all | solution.py:522
  136.7 1.9 %place_samples.1 = f32[32,1536]{1,0:T(8,128)} custom-call(f32[32,3,4,128]{3,2,1,0:T(4,128)} %all_to_all.10.in_ref), custom_call_target="tpu_custom_call" | custom-call | tf_op jit(solution)/shard_map/place_samples/pallas_call | solution.py:511
  (45 shorter events, 5.9 us)
Async XLA Ops:
  3.7 22.3 %collective-permute-start = (f32[16,3,1,16,128]{4,3,2,1,0:T(8,128)}, f32[16,3,1,16,128]{4,3,2,1,0:T(8,128)S(1)}, u32[]{:S(2)}, u32[]{:S(2)}) collective-permute-start(f32[16,3,1,16,128]{4,3,2,1,0:T(8,128)} %get-tuple-element.24), channel_id=1, source_target_pairs={{0,8},{4,12},{8,0},{12,4},{1,9},{5,13},{9,1},{13,5},{2,10},{6,14},... | collective-permute-start | bytes 1179656 | tf_op jit(solution)/shard_map/ppermute | solution.py:539
  17.9 4.0 %copy-start = (f32[1,768,768]{2,1,0:T(8,128)S(1)}, f32[1,768,768]{2,1,0:T(8,128)}, u32[]{:S(2)}) copy-start(f32[1,768,768]{2,1,0:T(8,128)} %param.17) | copy-start | bytes 7077892
  17.9 94.1 %all-to-all-start = ((f32[32,3,5,16,128]{4,3,2,1,0:T(8,128)}), f32[32,3,5,16,128]{4,3,2,1,0:T(8,128)}, u32[]{:S(2)}, u32[]{:S(2)}) async-start(f32[32,3,5,16,128]{4,3,2,1,0:T(8,128)} %range_compress_1.1), calls=%async_computation | async-start | bytes 7864320 | tf_op jit(solution)/shard_map/all_to_all | solution.py:522
  21.9 2.8 %copy-start.2 = (s32[2,2]{1,0:T(2,128)S(1)}, s32[2,2]{1,0:T(2,128)}, u32[]{:S(2)}) copy-start(s32[2,2]{1,0:T(2,128)} %param.18) | copy-start | bytes 52
  23.0 89.0 %collective-permute-start.16 = (f32[768,384]{1,0:T(8,128)}, f32[768,384]{1,0:T(8,128)}, u32[]{:S(2)}, u32[]{:S(2)}) collective-permute-start(f32[768,384]{1,0:T(8,128)} %dynamic-slice_bitcast_fusion), channel_id=1, source_target_pairs={{0,16},{16,0},{1,17},{17,1},{2,18},{18,2},{3,19},{19,3},{4,20},{20... | collective-permute-start | bytes 3538952 | tf_op jit(solution)/shard_map/ppermute | solution.py:532
  26.0 0.8 copy-start.3
  28.7 12.1 %collective-permute-start.1 = (f32[2,3,16,128]{3,2,1,0:T(8,128)}, f32[2,3,16,128]{3,2,1,0:T(8,128)S(1)}, u32[]{:S(2)}, u32[]{:S(2)}) collective-permute-start(f32[2,3,16,128]{3,2,1,0:T(8,128)} %get-tuple-element.26), channel_id=1, source_target_pairs={{0,1},{1,0},{2,3},{3,2},{4,5},{5,4},{6,7},{7,6},{8,9},{9,8},{10,11... | collective-permute-start | bytes 147464 | tf_op jit(solution)/shard_map/ppermute | solution.py:546
  29.6 18.5 %collective-permute-start.2 = (f32[2,3,16,128]{3,2,1,0:T(8,128)}, f32[2,3,16,128]{3,2,1,0:T(8,128)S(1)}, u32[]{:S(2)}, u32[]{:S(2)}) collective-permute-start(f32[2,3,16,128]{3,2,1,0:T(8,128)} %get-tuple-element.27), channel_id=1, source_target_pairs={{0,2},{1,3},{2,0},{3,1},{4,6},{5,7},{6,4},{7,5},{8,10},{9,11},{10,... | collective-permute-start | bytes 147464 | tf_op jit(solution)/shard_map/ppermute | solution.py:546
  31.1 18.6 %collective-permute-start.3 = (f32[2,3,16,128]{3,2,1,0:T(8,128)}, f32[2,3,16,128]{3,2,1,0:T(8,128)S(1)}, u32[]{:S(2)}, u32[]{:S(2)}) collective-permute-start(f32[2,3,16,128]{3,2,1,0:T(8,128)} %get-tuple-element.28), channel_id=1, source_target_pairs={{0,3},{1,2},{2,1},{3,0},{4,7},{5,6},{6,5},{7,4},{8,11},{9,10},{10,... | collective-permute-start | bytes 147464 | tf_op jit(solution)/shard_map/ppermute | solution.py:546
  31.4 57.3 %collective-permute-start.4 = (f32[2,3,16,128]{3,2,1,0:T(8,128)}, f32[2,3,16,128]{3,2,1,0:T(8,128)S(1)}, u32[]{:S(2)}, u32[]{:S(2)}) collective-permute-start(f32[2,3,16,128]{3,2,1,0:T(8,128)} %get-tuple-element.29), channel_id=1, source_target_pairs={{0,4},{1,5},{2,6},{3,7},{4,0},{5,1},{6,2},{7,3},{8,12},{9,13},{10,... | collective-permute-start | bytes 147464 | tf_op jit(solution)/shard_map/ppermute | solution.py:546
  40.8 49.8 %collective-permute-start.5 = (f32[2,3,16,128]{3,2,1,0:T(8,128)}, f32[2,3,16,128]{3,2,1,0:T(8,128)S(1)}, u32[]{:S(2)}, u32[]{:S(2)}) collective-permute-start(f32[2,3,16,128]{3,2,1,0:T(8,128)} %get-tuple-element.30), channel_id=1, source_target_pairs={{0,5},{1,4},{2,7},{3,6},{4,1},{5,0},{6,3},{7,2},{8,13},{9,12},{10,... | collective-permute-start | bytes 147464 | tf_op jit(solution)/shard_map/ppermute | solution.py:546
  48.1 42.7 %collective-permute-start.6 = (f32[2,3,16,128]{3,2,1,0:T(8,128)}, f32[2,3,16,128]{3,2,1,0:T(8,128)S(1)}, u32[]{:S(2)}, u32[]{:S(2)}) collective-permute-start(f32[2,3,16,128]{3,2,1,0:T(8,128)} %get-tuple-element.31), channel_id=1, source_target_pairs={{0,6},{1,7},{2,4},{3,5},{4,2},{5,3},{6,0},{7,1},{8,14},{9,15},{10,... | collective-permute-start | bytes 147464 | tf_op jit(solution)/shard_map/ppermute | solution.py:546
  49.7 43.0 %collective-permute-start.7 = (f32[2,3,16,128]{3,2,1,0:T(8,128)}, f32[2,3,16,128]{3,2,1,0:T(8,128)S(1)}, u32[]{:S(2)}, u32[]{:S(2)}) collective-permute-start(f32[2,3,16,128]{3,2,1,0:T(8,128)} %get-tuple-element.32), channel_id=1, source_target_pairs={{0,7},{1,6},{2,5},{3,4},{4,3},{5,2},{6,1},{7,0},{8,15},{9,14},{10,... | collective-permute-start | bytes 147464 | tf_op jit(solution)/shard_map/ppermute | solution.py:546
  88.7 8.2 %collective-permute-start.8 = (f32[2,3,16,128]{3,2,1,0:T(8,128)}, f32[2,3,16,128]{3,2,1,0:T(8,128)S(1)}, u32[]{:S(2)}, u32[]{:S(2)}) collective-permute-start(f32[2,3,16,128]{3,2,1,0:T(8,128)} %get-tuple-element.33), channel_id=1, source_target_pairs={{0,16},{1,17},{2,18},{3,19},{4,20},{5,21},{6,22},{7,23},{8,24},{9,... | collective-permute-start | bytes 147464 | tf_op jit(solution)/shard_map/ppermute | solution.py:546
  90.6 8.2 %collective-permute-start.9 = (f32[2,3,16,128]{3,2,1,0:T(8,128)}, f32[2,3,16,128]{3,2,1,0:T(8,128)S(1)}, u32[]{:S(2)}, u32[]{:S(2)}) collective-permute-start(f32[2,3,16,128]{3,2,1,0:T(8,128)} %get-tuple-element.34), channel_id=1, source_target_pairs={{0,17},{1,16},{2,19},{3,18},{4,21},{5,20},{6,23},{7,22},{8,25},{9,... | collective-permute-start | bytes 147464 | tf_op jit(solution)/shard_map/ppermute | solution.py:546
  90.8 11.8 %collective-permute-start.10 = (f32[2,3,16,128]{3,2,1,0:T(8,128)}, f32[2,3,16,128]{3,2,1,0:T(8,128)S(1)}, u32[]{:S(2)}, u32[]{:S(2)}) collective-permute-start(f32[2,3,16,128]{3,2,1,0:T(8,128)} %get-tuple-element.35), channel_id=1, source_target_pairs={{0,18},{1,19},{2,16},{3,17},{4,22},{5,23},{6,20},{7,21},{8,26},{9,... | collective-permute-start | bytes 147464 | tf_op jit(solution)/shard_map/ppermute | solution.py:546
  92.7 10.0 %collective-permute-start.11 = (f32[2,3,16,128]{3,2,1,0:T(8,128)}, f32[2,3,16,128]{3,2,1,0:T(8,128)S(1)}, u32[]{:S(2)}, u32[]{:S(2)}) collective-permute-start(f32[2,3,16,128]{3,2,1,0:T(8,128)} %get-tuple-element.36), channel_id=1, source_target_pairs={{0,19},{1,18},{2,17},{3,16},{4,23},{5,22},{6,21},{7,20},{8,27},{9,... | collective-permute-start | bytes 147464 | tf_op jit(solution)/shard_map/ppermute | solution.py:546
  96.9 6.4 %collective-permute-start.12 = (f32[2,3,16,128]{3,2,1,0:T(8,128)}, f32[2,3,16,128]{3,2,1,0:T(8,128)S(1)}, u32[]{:S(2)}, u32[]{:S(2)}) collective-permute-start(f32[2,3,16,128]{3,2,1,0:T(8,128)} %get-tuple-element.37), channel_id=1, source_target_pairs={{0,20},{1,21},{2,22},{3,23},{4,16},{5,17},{6,18},{7,19},{8,28},{9,... | collective-permute-start | bytes 147464 | tf_op jit(solution)/shard_map/ppermute | solution.py:546
  98.8 6.0 %collective-permute-start.13 = (f32[2,3,16,128]{3,2,1,0:T(8,128)}, f32[2,3,16,128]{3,2,1,0:T(8,128)S(1)}, u32[]{:S(2)}, u32[]{:S(2)}) collective-permute-start(f32[2,3,16,128]{3,2,1,0:T(8,128)} %get-tuple-element.38), channel_id=1, source_target_pairs={{0,21},{1,20},{2,23},{3,22},{4,17},{5,16},{6,19},{7,18},{8,29},{9,... | collective-permute-start | bytes 147464 | tf_op jit(solution)/shard_map/ppermute | solution.py:546
  102.6 9.4 %collective-permute-start.14 = (f32[2,3,16,128]{3,2,1,0:T(8,128)}, f32[2,3,16,128]{3,2,1,0:T(8,128)S(1)}, u32[]{:S(2)}, u32[]{:S(2)}) collective-permute-start(f32[2,3,16,128]{3,2,1,0:T(8,128)} %get-tuple-element.39), channel_id=1, source_target_pairs={{0,22},{1,23},{2,20},{3,21},{4,18},{5,19},{6,16},{7,17},{8,30},{9,... | collective-permute-start | bytes 147464 | tf_op jit(solution)/shard_map/ppermute | solution.py:546
  102.7 9.3 %collective-permute-start.15 = (f32[2,3,16,128]{3,2,1,0:T(8,128)}, f32[2,3,16,128]{3,2,1,0:T(8,128)S(1)}, u32[]{:S(2)}, u32[]{:S(2)}) collective-permute-start(f32[2,3,16,128]{3,2,1,0:T(8,128)} %get-tuple-element.40), channel_id=1, source_target_pairs={{0,23},{1,22},{2,21},{3,20},{4,19},{5,18},{6,17},{7,16},{8,31},{9,... | collective-permute-start | bytes 147464 | tf_op jit(solution)/shard_map/ppermute | solution.py:546
  112.0 0.9 copy-start.1

commit v9 on v8

--- a/solution.py
+++ b/solution.py
@@ -541,7 +541,7 @@
     array = turn(sent, axes)
     early = list(pair_call(kept, came))
     near = tiles // 2
-    for s in range(1, tiles):
+    for s in sorted(range(1, tiles), key=lambda s: (s % near) // FAR):
         flip = s // near * tiles + s % near
         early[s] = lax.ppermute(early[s], ("acq", "high", "low"), [(i, i ^ flip) for i in range(2 * tiles)])
     early = jnp.stack(early)

time: 139 us -> 139 us (level)
  no operation moved by 1% of the time
where the time goes in v9:
time: 139 us
  waiting for transfers between devices  59.4 us (43%)
  starting transfers between devices  32.6 us (23%)
  Pallas kernels  29.3 us (21%)
  blocking collectives  12.2 us (9%)
  local copies, waits for them, and re-layouts  3.6 us (3%)
    ppermute x15, waiting for transfers between devices, joint(): lax.ppermute(early[s], ('acq', 'high', 'low'), [(i, i ^ flip) for i in ra...  59.4 us
    ppermute x15, starting transfers between devices, joint(): lax.ppermute(early[s], ('acq', 'high', 'low'), [(i, i ^ flip) for i in ra...  22.9 us
    pallas_call x2, Pallas kernels, range_call(): pl.pallas_call(functools.partial(range_kernel, outer, early), grid=(steps...  13.9 us
    all_to_all x1, blocking collectives, turn(): return lax.all_to_all(array, axes, split_axis=0, concat_axis=0, tiled=True)  12.2 us
    pallas_call x1, Pallas kernels, joint_call(): pl.pallas_call(functools.partial(joint_kernel, order, rounds), grid_spec=...  11.6 us
    ppermute x1, starting transfers between devices, joint(): came = lax.ppermute(given, 'high', [(h, h ^ FAR // 2) for h in range(FAR)])  4.04 us
    all_to_all x1, starting transfers between devices, turn(): return lax.all_to_all(array, axes, split_axis=0, concat_axis=0, tiled=True)  3.94 us
  transfers between devices with their start and end apart: 18, of which 8 were waited for; matrix products, arithmetic and copies ran while one was open for 2% of the time, Pallas kernels for 9%

profile of v9, /device:TPU:0, one launch (start us, length us, event | category | flops | bytes accessed | tf_op | source)
XLA Modules:
  0.0 138.6 jit_solution(14104669249707766143)
XLA Ops:
  0.0 3.7 %range_compress_0.1 = (f32[16,3,1,16,128]{4,3,2,1,0:T(8,128)}, f32[16,3,1,16,128]{4,3,2,1,0:T(8,128)}) custom-call(f32[2,6,768,128]{3,2,1,0:T(8,128)} %bitcast.45, f32[2,1,12288]{2,1,0:T(1,128)} %slant_ref.3, bf16[3,128,128]{2,1,0:T(8,128)(2,1)} %constant.43.clone.a1_ref, bf16[512,256]{1,0:T(8,128)(2,1)} %constant.44.clone.b2_ref, ...), custom_call_target="tpu_custom_call" | custom-call | flops 1056964608 | bytes 1572864 | tf_op jit(solution)/shard_map/range_compress_0/pallas_call | solution.py:205
  3.7 4.0 %collective-permute-start = (f32[16,3,1,16,128]{4,3,2,1,0:T(8,128)}, f32[16,3,1,16,128]{4,3,2,1,0:T(8,128)S(1)}, u32[]{:S(2)}, u32[]{:S(2)}) collective-permute-start(f32[16,3,1,16,128]{4,3,2,1,0:T(8,128)} %get-tuple-element.24), channel_id=1, source_target_pairs={{0,8},{4,12},{8,0},{12,4},{1,9},{5,13},{9,1},{13,5},{2,10},{6,14},... | collective-permute-start | bytes 1179656 | tf_op jit(solution)/shard_map/ppermute | solution.py:539
  7.7 10.2 %range_compress_1.1 = f32[32,3,5,16,128]{4,3,2,1,0:T(8,128)} custom-call(f32[2,6,768,128]{3,2,1,0:T(8,128)} %bitcast.46, f32[2,1,12288]{2,1,0:T(1,128)} %slant_ref.3, bf16[3,128,128]{2,1,0:T(8,128)(2,1)} %constant.43.clone.a1_ref, bf16[512,256]{1,0:T(8,128)(2,1)} %constant.44.clone.b2_ref, bf16[3,128,128]{2,1,0:T(8,128)(2,1)} %constant.45.clone.a4_ref, ...), custom_call_target="tpu_custom_call" | custom-call | flops 5284823040 | bytes 7864320 | tf_op jit(solution)/shard_map/range_compress_1/pallas_call | solution.py:205
  17.9 3.9 %all-to-all-start = ((f32[32,3,5,16,128]{4,3,2,1,0:T(8,128)}), f32[32,3,5,16,128]{4,3,2,1,0:T(8,128)}, u32[]{:S(2)}, u32[]{:S(2)}) async-start(f32[32,3,5,16,128]{4,3,2,1,0:T(8,128)} %range_compress_1.1), calls=%async_computation | async-start | bytes 7864320 | tf_op jit(solution)/shard_map/all_to_all | solution.py:522
  21.9 1.1 dynamic-slice_bitcast_fusion
  23.0 1.7 %collective-permute-start.16 = (f32[768,384]{1,0:T(8,128)}, f32[768,384]{1,0:T(8,128)}, u32[]{:S(2)}, u32[]{:S(2)}) collective-permute-start(f32[768,384]{1,0:T(8,128)} %dynamic-slice_bitcast_fusion), channel_id=1, source_target_pairs={{0,16},{16,0},{1,17},{17,1},{2,18},{18,2},{3,19},{19,3},{4,20},{20... | collective-permute-start | bytes 3538952 | tf_op jit(solution)/shard_map/ppermute | solution.py:532
  26.8 2.0 %pair_halves.1 = (f32[2,3,16,128]{3,2,1,0:T(8,128)}, f32[2,3,16,128]{3,2,1,0:T(8,128)}, f32[2,3,16,128]{3,2,1,0:T(8,128)}, f32[2,3,16,128]{3,2,1,0:T(8,128)}, f3...) custom-call(f32[16,3,1,16,128]{4,3,2,1,0:T(8,128)} %get-tuple-elemen, ...), custom_call_target="tpu_custom_call" | custom-call | flops 999999995904 | bytes 393216 | tf_op jit(solution)/shard_map/pair_halves/pallas_call | solution.py:234
  29.6 1.5 %collective-permute-start.2 = (f32[2,3,16,128]{3,2,1,0:T(8,128)}, f32[2,3,16,128]{3,2,1,0:T(8,128)S(1)}, u32[]{:S(2)}, u32[]{:S(2)}) collective-permute-start(f32[2,3,16,128]{3,2,1,0:T(8,128)} %get-tuple-element.27), channel_id=1, source_target_pairs={{0,2},{1,3},{2,0},{3,1},{4,6},{5,7},{6,4},{7,5},{8,10},{9,11},{10,... | collective-permute-start | bytes 147464 | tf_op jit(solution)/shard_map/ppermute | solution.py:546
  31.4 9.4 %collective-permute-start.4 = (f32[2,3,16,128]{3,2,1,0:T(8,128)}, f32[2,3,16,128]{3,2,1,0:T(8,128)S(1)}, u32[]{:S(2)}, u32[]{:S(2)}) collective-permute-start(f32[2,3,16,128]{3,2,1,0:T(8,128)} %get-tuple-element.29), channel_id=1, source_target_pairs={{0,4},{1,5},{2,6},{3,7},{4,0},{5,1},{6,2},{7,3},{8,12},{9,13},{10,... | collective-permute-start | bytes 147464 | tf_op jit(solution)/shard_map/ppermute | solution.py:546
  40.8 7.3 %collective-permute-done.2 = f32[2,3,16,128]{3,2,1,0:T(8,128)S(1)} collective-permute-done((f32[2,3,16,128]{3,2,1,0:T(8,128)}, f32[2,3,16,128]{3,2,1,0:T(8,128)S(1)}, u32[]{:S(2)}, u32[]{:S(2)}) %collective-permute-start.2) | collective-permute-done | bytes 49184 | tf_op jit(solution)/shard_map/ppermute | solution.py:546
  48.1 1.5 %collective-permute-done.3 = f32[2,3,16,128]{3,2,1,0:T(8,128)S(1)} collective-permute-done((f32[2,3,16,128]{3,2,1,0:T(8,128)}, f32[2,3,16,128]{3,2,1,0:T(8,128)S(1)}, u32[]{:S(2)}, u32[]{:S(2)}) %collective-permute-start.3) | collective-permute-done | bytes 49184 | tf_op jit(solution)/shard_map/ppermute | solution.py:546
  49.7 1.1 collective-permute-start.7
  50.8 37.9 %collective-permute-done.4 = f32[2,3,16,128]{3,2,1,0:T(8,128)S(1)} collective-permute-done((f32[2,3,16,128]{3,2,1,0:T(8,128)}, f32[2,3,16,128]{3,2,1,0:T(8,128)S(1)}, u32[]{:S(2)}, u32[]{:S(2)}) %collective-permute-start.4) | collective-permute-done | bytes 49184 | tf_op jit(solution)/shard_map/ppermute | solution.py:546
  88.7 1.9 %collective-permute-start.8 = (f32[2,3,16,128]{3,2,1,0:T(8,128)}, f32[2,3,16,128]{3,2,1,0:T(8,128)S(1)}, u32[]{:S(2)}, u32[]{:S(2)}) collective-permute-start(f32[2,3,16,128]{3,2,1,0:T(8,128)} %get-tuple-element.33), channel_id=1, source_target_pairs={{0,16},{1,17},{2,18},{3,19},{4,20},{5,21},{6,22},{7,23},{8,24},{9,... | collective-permute-start | bytes 147464 | tf_op jit(solution)/shard_map/ppermute | solution.py:546
  90.8 1.9 %collective-permute-start.10 = (f32[2,3,16,128]{3,2,1,0:T(8,128)}, f32[2,3,16,128]{3,2,1,0:T(8,128)S(1)}, u32[]{:S(2)}, u32[]{:S(2)}) collective-permute-start(f32[2,3,16,128]{3,2,1,0:T(8,128)} %get-tuple-element.35), channel_id=1, source_target_pairs={{0,18},{1,19},{2,16},{3,17},{4,22},{5,23},{6,20},{7,21},{8,26},{9,... | collective-permute-start | bytes 147464 | tf_op jit(solution)/shard_map/ppermute | solution.py:546
  92.7 1.5 %collective-permute-start.11 = (f32[2,3,16,128]{3,2,1,0:T(8,128)}, f32[2,3,16,128]{3,2,1,0:T(8,128)S(1)}, u32[]{:S(2)}, u32[]{:S(2)}) collective-permute-start(f32[2,3,16,128]{3,2,1,0:T(8,128)} %get-tuple-element.36), channel_id=1, source_target_pairs={{0,19},{1,18},{2,17},{3,16},{4,23},{5,22},{6,21},{7,20},{8,27},{9,... | collective-permute-start | bytes 147464 | tf_op jit(solution)/shard_map/ppermute | solution.py:546
  94.2 2.7 %collective-permute-done.8 = f32[2,3,16,128]{3,2,1,0:T(8,128)S(1)} collective-permute-done((f32[2,3,16,128]{3,2,1,0:T(8,128)}, f32[2,3,16,128]{3,2,1,0:T(8,128)S(1)}, u32[]{:S(2)}, u32[]{:S(2)}) %collective-permute-start.8) | collective-permute-done | bytes 49184 | tf_op jit(solution)/shard_map/ppermute | solution.py:546
  97.6 1.2 collective-permute-done.9
  98.8 3.8 %collective-permute-start.13 = (f32[2,3,16,128]{3,2,1,0:T(8,128)}, f32[2,3,16,128]{3,2,1,0:T(8,128)S(1)}, u32[]{:S(2)}, u32[]{:S(2)}) collective-permute-start(f32[2,3,16,128]{3,2,1,0:T(8,128)} %get-tuple-element.38), channel_id=1, source_target_pairs={{0,21},{1,20},{2,23},{3,22},{4,17},{5,16},{6,19},{7,18},{8,29},{9,... | collective-permute-start | bytes 147464 | tf_op jit(solution)/shard_map/ppermute | solution.py:546
  103.3 1.5 %collective-permute-done.13 = f32[2,3,16,128]{3,2,1,0:T(8,128)S(1)} collective-permute-done((f32[2,3,16,128]{3,2,1,0:T(8,128)}, f32[2,3,16,128]{3,2,1,0:T(8,128)S(1)}, u32[]{:S(2)}, u32[]{:S(2)}) %collective-permute-start.13) | collective-permute-done | bytes 49184 | tf_op jit(solution)/shard_map/ppermute | solution.py:546
  104.8 7.1 %collective-permute-done.14 = f32[2,3,16,128]{3,2,1,0:T(8,128)S(1)} collective-permute-done((f32[2,3,16,128]{3,2,1,0:T(8,128)}, f32[2,3,16,128]{3,2,1,0:T(8,128)S(1)}, u32[]{:S(2)}, u32[]{:S(2)}) %collective-permute-start.14) | collective-permute-done | bytes 49184 | tf_op jit(solution)/shard_map/ppermute | solution.py:546
  112.9 11.6 %azimuth_interferogram.1 = f32[32,3,4,128]{3,2,1,0:T(4,128)} custom-call(s32[2]{0:T(128)} %pad_add_fusion.me_ref, s32[2]{0:T(128)} %fusion.same_ref, f32[32,3,5,16,128]{4,3,2,1,0:T(8,128)} %all-to-all-done.x_ref, f32[16,2,3,16,128]{4,3,2,1,0:T(8,128)} %copy-done.1, f32[768,768]{1,0:T(8,128)} %bitcast.47, f32[768,384]{1,0:T(8,128)} %collective-permute-done.16.other_angle, ...), custom_call_target="tpu_custom_call" | custom-call | flops 3623878656 | bytes 11796480 | tf_op jit(solution)/shard_map/azimuth_interferogram/pallas_call | solution.py:398
  124.5 12.2 %all_to_all.10.in_ref = f32[32,3,4,128]{3,2,1,0:T(4,128)} all-to-all(f32[32,3,4,128]{3,2,1,0:T(4,128)} %azimuth_interferogram.1), channel_id=1, replica_groups=mesh['acq'=2,'high'=4,'low'=4] {'acq','high','low'}, dimensions={0} | all-to-all | bytes 393216 | tf_op jit(solution)/shard_map/all_to_all | solution.py:522
  136.7 1.9 %place_samples.1 = f32[32,1536]{1,0:T(8,128)} custom-call(f32[32,3,4,128]{3,2,1,0:T(4,128)} %all_to_all.10.in_ref), custom_call_target="tpu_custom_call" | custom-call | tf_op jit(solution)/shard_map/place_samples/pallas_call | solution.py:511
  (45 shorter events, 5.9 us)
Async XLA Ops:
  3.7 22.3 %collective-permute-start = (f32[16,3,1,16,128]{4,3,2,1,0:T(8,128)}, f32[16,3,1,16,128]{4,3,2,1,0:T(8,128)S(1)}, u32[]{:S(2)}, u32[]{:S(2)}) collective-permute-start(f32[16,3,1,16,128]{4,3,2,1,0:T(8,128)} %get-tuple-element.24), channel_id=1, source_target_pairs={{0,8},{4,12},{8,0},{12,4},{1,9},{5,13},{9,1},{13,5},{2,10},{6,14},... | collective-permute-start | bytes 1179656 | tf_op jit(solution)/shard_map/ppermute | solution.py:539
  17.9 4.0 %copy-start = (f32[1,768,768]{2,1,0:T(8,128)S(1)}, f32[1,768,768]{2,1,0:T(8,128)}, u32[]{:S(2)}) copy-start(f32[1,768,768]{2,1,0:T(8,128)} %param.17) | copy-start | bytes 7077892
  17.9 94.1 %all-to-all-start = ((f32[32,3,5,16,128]{4,3,2,1,0:T(8,128)}), f32[32,3,5,16,128]{4,3,2,1,0:T(8,128)}, u32[]{:S(2)}, u32[]{:S(2)}) async-start(f32[32,3,5,16,128]{4,3,2,1,0:T(8,128)} %range_compress_1.1), calls=%async_computation | async-start | bytes 7864320 | tf_op jit(solution)/shard_map/all_to_all | solution.py:522
  21.9 2.8 %copy-start.2 = (s32[2,2]{1,0:T(2,128)S(1)}, s32[2,2]{1,0:T(2,128)}, u32[]{:S(2)}) copy-start(s32[2,2]{1,0:T(2,128)} %param.18) | copy-start | bytes 52
  23.0 89.0 %collective-permute-start.16 = (f32[768,384]{1,0:T(8,128)}, f32[768,384]{1,0:T(8,128)}, u32[]{:S(2)}, u32[]{:S(2)}) collective-permute-start(f32[768,384]{1,0:T(8,128)} %dynamic-slice_bitcast_fusion), channel_id=1, source_target_pairs={{0,16},{16,0},{1,17},{17,1},{2,18},{18,2},{3,19},{19,3},{4,20},{20... | collective-permute-start | bytes 3538952 | tf_op jit(solution)/shard_map/ppermute | solution.py:532
  26.0 0.8 copy-start.3
  28.7 12.1 %collective-permute-start.1 = (f32[2,3,16,128]{3,2,1,0:T(8,128)}, f32[2,3,16,128]{3,2,1,0:T(8,128)S(1)}, u32[]{:S(2)}, u32[]{:S(2)}) collective-permute-start(f32[2,3,16,128]{3,2,1,0:T(8,128)} %get-tuple-element.26), channel_id=1, source_target_pairs={{0,1},{1,0},{2,3},{3,2},{4,5},{5,4},{6,7},{7,6},{8,9},{9,8},{10,11... | collective-permute-start | bytes 147464 | tf_op jit(solution)/shard_map/ppermute | solution.py:546
  29.6 18.5 %collective-permute-start.2 = (f32[2,3,16,128]{3,2,1,0:T(8,128)}, f32[2,3,16,128]{3,2,1,0:T(8,128)S(1)}, u32[]{:S(2)}, u32[]{:S(2)}) collective-permute-start(f32[2,3,16,128]{3,2,1,0:T(8,128)} %get-tuple-element.27), channel_id=1, source_target_pairs={{0,2},{1,3},{2,0},{3,1},{4,6},{5,7},{6,4},{7,5},{8,10},{9,11},{10,... | collective-permute-start | bytes 147464 | tf_op jit(solution)/shard_map/ppermute | solution.py:546
  31.1 18.6 %collective-permute-start.3 = (f32[2,3,16,128]{3,2,1,0:T(8,128)}, f32[2,3,16,128]{3,2,1,0:T(8,128)S(1)}, u32[]{:S(2)}, u32[]{:S(2)}) collective-permute-start(f32[2,3,16,128]{3,2,1,0:T(8,128)} %get-tuple-element.28), channel_id=1, source_target_pairs={{0,3},{1,2},{2,1},{3,0},{4,7},{5,6},{6,5},{7,4},{8,11},{9,10},{10,... | collective-permute-start | bytes 147464 | tf_op jit(solution)/shard_map/ppermute | solution.py:546
  31.4 57.3 %collective-permute-start.4 = (f32[2,3,16,128]{3,2,1,0:T(8,128)}, f32[2,3,16,128]{3,2,1,0:T(8,128)S(1)}, u32[]{:S(2)}, u32[]{:S(2)}) collective-permute-start(f32[2,3,16,128]{3,2,1,0:T(8,128)} %get-tuple-element.29), channel_id=1, source_target_pairs={{0,4},{1,5},{2,6},{3,7},{4,0},{5,1},{6,2},{7,3},{8,12},{9,13},{10,... | collective-permute-start | bytes 147464 | tf_op jit(solution)/shard_map/ppermute | solution.py:546
  40.8 49.8 %collective-permute-start.5 = (f32[2,3,16,128]{3,2,1,0:T(8,128)}, f32[2,3,16,128]{3,2,1,0:T(8,128)S(1)}, u32[]{:S(2)}, u32[]{:S(2)}) collective-permute-start(f32[2,3,16,128]{3,2,1,0:T(8,128)} %get-tuple-element.30), channel_id=1, source_target_pairs={{0,5},{1,4},{2,7},{3,6},{4,1},{5,0},{6,3},{7,2},{8,13},{9,12},{10,... | collective-permute-start | bytes 147464 | tf_op jit(solution)/shard_map/ppermute | solution.py:546
  48.1 42.7 %collective-permute-start.6 = (f32[2,3,16,128]{3,2,1,0:T(8,128)}, f32[2,3,16,128]{3,2,1,0:T(8,128)S(1)}, u32[]{:S(2)}, u32[]{:S(2)}) collective-permute-start(f32[2,3,16,128]{3,2,1,0:T(8,128)} %get-tuple-element.31), channel_id=1, source_target_pairs={{0,6},{1,7},{2,4},{3,5},{4,2},{5,3},{6,0},{7,1},{8,14},{9,15},{10,... | collective-permute-start | bytes 147464 | tf_op jit(solution)/shard_map/ppermute | solution.py:546
  49.7 43.0 %collective-permute-start.7 = (f32[2,3,16,128]{3,2,1,0:T(8,128)}, f32[2,3,16,128]{3,2,1,0:T(8,128)S(1)}, u32[]{:S(2)}, u32[]{:S(2)}) collective-permute-start(f32[2,3,16,128]{3,2,1,0:T(8,128)} %get-tuple-element.32), channel_id=1, source_target_pairs={{0,7},{1,6},{2,5},{3,4},{4,3},{5,2},{6,1},{7,0},{8,15},{9,14},{10,... | collective-permute-start | bytes 147464 | tf_op jit(solution)/shard_map/ppermute | solution.py:546
  88.7 8.2 %collective-permute-start.8 = (f32[2,3,16,128]{3,2,1,0:T(8,128)}, f32[2,3,16,128]{3,2,1,0:T(8,128)S(1)}, u32[]{:S(2)}, u32[]{:S(2)}) collective-permute-start(f32[2,3,16,128]{3,2,1,0:T(8,128)} %get-tuple-element.33), channel_id=1, source_target_pairs={{0,16},{1,17},{2,18},{3,19},{4,20},{5,21},{6,22},{7,23},{8,24},{9,... | collective-permute-start | bytes 147464 | tf_op jit(solution)/shard_map/ppermute | solution.py:546
  90.6 8.2 %collective-permute-start.9 = (f32[2,3,16,128]{3,2,1,0:T(8,128)}, f32[2,3,16,128]{3,2,1,0:T(8,128)S(1)}, u32[]{:S(2)}, u32[]{:S(2)}) collective-permute-start(f32[2,3,16,128]{3,2,1,0:T(8,128)} %get-tuple-element.34), channel_id=1, source_target_pairs={{0,17},{1,16},{2,19},{3,18},{4,21},{5,20},{6,23},{7,22},{8,25},{9,... | collective-permute-start | bytes 147464 | tf_op jit(solution)/shard_map/ppermute | solution.py:546
  90.8 11.8 %collective-permute-start.10 = (f32[2,3,16,128]{3,2,1,0:T(8,128)}, f32[2,3,16,128]{3,2,1,0:T(8,128)S(1)}, u32[]{:S(2)}, u32[]{:S(2)}) collective-permute-start(f32[2,3,16,128]{3,2,1,0:T(8,128)} %get-tuple-element.35), channel_id=1, source_target_pairs={{0,18},{1,19},{2,16},{3,17},{4,22},{5,23},{6,20},{7,21},{8,26},{9,... | collective-permute-start | bytes 147464 | tf_op jit(solution)/shard_map/ppermute | solution.py:546
  92.7 10.0 %collective-permute-start.11 = (f32[2,3,16,128]{3,2,1,0:T(8,128)}, f32[2,3,16,128]{3,2,1,0:T(8,128)S(1)}, u32[]{:S(2)}, u32[]{:S(2)}) collective-permute-start(f32[2,3,16,128]{3,2,1,0:T(8,128)} %get-tuple-element.36), channel_id=1, source_target_pairs={{0,19},{1,18},{2,17},{3,16},{4,23},{5,22},{6,21},{7,20},{8,27},{9,... | collective-permute-start | bytes 147464 | tf_op jit(solution)/shard_map/ppermute | solution.py:546
  96.9 6.4 %collective-permute-start.12 = (f32[2,3,16,128]{3,2,1,0:T(8,128)}, f32[2,3,16,128]{3,2,1,0:T(8,128)S(1)}, u32[]{:S(2)}, u32[]{:S(2)}) collective-permute-start(f32[2,3,16,128]{3,2,1,0:T(8,128)} %get-tuple-element.37), channel_id=1, source_target_pairs={{0,20},{1,21},{2,22},{3,23},{4,16},{5,17},{6,18},{7,19},{8,28},{9,... | collective-permute-start | bytes 147464 | tf_op jit(solution)/shard_map/ppermute | solution.py:546
  98.8 6.0 %collective-permute-start.13 = (f32[2,3,16,128]{3,2,1,0:T(8,128)}, f32[2,3,16,128]{3,2,1,0:T(8,128)S(1)}, u32[]{:S(2)}, u32[]{:S(2)}) collective-permute-start(f32[2,3,16,128]{3,2,1,0:T(8,128)} %get-tuple-element.38), channel_id=1, source_target_pairs={{0,21},{1,20},{2,23},{3,22},{4,17},{5,16},{6,19},{7,18},{8,29},{9,... | collective-permute-start | bytes 147464 | tf_op jit(solution)/shard_map/ppermute | solution.py:546
  102.6 9.4 %collective-permute-start.14 = (f32[2,3,16,128]{3,2,1,0:T(8,128)}, f32[2,3,16,128]{3,2,1,0:T(8,128)S(1)}, u32[]{:S(2)}, u32[]{:S(2)}) collective-permute-start(f32[2,3,16,128]{3,2,1,0:T(8,128)} %get-tuple-element.39), channel_id=1, source_target_pairs={{0,22},{1,23},{2,20},{3,21},{4,18},{5,19},{6,16},{7,17},{8,30},{9,... | collective-permute-start | bytes 147464 | tf_op jit(solution)/shard_map/ppermute | solution.py:546
  102.7 9.3 %collective-permute-start.15 = (f32[2,3,16,128]{3,2,1,0:T(8,128)}, f32[2,3,16,128]{3,2,1,0:T(8,128)S(1)}, u32[]{:S(2)}, u32[]{:S(2)}) collective-permute-start(f32[2,3,16,128]{3,2,1,0:T(8,128)} %get-tuple-element.40), channel_id=1, source_target_pairs={{0,23},{1,22},{2,21},{3,20},{4,19},{5,18},{6,17},{7,16},{8,31},{9,... | collective-permute-start | bytes 147464 | tf_op jit(solution)/shard_map/ppermute | solution.py:546
  112.0 0.9 copy-start.1
